TPU v7x, 512 devices: a whole 4x8x8 slice. The times are simulated.
512 devices in a mesh: tm: 16 (over y, core), space: 32 (over x, z).
Axes of the slice: x: 4, y: 8, z: 8, core: 2. Of those that a mesh axis runs over, the one named last changes fastest.
Arguments:
- basis: float32 [4, 16, 64, 64, 8, 128], P(None, None, 'tm', 'space'), may hold values from -60 to 60
- step_numerator: int32 [64], P('tm'), may hold values from 3 to 5
- step_denominator: int32 [64], P('tm'), may hold values from 3 to 4
Outputs:
- hessenberg: float32 [4, 16, 16], replicated
- triangle: float32 [16, 16], replicated
- next_block: float32 [16, 64, 64, 8, 128], P(None, 'tm', 'space')
All inputs are finite; a program needn't handle non-finite values.
Results may differ from a plain program's by a relative error of at most 0.0003.
Values sent between devices are 32-bit elements; how exact they have to be, the bound alone decides.
No kernel may reach another device: no remote copies, remote signals or barrier semaphores. Data moves between devices by JAX's collectives and lax.ppermute only.
A program may use at most 64 MiB of HBM per device.

v0:
```python
import jax
import jax.numpy as jnp
from jax import lax
from jax.sharding import PartitionSpec as P


def passed_along(block, axis, distance):
    devices = range(lax.axis_size(axis))
    route = [(i - distance, i) for i in devices if i - distance in devices]
    return lax.ppermute(block, axis, route)


def with_halo(block, sides, width):
    for axis, dim in sides:
        count = lax.axis_size(axis)
        forward = [(i, i + 1) for i in range(count - 1)]
        backward = [(target, source) for source, target in forward]
        low = lax.ppermute(
            lax.slice_in_dim(block, block.shape[dim] - width, None, axis=dim), axis, forward
        )
        high = lax.ppermute(lax.slice_in_dim(block, 0, width, axis=dim), axis, backward)
        block = jnp.concatenate([low, block, high], axis=dim)
    return block


def step_weights(size_now, size_prev, first_row):
    step_ratio = size_now / size_prev
    ones_like = jnp.ones_like(step_ratio)
    weight_now = jnp.where(first_row, ones_like, (1.0 + 2.0 * step_ratio) / (1.0 + step_ratio))
    weight_one = jnp.where(first_row, ones_like, 1.0 + step_ratio)
    weight_two = jnp.where(
        first_row, jnp.zeros_like(step_ratio), step_ratio * step_ratio / (1.0 + step_ratio)
    )
    return (weight_now, weight_one, weight_two, 0.5 * size_now)


def spread(values):
    return values[None, :, None, None, None]


def per_device(basis, step_numerator, step_denominator):
    highest = lax.Precision.HIGHEST
    blocks, columns, step_count, planes, grid_y, grid_x = basis.shape
    current = basis[blocks - 1]
    size_now = step_numerator.astype(jnp.float32) / step_denominator.astype(jnp.float32)
    earlier, size_before = passed_along(
        (current[:, step_count - 2 :], size_now[step_count - 1 :]), "tm", 1
    )
    global_step = lax.axis_index("tm") * step_count + jnp.arange(step_count, dtype=jnp.int32)
    first_row = global_step == 0
    size_prev = jnp.concatenate([size_before, size_now[:-1]])
    size_prev = jnp.where(first_row, size_now, size_prev)
    weight_now, weight_one, weight_two, kappa_step = step_weights(size_now, size_prev, first_row)
    extended = jnp.concatenate([earlier, current], axis=1)
    back_one = extended[:, 1 : step_count + 1]
    back_two = extended[:, 0:step_count]
    padded = with_halo(current, (("space", 2),), 1)
    beside = padded[:, :, 2:] + padded[:, :, :-2]
    pad_y = jnp.pad(current, ((0, 0), (0, 0), (0, 0), (1, 1), (0, 0)))
    beside = beside + pad_y[:, :, :, 2:] + pad_y[:, :, :, :-2]
    pad_x = jnp.pad(current, ((0, 0), (0, 0), (0, 0), (0, 0), (1, 1)))
    beside = beside + pad_x[..., 2:] + pad_x[..., :-2]
    image = (
        spread(weight_now) * current
        - spread(weight_one) * back_one
        + spread(weight_two) * back_two
        + spread(kappa_step) * (6.0 * current - beside)
    )
    cell_count = step_count * planes * grid_y * grid_x
    total_cells = cell_count * lax.axis_size("tm") * lax.axis_size("space")
    flat_basis = basis.reshape(blocks * columns, cell_count)
    wide_image = image.reshape(columns, cell_count)
    partial_proj = jnp.dot(
        flat_basis, wide_image.T, precision=highest, preferred_element_type=jnp.float32
    )
    projection = lax.psum(partial_proj, ("tm", "space")) / total_cells
    projected = wide_image - jnp.dot(
        projection.T, flat_basis, precision=highest, preferred_element_type=jnp.float32
    )
    partial_gram = jnp.dot(
        projected, projected.T, precision=highest, preferred_element_type=jnp.float32
    )
    gram_matrix = lax.psum(partial_gram, ("tm", "space")) / total_cells
    lower_factor = jnp.linalg.cholesky(gram_matrix)
    solved = lax.linalg.triangular_solve(lower_factor, projected, left_side=True, lower=True)
    return (
        projection.reshape(blocks, columns, columns),
        lower_factor.T,
        solved.reshape(columns, step_count, planes, grid_y, grid_x),
    )


def solution(mesh):
    placed = (P(None, None, "tm", "space", None, None), P("tm"), P("tm"))
    return jax.shard_map(
        per_device,
        mesh=mesh,
        in_specs=placed,
        out_specs=(P(), P(), P(None, "tm", "space", None, None)),
        check_vma=False,
    )
```

profile of v0, /device:TPU:1, one launch (start us, length us, event | category | flops | bytes accessed | tf_op | source)
XLA Modules:
  0.0 237.1 jit_solution(6677812733898491693)
XLA Ops:
  0.6 0.7 broadcast_multiply_fusion.2
  1.3 0.6 slice.54
  1.9 4.6 %collective-permute-start = (f32[1]{0:T(128)}, f32[1]{0:T(128)}, u32[]{:S(2)}, u32[]{:S(2)}) collective-permute-start(f32[1]{0:T(128)} %slice.54), channel_id=1, source_target_pairs={{0,32},{32,64},{64,96},{96,128},{128,160},{160,192},{192,224},{224... | collective-permute-start | bytes 20 | tf_op jit(solution)/shard_map/ppermute | solution.py:10
  6.5 1.1 slice_bitcast_fusion
  7.6 1.9 collective-permute-start.1
  9.5 0.8 fusion.23
  10.4 1.3 collective-permute-start.2
  11.7 5.3 %collective-permute-start.3 = (f32[16,4,1,8,128]{4,3,2,1,0:T(8,128)}, f32[16,4,1,8,128]{4,3,2,1,0:T(8,128)}, u32[]{:S(2)}, u32[]{:S(2)}) collective-permute-start(f32[16,4,1,8,128]{4,3,2,1,0:T(8,128)} %get-tuple-element.11), channel_id=1, source_target_pairs={{0,1},{1,2},{2,3},{3,4},{4,5},{5,6},{6,7},{7,8},{8,9},{9,10},{10,1... | collective-permute-start | bytes 786440 | tf_op jit(solution)/shard_map/ppermute | solution.py:18
  17.0 1.8 reshape.31
  18.8 0.6 divide_select_fusion.1
  20.2 1.4 fusion.4
  21.7 1.7 convolution_bitcast_fusion
  23.4 109.8 %psum.14 = f32[64,16]{0,1:T(8,128)S(1)} all-reduce(f32[64,16]{0,1:T(8,128)S(1)} %convolution_bitcast_fusion), channel_id=1, replica_groups=mesh['tm'=16,'space'=32] {'tm','space'}, use_global_device_ids=true, to_apply=%region_0.1 | all-reduce | flops 1024 | bytes 8192 | tf_op jit(solution)/shard_map/psum | solution.py:76
  133.2 1.3 convolution_subtract_fusion
  134.5 0.8 fusion.24
  135.3 94.4 %psum.15 = f32[16,16]{0,1:T(8,128)S(1)} all-reduce(f32[16,16]{0,1:T(8,128)S(1)} %fusion.24), channel_id=1, replica_groups=mesh['tm'=16,'space'=32] {'tm','space'}, use_global_device_ids=true, to_apply=%region_1.2 | all-reduce | flops 256 | bytes 2048 | tf_op jit(solution)/shard_map/psum | solution.py:83
  229.8 1.5 cholesky.18
  231.3 0.6 compare_reduce_fusion
  231.9 0.6 select_bitcast_fusion
  232.6 1.2 custom-call.6
  233.8 0.7 copy.11
  234.5 0.7 copy.15
  235.3 0.8 fusion.14
  236.1 1.0 copy.12
  (18 shorter events, 1.0 us)
Async XLA Ops:
  1.9 16.9 %collective-permute-start = (f32[1]{0:T(128)}, f32[1]{0:T(128)}, u32[]{:S(2)}, u32[]{:S(2)}) collective-permute-start(f32[1]{0:T(128)} %slice.54), channel_id=1, source_target_pairs={{0,32},{32,64},{64,96},{96,128},{128,160},{160,192},{192,224},{224... | collective-permute-start | bytes 20 | tf_op jit(solution)/shard_map/ppermute | solution.py:10
  7.6 11.9 %collective-permute-start.1 = (f32[16,2,2,8,128]{4,3,2,1,0:T(8,128)S(1)}, f32[16,2,2,8,128]{4,3,2,1,0:T(8,128)S(1)}, u32[]{:S(2)}, u32[]{:S(2)}) collective-permute-start(f32[16,2,2,8,128]{4,3,2,1,0:T(8,128)S(1)} %slice.68), channel_id=1, source_target_pairs={{0,32},{32,64},{64,96},{96,128},{128,160},{160,192},{192,224},{224... | collective-permute-start | bytes 786440 | tf_op jit(solution)/shard_map/ppermute | solution.py:10
  10.4 9.1 %collective-permute-start.2 = (f32[16,4,1,8,128]{4,3,2,1,0:T(8,128)}, f32[16,4,1,8,128]{4,3,2,1,0:T(8,128)S(1)}, u32[]{:S(2)}, u32[]{:S(2)}) collective-permute-start(f32[16,4,1,8,128]{4,3,2,1,0:T(8,128)} %get-tuple-element.10), channel_id=1, source_target_pairs={{1,0},{2,1},{3,2},{4,3},{5,4},{6,5},{7,6},{8,7},{9,8},{10,9},{11,1... | collective-permute-start | bytes 786440 | tf_op jit(solution)/shard_map/ppermute | solution.py:21
  11.7 8.2 %collective-permute-start.3 = (f32[16,4,1,8,128]{4,3,2,1,0:T(8,128)}, f32[16,4,1,8,128]{4,3,2,1,0:T(8,128)}, u32[]{:S(2)}, u32[]{:S(2)}) collective-permute-start(f32[16,4,1,8,128]{4,3,2,1,0:T(8,128)} %get-tuple-element.11), channel_id=1, source_target_pairs={{0,1},{1,2},{2,3},{3,4},{4,5},{5,6},{6,7},{7,8},{8,9},{9,10},{10,1... | collective-permute-start | bytes 786440 | tf_op jit(solution)/shard_map/ppermute | solution.py:18
  17.0 1.8 copy-start.1
  17.0 1.8 copy-start.2
  19.5 0.7 copy-start
where the time goes:
time: 238 us; the launch traced here: 237 us
  blocking collectives  204 us (86%)
  starting transfers between devices  13.1 us (6%)
  local copies, waits for them, and re-layouts  7.11 us (3%)
  other arithmetic  6.8 us (3%)
  matrix products  4.64 us (2%)
    psum x1, blocking collectives, per_device(): projection = lax.psum(partial_proj, ('tm', 'space')) / total_cells  110 us
    psum x1, blocking collectives, per_device(): gram_matrix = lax.psum(partial_gram, ('tm', 'space')) / total_cells  94.4 us
    ppermute x2, starting transfers between devices, passed_along(): return lax.ppermute(block, axis, route)  6.5 us
    ppermute x1, starting transfers between devices, with_halo(): lax.ppermute(lax.slice_in_dim(block, block.shape[dim] - width, None, axis...  5.33 us
  transfers between devices with their start and end apart: 4, of which 1 were waited for; matrix products, arithmetic and copies ran while one was open for 2% of the time, Pallas kernels for 0%

commit v1 on v0

v1 whole, which is shorter than its diff:
```python
import jax
import jax.numpy as jnp
from jax import lax
from jax.sharding import Mesh, PartitionSpec as P

TM = ("y", "core")
SPACE = ("x", "z")


def size_of(axes):
    count = 1
    for axis in axes:
        count *= lax.axis_size(axis)
    return count


def group_sum(block, axes):
    count = size_of(axes)
    copies = jnp.broadcast_to(block, (count,) + block.shape)
    return lax.all_to_all(copies, axes, 0, 0).sum(0)


def step_weights(size_now, size_prev, first_row):
    step_ratio = size_now / size_prev
    ones_like = jnp.ones_like(step_ratio)
    weight_now = jnp.where(first_row, ones_like, (1.0 + 2.0 * step_ratio) / (1.0 + step_ratio))
    weight_one = jnp.where(first_row, ones_like, 1.0 + step_ratio)
    weight_two = jnp.where(
        first_row, jnp.zeros_like(step_ratio), step_ratio * step_ratio / (1.0 + step_ratio)
    )
    return (weight_now, weight_one, weight_two, 0.5 * size_now)


def spread(values):
    return values[None, :, None, None, None]


def per_device(basis, step_numerator, step_denominator):
    highest = lax.Precision.HIGHEST
    blocks, columns, step_count, planes, grid_y, grid_x = basis.shape
    current = basis[blocks - 1]
    size_now = step_numerator.astype(jnp.float32) / step_denominator.astype(jnp.float32)
    slabs = size_of(SPACE)
    groups = size_of(TM)
    up = [(i, i + 1) for i in range(slabs - 1)]
    down = [(i + 1, i) for i in range(slabs - 1)]
    later = [(i, i + 1) for i in range(groups - 1)]
    low = lax.ppermute(current[:, :, planes - 1 :], SPACE, up)
    high = lax.ppermute(current[:, :, :1], SPACE, down)
    earlier = lax.ppermute(current[:, step_count - 2 :], TM, later)
    size_before = lax.ppermute(size_now[step_count - 1 :], TM, later)
    global_step = lax.axis_index(TM) * step_count + jnp.arange(step_count, dtype=jnp.int32)
    first_row = global_step == 0
    size_prev = jnp.concatenate([size_before, size_now[:-1]])
    size_prev = jnp.where(first_row, size_now, size_prev)
    weight_now, weight_one, weight_two, kappa_step = step_weights(size_now, size_prev, first_row)
    extended = jnp.concatenate([earlier, current], axis=1)
    back_one = extended[:, 1 : step_count + 1]
    back_two = extended[:, 0:step_count]
    padded = jnp.concatenate([low, current, high], axis=2)
    beside = padded[:, :, 2:] + padded[:, :, :-2]
    pad_y = jnp.pad(current, ((0, 0), (0, 0), (0, 0), (1, 1), (0, 0)))
    beside = beside + pad_y[:, :, :, 2:] + pad_y[:, :, :, :-2]
    pad_x = jnp.pad(current, ((0, 0), (0, 0), (0, 0), (0, 0), (1, 1)))
    beside = beside + pad_x[..., 2:] + pad_x[..., :-2]
    image = (
        spread(weight_now) * current
        - spread(weight_one) * back_one
        + spread(weight_two) * back_two
        + spread(kappa_step) * (6.0 * current - beside)
    )
    cell_count = step_count * planes * grid_y * grid_x
    total_cells = cell_count * groups * slabs
    rows = blocks * columns
    flat_basis = basis.reshape(rows, cell_count)
    wide_image = image.reshape(columns, cell_count)
    both = jnp.concatenate([flat_basis, wide_image], axis=0)
    partial = jnp.dot(both, both.T, precision=highest, preferred_element_type=jnp.float32)
    products = group_sum(group_sum(partial, TM), SPACE) / total_cells
    projection = products[:rows, rows:]
    image_gram = products[rows:, rows:]
    basis_gram = products[:rows, :rows]
    twice = jnp.dot(projection.T, projection, precision=highest)
    quad = jnp.dot(projection.T, jnp.dot(basis_gram, projection, precision=highest), precision=highest)
    gram_matrix = image_gram - twice - twice + quad
    projected = wide_image - jnp.dot(
        projection.T, flat_basis, precision=highest, preferred_element_type=jnp.float32
    )
    lower_factor = jnp.linalg.cholesky(gram_matrix)
    solved = lax.linalg.triangular_solve(lower_factor, projected, left_side=True, lower=True)
    return (
        projection.reshape(blocks, columns, columns),
        lower_factor.T,
        solved.reshape(columns, step_count, planes, grid_y, grid_x),
    )


def solution(mesh):
    fine = Mesh(mesh.devices.reshape(8, 2, 4, 8), ("y", "core", "x", "z"))
    placed = (P(None, None, TM, SPACE, None, None), P(TM), P(TM))
    return jax.shard_map(
        per_device,
        mesh=fine,
        in_specs=placed,
        out_specs=(P(), P(), P(None, TM, SPACE, None, None)),
        check_vma=False,
    )
```

time: 238 us -> 114 us (0.48)
  blocking collectives: 204 us -> 78.3 us
    psum x2 -> x0, blocking collectives: 204 us -> none  [the longest x1 110 us: per_device(): projection = lax.psum(partial_proj, ('tm', 'space')) / total_cells]
    all_to_all x0 -> x2, blocking collectives: none -> 78.3 us  [group_sum(): return lax.all_to_all(copies, axes, 0, 0).sum(0)]
  transfers between devices with their start and end apart: 4 -> 4, of which waited for: 1 -> 1; matrix products, arithmetic and copies ran while one was open for 2% -> 4% of each run, Pallas kernels for 0% -> 0%
where the time goes in v1:
time: 114 us
  blocking collectives  78.3 us (69%)
  starting transfers between devices  13.1 us (11%)
  local copies, waits for them, and re-layouts  8.13 us (7%)
  other arithmetic  6.9 us (6%)
  matrix products  5.92 us (5%)
    all_to_all x2, blocking collectives, group_sum(): return lax.all_to_all(copies, axes, 0, 0).sum(0)  78.3 us
    ppermute x1, starting transfers between devices, per_device(): low = lax.ppermute(current[:, :, planes - 1:], SPACE, up)  5.33 us
    ppermute x1, starting transfers between devices, per_device(): size_before = lax.ppermute(size_now[step_count - 1:], TM, later)  4.58 us
    unnamed x11, local copies, waits for them, and re-layouts  3.53 us
    dot_general x1, matrix products, per_device(): jnp.dot(projection.T, flat_basis, precision=highest, preferred_element_ty...  2.31 us
  transfers between devices with their start and end apart: 4, of which 1 were waited for; matrix products, arithmetic and copies ran while one was open for 4% of the time, Pallas kernels for 0%

profile of v1, /device:TPU:1, one launch (start us, length us, event | category | flops | bytes accessed | tf_op | source)
XLA Modules:
  0.0 113.6 jit_solution(6325951983086104745)
XLA Ops:
  0.6 0.7 broadcast_multiply_fusion.1
  1.3 0.6 slice.63
  1.9 4.6 %collective-permute-start = (f32[1]{0:T(128)}, f32[1]{0:T(128)}, u32[]{:S(2)}, u32[]{:S(2)}) collective-permute-start(f32[1]{0:T(128)} %slice.63), channel_id=1, source_target_pairs={{0,32},{32,64},{64,96},{96,128},{128,160},{160,192},{192,224},{224... | collective-permute-start | bytes 20 | tf_op jit(solution)/shard_map/ppermute | solution.py:51
  6.5 1.1 slice_bitcast_fusion
  7.6 1.9 %collective-permute-start.1 = (f32[16,2,2,8,128]{4,3,2,1,0:T(8,128)S(1)}, f32[16,2,2,8,128]{4,3,2,1,0:T(8,128)S(1)}, u32[]{:S(2)}, u32[]{:S(2)}) collective-permute-start(f32[16,2,2,8,128]{4,3,2,1,0:T(8,128)S(1)} %slice.80), channel_id=1, source_target_pairs={{0,32},{32,64},{64,96},{96,128},{128,160},{160,192},{192,224},{224... | collective-permute-start | bytes 786440 | tf_op jit(solution)/shard_map/ppermute | solution.py:50
  9.5 0.8 fusion.34
  10.4 1.3 %collective-permute-start.2 = (f32[16,4,1,8,128]{4,3,2,1,0:T(8,128)}, f32[16,4,1,8,128]{4,3,2,1,0:T(8,128)S(1)}, u32[]{:S(2)}, u32[]{:S(2)}) collective-permute-start(f32[16,4,1,8,128]{4,3,2,1,0:T(8,128)} %get-tuple-element.13), channel_id=1, source_target_pairs={{1,0},{2,1},{3,2},{4,3},{5,4},{6,5},{7,6},{8,7},{9,8},{10,9},{11,1... | collective-permute-start | bytes 786440 | tf_op jit(solution)/shard_map/ppermute | solution.py:49
  11.7 5.3 %collective-permute-start.3 = (f32[16,4,1,8,128]{4,3,2,1,0:T(8,128)}, f32[16,4,1,8,128]{4,3,2,1,0:T(8,128)}, u32[]{:S(2)}, u32[]{:S(2)}) collective-permute-start(f32[16,4,1,8,128]{4,3,2,1,0:T(8,128)} %get-tuple-element.14), channel_id=1, source_target_pairs={{0,1},{1,2},{2,3},{3,4},{4,5},{5,6},{6,7},{7,8},{8,9},{9,10},{10,1... | collective-permute-start | bytes 786440 | tf_op jit(solution)/shard_map/ppermute | solution.py:48
  17.0 1.8 %reshape.30 = f32[64,8192]{1,0:T(8,128)S(1)} reshape(f32[4,16,4,2,8,128]{5,4,3,2,1,0:T(8,128)} %param.3) | data formatting | bytes 4194304 | tf_op jit(solution)/shard_map/reshape | solution.py:75
  18.8 0.6 divide_select_fusion.1
  19.9 1.4 %fusion.9 = f32[16,4,2,8,128]{4,3,2,1,0:T(8,128)S(1)} fusion(f32[16,2,2,8,128]{4,3,2,1,0:T(8,128)S(1)} %collective-permute-done.1, f32[16,4,2,8,128]{4,3,2,1,0:T(8,128)S(1)} %slice_bitcast_fusion, f32[16,4,1,8,128]{4,3,2,1,0:T(8,128)} %collective-permute-done.3, f32[16,4,1,8,128]{4,3,2,1,0:T(8,128)S(1)} %collective-permute-done.2, ...), kind=kLoop, calls=%fused_computation.17 | loop fusion | flops 2359296 | bytes 1835072 | tf_op jit(solution)/shard_map/add | solution.py:67
  21.3 0.8 copy-done
  22.4 2.2 %fusion = f32[80,80]{1,0:T(8,128)S(1)} fusion(f32[16,8192]{1,0:T(8,128)S(1)} %bitcast.38, f32[64,8192]{1,0:T(8,128)S(1)} %reshape.30), kind=kOutput, calls=%fused_computation.1 | convolution fusion | flops 629800960 | bytes 2647040 | tf_op jit(solution)/shard_map/dot_general | solution.py:78
  24.6 29.4 %all_to_all.10 = f32[16,80,80]{2,1,0:T(8,128)S(1)} all-to-all(f32[16,80,80]{2,1,0:T(8,128)S(1)} %broadcast_in_dim.5), channel_id=1, replica_groups=mesh['y'=8,'core'=2,'x'=4,'z'=8] {'y','core'}, dimensions={0} | all-to-all | bytes 819200 | tf_op jit(solution)/shard_map/all_to_all | solution.py:20
  54.2 48.9 %all_to_all.11 = f32[32,80,80]{2,1,0:T(8,128)S(1)} all-to-all(f32[32,80,80]{2,1,0:T(8,128)S(1)} %broadcast_in_dim.6), channel_id=1, replica_groups=mesh['y'=8,'core'=2,'x'=4,'z'=8] {'x','z'}, dimensions={0} | all-to-all | bytes 1638400 | tf_op jit(solution)/shard_map/all_to_all | solution.py:20
  103.3 2.3 %fusion.4 = f32[2,8,64,128]{3,1,2,0:T(8,128)S(1)} fusion(f32[64,8192]{1,0:T(8,128)S(1)} %reshape.30, f32[80,80]{0,1:T(8,128)S(1)} %broadcast_multiply_fusion, f32[2,8,64,128]{3,2,1,0:T(8,128)} %bitcast.36), kind=kOutput, calls=%fused_computation.9 | convolution fusion | flops 100794368 | bytes 3153920 | tf_op jit(solution)/shard_map/dot_general | solution.py:86
  106.1 0.7 copy.28
  107.1 1.5 %cholesky.18 = f32[16,16]{1,0:T(8,128)S(1)} custom-call(f32[16,16]{1,0:T(8,128)S(1)} %fusion.23), custom_call_target="Cholesky" | custom-call | tf_op jit(solution)/shard_map/jit(cholesky)/cholesky | solution.py:89
  108.6 0.6 compare_reduce_fusion
  109.2 0.6 select_bitcast_fusion
  109.9 1.2 %custom-call.6 = f32[1,16,16]{1,2,0:T(8,128)S(1)} custom-call(f32[1,16,16]{2,1,0:T(8,128)S(1)} %get-tuple-element.15), custom_call_target="InvertDiagBlocksLowerTriangular" | custom-call | tf_op jit(solution)/shard_map/triangular_solve | solution.py:90
  111.1 0.8 fusion.18
  112.0 1.0 copy.24
  112.9 0.7 copy.23
  (26 shorter events, 1.9 us)
Async XLA Ops:
  1.9 16.9 %collective-permute-start = (f32[1]{0:T(128)}, f32[1]{0:T(128)}, u32[]{:S(2)}, u32[]{:S(2)}) collective-permute-start(f32[1]{0:T(128)} %slice.63), channel_id=1, source_target_pairs={{0,32},{32,64},{64,96},{96,128},{128,160},{160,192},{192,224},{224... | collective-permute-start | bytes 20 | tf_op jit(solution)/shard_map/ppermute | solution.py:51
  7.6 11.9 %collective-permute-start.1 = (f32[16,2,2,8,128]{4,3,2,1,0:T(8,128)S(1)}, f32[16,2,2,8,128]{4,3,2,1,0:T(8,128)S(1)}, u32[]{:S(2)}, u32[]{:S(2)}) collective-permute-start(f32[16,2,2,8,128]{4,3,2,1,0:T(8,128)S(1)} %slice.80), channel_id=1, source_target_pairs={{0,32},{32,64},{64,96},{96,128},{128,160},{160,192},{192,224},{224... | collective-permute-start | bytes 786440 | tf_op jit(solution)/shard_map/ppermute | solution.py:50
  10.4 9.1 %collective-permute-start.2 = (f32[16,4,1,8,128]{4,3,2,1,0:T(8,128)}, f32[16,4,1,8,128]{4,3,2,1,0:T(8,128)S(1)}, u32[]{:S(2)}, u32[]{:S(2)}) collective-permute-start(f32[16,4,1,8,128]{4,3,2,1,0:T(8,128)} %get-tuple-element.13), channel_id=1, source_target_pairs={{1,0},{2,1},{3,2},{4,3},{5,4},{6,5},{7,6},{8,7},{9,8},{10,9},{11,1... | collective-permute-start | bytes 786440 | tf_op jit(solution)/shard_map/ppermute | solution.py:49
  11.7 8.2 %collective-permute-start.3 = (f32[16,4,1,8,128]{4,3,2,1,0:T(8,128)}, f32[16,4,1,8,128]{4,3,2,1,0:T(8,128)}, u32[]{:S(2)}, u32[]{:S(2)}) collective-permute-start(f32[16,4,1,8,128]{4,3,2,1,0:T(8,128)} %get-tuple-element.14), channel_id=1, source_target_pairs={{0,1},{1,2},{2,3},{3,4},{4,5},{5,6},{6,7},{7,8},{8,9},{9,10},{10,1... | collective-permute-start | bytes 786440 | tf_op jit(solution)/shard_map/ppermute | solution.py:48
  17.0 1.8 %copy-start.1 = (s32[4]{0:T(128)S(1)}, s32[4]{0:T(128)}, u32[]{:S(2)}) copy-start(s32[4]{0:T(128)} %param.5) | copy-start | bytes 52
  17.0 1.8 %copy-start.2 = (s32[4]{0:T(128)S(1)}, s32[4]{0:T(128)}, u32[]{:S(2)}) copy-start(s32[4]{0:T(128)} %param.4) | copy-start | bytes 52
  21.3 0.8 copy-start

commit v2 on v1

v2 whole, which is shorter than its diff:
```python
import jax
import jax.numpy as jnp
from jax import lax
from jax.experimental import pallas as pl
from jax.experimental.pallas import tpu as pltpu
from jax.sharding import Mesh, PartitionSpec as P

TM = ("y", "core")
SPACE = ("x", "z")
COLS = 16
BLOCKS = 4
ROWS = BLOCKS * COLS
STEPS = 4
PLANES = 2
TILES = STEPS * PLANES
LINES = TILES * 8
CELLS = LINES * 128
TOTAL = 64 * 64 * 8 * 128
PARTS = 3
FULL = ROWS + COLS
HIGHEST = lax.Precision.HIGHEST
F32 = jnp.float32
BF16 = jnp.bfloat16
NT = (((1,), (1,)), ((), ()))
NN = (((1,), (0,)), ((), ()))


def params(megabytes):
    return pltpu.CompilerParams(vmem_limit_bytes=megabytes * 1024 * 1024)


def size_of(axes):
    count = 1
    for axis in axes:
        count *= lax.axis_size(axis)
    return count


def split(value):
    first = value.astype(BF16)
    rest = value - first.astype(F32)
    second = rest.astype(BF16)
    third = (rest - second.astype(F32)).astype(BF16)
    return first, second, third


def step_sizes(num_ref, den_ref):
    sizes = []
    for step in range(STEPS):
        top = jnp.full((8, 128), num_ref[step]).astype(F32)
        bottom = jnp.full((8, 128), den_ref[step]).astype(F32)
        sizes.append(top / bottom)
    return sizes


def edges_kernel(num_ref, den_ref, basis_ref, up_ref, down_ref, late_ref, size_ref, sems):
    last = BLOCKS - 1
    copies = [
        pltpu.make_async_copy(basis_ref.at[last, :, :, PLANES - 1], up_ref, sems.at[0]),
        pltpu.make_async_copy(basis_ref.at[last, :, :, 0], down_ref, sems.at[1]),
        pltpu.make_async_copy(
            basis_ref.at[last, :, pl.ds(STEPS - 2, 2)], late_ref.at[pl.ds(0, COLS)], sems.at[2]
        ),
    ]
    for copy in copies:
        copy.start()
    final_size = step_sizes(num_ref, den_ref)[STEPS - 1]
    for step in range(2):
        for plane in range(PLANES):
            size_ref[step, plane] = final_size
    tail = pltpu.make_async_copy(size_ref, late_ref.at[COLS], sems.at[3])
    tail.start()
    for copy in copies:
        copy.wait()
    tail.wait()


def edges(basis, num, den):
    smem = pl.BlockSpec(memory_space=pltpu.SMEM)
    anywhere = pl.BlockSpec(memory_space=pl.ANY)
    return pl.pallas_call(
        edges_kernel,
        out_shape=(
            jax.ShapeDtypeStruct((COLS, STEPS, 8, 128), F32),
            jax.ShapeDtypeStruct((COLS, STEPS, 8, 128), F32),
            jax.ShapeDtypeStruct((COLS + 1, 2, PLANES, 8, 128), F32),
        ),
        in_specs=[smem, smem, anywhere],
        out_specs=(anywhere, anywhere, anywhere),
        scratch_shapes=[pltpu.VMEM((2, PLANES, 8, 128), F32), pltpu.SemaphoreType.DMA((4,))],
        compiler_params=params(4),
        name="edges",
    )(num, den, basis)


def gathered_rows(field_ref, parts_ref, count):
    @pl.loop(0, TILES)
    def _(tile):
        for line in range(8):
            place = tile * 8 + line
            value = field_ref[pl.ds(place, count, stride=LINES), :]
            lanes = pl.ds(pl.multiple_of(place * 128, 128), 128)
            for part, piece in enumerate(split(value)):
                parts_ref[pl.ds(part * count, count), lanes] = piece


def part_products(products, count, offset, width):
    total = None
    for b in range(PARTS):
        group = None
        for a in range(PARTS - b):
            piece = products[a * count : (a + 1) * count, offset + b * width : offset + (b + 1) * width]
            group = piece if group is None else group + piece
        total = group if total is None else total + group
    return total


def basis_kernel(field_ref, parts_ref, packed_ref):
    gathered_rows(field_ref, parts_ref, ROWS)
    whole = parts_ref[...]
    products = lax.dot_general(whole, whole, NT, preferred_element_type=F32)
    gram = part_products(products, ROWS, 0, ROWS)
    pieces = [jnp.zeros((COLS, FULL), F32)]
    for block in range(BLOCKS):
        pieces.append(gram[block * COLS : (block + 1) * COLS, block * COLS :])
    used = FULL + sum(ROWS - block * COLS for block in range(BLOCKS))
    pieces.append(jnp.zeros((COLS, 256 - used), F32))
    packed_ref[...] = jnp.concatenate(pieces, axis=1)


def basis_products(flat):
    vmem = pl.BlockSpec(memory_space=pltpu.VMEM)
    return pl.pallas_call(
        basis_kernel,
        out_shape=(
            jax.ShapeDtypeStruct((PARTS * ROWS, CELLS), BF16),
            jax.ShapeDtypeStruct((COLS, 256), F32),
        ),
        in_specs=[vmem],
        out_specs=(vmem, vmem),
        compiler_params=params(20),
        name="basis_products",
    )(flat)


def image_kernel(
    num_ref, den_ref, field_ref, low_ref, high_ref, late_ref, basis_ref, packed_ref,
    parts_ref, copies_ref, image_ref,
):
    sizes = step_sizes(num_ref, den_ref)
    first = (lax.axis_index("y") == 0) & (lax.axis_index("core") == 0)
    start = jnp.full((8, 128), first.astype(jnp.int32)) == 1
    weights = []
    for step in range(STEPS):
        if step == 0:
            before = jnp.where(start, sizes[0], late_ref[COLS, 0, 0])
        else:
            before = sizes[step - 1]
        ratio = sizes[step] / before
        now = (1.0 + 2.0 * ratio) / (1.0 + ratio)
        one = 1.0 + ratio
        two = ratio * ratio / (1.0 + ratio)
        if step == 0:
            now = jnp.where(start, 1.0, now)
            one = jnp.where(start, 1.0, one)
            two = jnp.where(start, 0.0, two)
        weights.append((now, one, two, 0.5 * sizes[step]))
    line = lax.broadcasted_iota(jnp.int32, (8, 128), 0)
    lane = lax.broadcasted_iota(jnp.int32, (8, 128), 1)

    @pl.loop(0, COLS)
    def _(col):
        def own(step, plane):
            place = pl.multiple_of(col * LINES + (step * PLANES + plane) * 8, 8)
            return field_ref[pl.ds(place, 8), :]

        here = [[own(step, plane) for plane in range(PLANES)] for step in range(STEPS)]
        past = [[late_ref[col, step, plane] for plane in range(PLANES)] for step in range(2)]
        line_up = past + here
        for step in range(STEPS):
            now, one, two, kappa = weights[step]
            for plane in range(PLANES):
                value = here[step][plane]
                below = low_ref[col, step] if plane == 0 else here[step][plane - 1]
                above = high_ref[col, step] if plane == PLANES - 1 else here[step][plane + 1]
                beside = above + below
                beside += jnp.where(line < 7, pltpu.roll(value, 7, 0), 0.0)
                beside += jnp.where(line > 0, pltpu.roll(value, 1, 0), 0.0)
                beside += jnp.where(lane < 127, pltpu.roll(value, 127, 1), 0.0)
                beside += jnp.where(lane > 0, pltpu.roll(value, 1, 1), 0.0)
                result = (
                    now * value
                    - one * line_up[step + 1][plane]
                    + two * line_up[step][plane]
                    + kappa * (6.0 * value - beside)
                )
                place = pl.multiple_of(col * LINES + (step * PLANES + plane) * 8, 8)
                image_ref[pl.ds(place, 8), :] = result

    gathered_rows(image_ref, parts_ref, COLS)
    own_parts = parts_ref[...]
    with_basis = lax.dot_general(own_parts, basis_ref[...], NT, preferred_element_type=F32)
    with_self = lax.dot_general(own_parts, own_parts, NT, preferred_element_type=F32)
    main = jnp.concatenate(
        [
            part_products(with_basis, COLS, 0, ROWS),
            part_products(with_self, COLS, 0, COLS),
            jnp.zeros((COLS, 256 - FULL), F32),
        ],
        axis=1,
    )
    payload = main + packed_ref[...]
    for copy in range(copies_ref.shape[0]):
        copies_ref[copy, 0] = payload[:, :128]
        copies_ref[copy, 1] = payload[:, 128:]


def image_products(num, den, flat, low, high, late, basis_parts, packed, count):
    smem = pl.BlockSpec(memory_space=pltpu.SMEM)
    vmem = pl.BlockSpec(memory_space=pltpu.VMEM)
    per_block = COLS * LINES
    return pl.pallas_call(
        image_kernel,
        grid=(1,),
        out_shape=(
            jax.ShapeDtypeStruct((PARTS * COLS, CELLS), BF16),
            jax.ShapeDtypeStruct((count, 2, COLS, 128), F32),
        ),
        in_specs=[
            smem,
            smem,
            pl.BlockSpec((per_block, 128), lambda i: (BLOCKS - 1, 0)),
            vmem,
            vmem,
            vmem,
            vmem,
            vmem,
        ],
        out_specs=(vmem, vmem),
        scratch_shapes=[pltpu.VMEM((per_block, 128), F32)],
        compiler_params=params(20),
        name="image_products",
    )(num, den, flat, low, high, late, basis_parts, packed)


def finish_kernel(sums_ref, parts_ref, hess_ref, triangle_ref, next_ref):
    sums = sums_ref[0]
    for piece in range(1, sums_ref.shape[0]):
        sums = sums + sums_ref[piece]
    sums = sums * (1.0 / TOTAL)
    left, right = sums[0], sums[1]
    packed = jnp.concatenate([left, right], axis=1)
    proj = packed[:, :ROWS]
    image_gram = packed[:, ROWS:FULL]
    row = lax.broadcasted_iota(jnp.int32, (COLS, COLS), 0)
    col = lax.broadcasted_iota(jnp.int32, (COLS, COLS), 1)
    upper = []
    offset = FULL
    for block in range(BLOCKS):
        width = ROWS - block * COLS
        rows = packed[:, offset : offset + width]
        pieces = [0.5 * rows[:, :COLS]]
        if block:
            pieces.insert(0, jnp.zeros((COLS, block * COLS), F32))
        if width > COLS:
            pieces.append(rows[:, COLS:])
        upper.append(jnp.concatenate(pieces, axis=1))
        offset += width
    half = jnp.concatenate(upper, axis=0)
    carried = lax.dot_general(proj, half, NN, precision=HIGHEST, preferred_element_type=F32) - proj
    cross = lax.dot_general(carried, proj, NT, precision=HIGHEST, preferred_element_type=F32)
    cross_t = lax.dot_general(proj, carried, NT, precision=HIGHEST, preferred_element_type=F32)
    gram = image_gram + (cross + cross_t)
    eye = jnp.where(row == col, 1.0, 0.0).astype(F32)
    work = jnp.concatenate(
        [gram, -proj, eye, jnp.zeros((COLS, 128 - FULL - COLS), F32)], axis=1
    )
    wide_row = lax.broadcasted_iota(jnp.int32, (COLS, 128), 0)
    scale = jnp.zeros((COLS, 128), F32)
    for step in range(COLS):
        column = jnp.broadcast_to(work[:, step : step + 1], (COLS, 128))
        pivot = jnp.broadcast_to(column[step : step + 1], (COLS, 128))
        pivot_row = jnp.broadcast_to(work[step : step + 1], (COLS, 128))
        work = work - jnp.where(wide_row > step, column / pivot, 0.0) * pivot_row
        scale = jnp.where(wide_row == step, lax.rsqrt(pivot), scale)
    work = work * scale
    hess_ref[...] = proj.T
    triangle_ref[...] = jnp.where(row <= col, work[:, :COLS], 0.0)
    factors = split(work[:, COLS : COLS + FULL])
    stacked = []
    for part in range(PARTS):
        on_basis = factors[part][:, :ROWS]
        on_image = factors[part][:, ROWS:]
        pieces = []
        for piece in (on_basis, on_image):
            for other in range(PARTS):
                pieces.append(piece if other < PARTS - part else jnp.zeros_like(piece))
        stacked.append(jnp.concatenate(pieces, axis=1))
    factor = jnp.concatenate(stacked, axis=0)
    for tile in range(TILES):
        lanes = pl.ds(tile * 1024, 1024)
        product = lax.dot_general(factor, parts_ref[:, lanes], NN, preferred_element_type=F32)
        value = product[:COLS] + (product[COLS : 2 * COLS] + product[2 * COLS :])
        for line in range(8):
            next_ref[pl.ds(tile * 8 + line, COLS, stride=LINES), :] = value[
                :, line * 128 : (line + 1) * 128
            ]


def finish(sums, parts):
    vmem = pl.BlockSpec(memory_space=pltpu.VMEM)
    return pl.pallas_call(
        finish_kernel,
        out_shape=(
            jax.ShapeDtypeStruct((ROWS, COLS), F32),
            jax.ShapeDtypeStruct((COLS, COLS), F32),
            jax.ShapeDtypeStruct((COLS * LINES, 128), F32),
        ),
        in_specs=[vmem, vmem],
        out_specs=(vmem, vmem, vmem),
        compiler_params=params(20),
        name="finish",
    )(sums, parts)


def exchanged(copies, axes):
    return lax.all_to_all(copies, axes, 0, 0)


def per_device(basis, num, den):
    slabs = size_of(SPACE)
    groups = size_of(TM)
    above = [(i, i + 1) for i in range(slabs - 1)]
    below = [(i + 1, i) for i in range(slabs - 1)]
    later = [(i, i + 1) for i in range(groups - 1)]
    flat = basis.reshape(ROWS * LINES, 128)
    up, down, late = edges(basis, num, den)
    low = lax.ppermute(up, SPACE, above)
    high = lax.ppermute(down, SPACE, below)
    earlier = lax.ppermute(late, TM, later)
    basis_parts, packed = basis_products(flat)
    image_parts, copies = image_products(
        num, den, flat, low, high, earlier, basis_parts, packed, groups
    )
    sums = exchanged(copies, TM).sum(0)
    sums = exchanged(jnp.broadcast_to(sums, (slabs,) + sums.shape), SPACE)
    parts = jnp.concatenate([basis_parts, image_parts], axis=0)
    hess, triangle, following = finish(sums, parts)
    return (
        hess.reshape(BLOCKS, COLS, COLS),
        triangle,
        following.reshape(COLS, STEPS, PLANES, 8, 128),
    )


def solution(mesh):
    fine = Mesh(mesh.devices.reshape(8, 2, 4, 8), ("y", "core", "x", "z"))
    placed = (P(None, None, TM, SPACE, None, None), P(TM), P(TM))
    return jax.shard_map(
        per_device,
        mesh=fine,
        in_specs=placed,
        out_specs=(P(), P(), P(None, TM, SPACE, None, None)),
        check_vma=False,
    )
```

time: 114 us -> 84 us (0.74)
  blocking collectives: 78.3 us -> 18.8 us
  waiting for transfers between devices: 0.42 us -> 17.6 us
  Pallas kernels: 0 us -> 12.5 us
  starting transfers between devices: 13.1 us -> 22.3 us
  matrix products: 5.92 us -> 0 us
  other arithmetic: 6.9 us -> 3.27 us
    all_to_all x2 -> x1, blocking collectives: 78.3 us -> 18.8 us  [exchanged(): return lax.all_to_all(copies, axes, 0, 0)]
    all_to_all x0 -> x1, waiting for transfers between devices: none -> 13.2 us  [exchanged(): return lax.all_to_all(copies, axes, 0, 0)]
    pallas_call x0 -> x4, Pallas kernels: none -> 12.5 us  [the longest x1 5.07 us: finish(): pl.pallas_call(finish_kernel, out_shape=(jax.ShapeDtypeStruct((ROWS, COLS...]
    all_to_all x0 -> x1, starting transfers between devices: none -> 12.4 us  [exchanged(): return lax.all_to_all(copies, axes, 0, 0)]
    dot_general x5 -> x0, matrix products: 5.07 us -> none  [the longest x1 2.31 us: per_device(): jnp.dot(projection.T, flat_basis, precision=highest, preferred_element_ty...]
    another operation x5 -> x0, other arithmetic: 4.03 us -> none  [the longest x3 2.15 us: per_device(): lower_factor = jnp.linalg.cholesky(gram_matrix)]
    unnamed x11 -> x18, local copies, waits for them, and re-layouts: 3.53 us -> 7.48 us
    ppermute x4 -> x3, waiting for transfers between devices: 0.42 us -> 4.35 us  [the longest x1 4.35 us: per_device(): high = lax.ppermute(down, SPACE, below)]
  transfers between devices with their start and end apart: 4 -> 4, of which waited for: 1 -> 2; matrix products, arithmetic and copies ran while one was open for 4% -> 4% of each run, Pallas kernels for 0% -> 4%
where the time goes in v2:
time: 84 us; the launch traced here: 83.5 us
  starting transfers between devices  22.3 us (27%)
  blocking collectives  18.8 us (22%)
  waiting for transfers between devices  17.6 us (21%)
  Pallas kernels  12.5 us (15%)
  local copies, waits for them, and re-layouts  8.33 us (10%)
  other arithmetic  3.27 us (4%)
    all_to_all x1, blocking collectives, exchanged(): return lax.all_to_all(copies, axes, 0, 0)  18.8 us
    all_to_all x1, waiting for transfers between devices, exchanged(): return lax.all_to_all(copies, axes, 0, 0)  13.2 us
    all_to_all x1, starting transfers between devices, exchanged(): return lax.all_to_all(copies, axes, 0, 0)  12.4 us
    unnamed x18, local copies, waits for them, and re-layouts  7.48 us
    pallas_call x1, Pallas kernels, finish(): pl.pallas_call(finish_kernel, out_shape=(jax.ShapeDtypeStruct((ROWS, COLS...  5.07 us
    ppermute x1, starting transfers between devices, per_device(): earlier = lax.ppermute(late, TM, later)  4.59 us
    ppermute x1, waiting for transfers between devices, per_device(): high = lax.ppermute(down, SPACE, below)  4.35 us
    ppermute x1, starting transfers between devices, per_device(): low = lax.ppermute(up, SPACE, above)  4.01 us
  transfers between devices with their start and end apart: 4, of which 2 were waited for; matrix products, arithmetic and copies ran while one was open for 4% of the time, Pallas kernels for 4%

profile of v2, /device:TPU:1, one launch (start us, length us, event | category | flops | bytes accessed | tf_op | source)
XLA Modules:
  0.0 83.5 jit_solution(6855903560738014044)
XLA Ops:
  0.6 0.0 copy-start
  0.6 1.6 %copy-done = f32[4,16,4,2,8,128]{5,4,3,2,1,0:T(8,128)S(1)} copy-done((f32[4,16,4,2,8,128]{5,4,3,2,1,0:T(8,128)S(1)}, f32[4,16,4,2,8,128]{5,4,3,2,1,0:T(8,128)}, u32[]{:S(2)}) %copy-start) | copy-done | bytes 2097176
  2.2 0.7 copy-done.5
  2.9 0.7 copy-done.7
  3.5 0.7 edges.1
  4.2 4.6 %collective-permute-start.2 = (f32[17,2,2,8,128]{4,3,2,1,0:T(8,128)S(1)}, f32[17,2,2,8,128]{4,3,2,1,0:T(8,128)S(1)}, u32[]{:S(2)}, u32[]{:S(2)}) collective-permute-start(f32[17,2,2,8,128]{4,3,2,1,0:T(8,128)S(1)} %get-tuple-element.15), channel_id=1, source_target_pairs={{0,32},{32,64},{64,96},{96,128},{128,160},{160,192},{192,224},{224... | collective-permute-start | bytes 835592 | tf_op jit(solution)/shard_map/ppermute | solution.py:340
  8.8 4.0 %collective-permute-start = (f32[16,4,8,128]{3,2,1,0:T(8,128)S(1)}, f32[16,4,8,128]{3,2,1,0:T(8,128)S(1)}, u32[]{:S(2)}, u32[]{:S(2)}) collective-permute-start(f32[16,4,8,128]{3,2,1,0:T(8,128)S(1)} %get-tuple-element.13), channel_id=1, source_target_pairs={{0,1},{1,2},{2,3},{3,4},{4,5},{5,6},{6,7},{7,8},{8,9},{9,10},{10,1... | collective-permute-start | bytes 786440 | tf_op jit(solution)/shard_map/ppermute | solution.py:338
  12.8 1.3 %collective-permute-start.1 = (f32[16,4,8,128]{3,2,1,0:T(8,128)S(1)}, f32[16,4,8,128]{3,2,1,0:T(8,128)S(1)}, u32[]{:S(2)}, u32[]{:S(2)}) collective-permute-start(f32[16,4,8,128]{3,2,1,0:T(8,128)S(1)} %get-tuple-element.14), channel_id=1, source_target_pairs={{1,0},{2,1},{3,2},{4,3},{5,4},{6,5},{7,6},{8,7},{9,8},{10,9},{11,1... | collective-permute-start | bytes 786440 | tf_op jit(solution)/shard_map/ppermute | solution.py:339
  14.1 0.0 copy-start.1
  14.2 1.6 %copy-done.1 = f32[4,16,4,2,8,128]{5,4,3,2,1,0:T(8,128)S(1)} copy-done((f32[4,16,4,2,8,128]{5,4,3,2,1,0:T(8,128)S(1)}, f32[4,16,4,2,8,128]{5,4,3,2,1,0:T(8,128)}, u32[]{:S(2)}) %copy-start.1) | copy-done | bytes 2097176
  15.7 2.9 %basis_products.1 = (bf16[192,8192]{1,0:T(8,128)(2,1)S(1)}, f32[16,256]{1,0:T(8,128)S(1)}) custom-call(f32[4096,128]{1,0:T(8,128)S(1)} %bitcast.3), custom_call_target="tpu_custom_call" | custom-call | tf_op jit(solution)/shard_map/basis_products/pallas_call | solution.py:133
  18.7 0.0 collective-permute-done.low_ref
  18.7 4.3 %collective-permute-done.1.high_ref = f32[16,4,8,128]{3,2,1,0:T(8,128)S(1)} collective-permute-done((f32[16,4,8,128]{3,2,1,0:T(8,128)S(1)}, f32[16,4,8,128]{3,2,1,0:T(8,128)S(1)}, u32[]{:S(2)}, u32[]{:S(2)}) %collective-permute-start.1) | collective-permute-done | bytes 262176 | tf_op jit(solution)/shard_map/ppermute | solution.py:339
  23.0 0.0 collective-permute-done.2.late_ref
  23.0 0.0 copy-done.8
  23.0 3.9 %image_products.1 = (bf16[48,8192]{1,0:T(8,128)(2,1)S(1)}, f32[16,2,16,128]{3,2,1,0:T(8,128)S(1)}) custom-call(s32[4]{0:T(128)S(1)} %copy-done.6, s32[4]{0:T(128)S(1)} %copy-done.8, f32[4096,128]{1,0:T(8,128)S(1)} %bitcast.4, f32[16,4,8,128]{3,2,1,0:T(8,128)S(1)} %collective-permute-done.low_ref, f32[16,4,8,128]{3,2,1,0:T(8,128)S(1)} %collective-permute-done.1.high_ref, ...), custom_call_target="tpu_custom_call" | custom-call | tf_op jit(solution)/shard_map/image_products/pallas_call | solution.py:222
  26.9 0.9 %copy-done.4 = bf16[48,8192]{1,0:T(8,128)(2,1)} copy-done((bf16[48,8192]{1,0:T(8,128)(2,1)}, bf16[48,8192]{1,0:T(8,128)(2,1)S(1)}, u32[]{:S(2)}) %copy-start.4) | copy-done | bytes 786456
  27.8 18.8 %all_to_all.10 = f32[16,2,16,128]{3,2,1,0:T(8,128)S(1)} all-to-all(f32[16,2,16,128]{3,2,1,0:T(8,128)S(1)} %get-tuple-element.18), channel_id=1, replica_groups=mesh['y'=8,'core'=2,'x'=4,'z'=8] {'y','core'}, dimensions={0} | all-to-all | bytes 524288 | tf_op jit(solution)/shard_map/all_to_all | solution.py:327
  46.6 0.9 %broadcast_in_dim.3 = f32[32,2,16,128]{3,2,1,0:T(8,128)} broadcast(f32[2,16,128]{2,1,0:T(8,128)S(1)} %reduce_sum.9), dimensions={1,2,3} | broadcast | bytes 540672 | tf_op jit(solution)/shard_map/broadcast_in_dim | solution.py:346
  47.4 12.4 %all-to-all-start.1 = ((f32[32,2,16,128]{3,2,1,0:T(8,128)}), f32[32,2,16,128]{3,2,1,0:T(8,128)}, u32[]{:S(2)}, u32[]{:S(2)}) async-start(f32[32,2,16,128]{3,2,1,0:T(8,128)} %broadcast_in_dim.3), calls=%async_computation.1 | async-start | bytes 1048576 | tf_op jit(solution)/shard_map/all_to_all | solution.py:327
  59.8 3.3 %pad_maximum_fusion.parts_ref = bf16[240,8192]{1,0:T(8,128)(2,1)} fusion(bf16[48,8192]{1,0:T(8,128)(2,1)} %copy-done.4, bf16[192,8192]{1,0:T(8,128)(2,1)S(1)} %get-tuple-element.16.basis_ref), kind=kLoop, calls=%fused_computation | loop fusion | flops 7864320 | bytes 7864320 | tf_op jit(solution)/shard_map/concatenate | solution.py:347
  63.1 13.2 %all-to-all-done.1.sums_ref = f32[32,2,16,128]{3,2,1,0:T(8,128)} async-done(((f32[32,2,16,128]{3,2,1,0:T(8,128)}), f32[32,2,16,128]{3,2,1,0:T(8,128)}, u32[]{:S(2)}, u32[]{:S(2)}) %all-to-all-start.1) | async-done | bytes 524320 | tf_op jit(solution)/shard_map/all_to_all | solution.py:327
  76.3 2.1 %copy-done.3 = bf16[240,8192]{1,0:T(8,128)(2,1)S(1)} copy-done((bf16[240,8192]{1,0:T(8,128)(2,1)S(1)}, bf16[240,8192]{1,0:T(8,128)(2,1)}, u32[]{:S(2)}) %copy-start.3) | copy-done | bytes 3932184
  78.4 5.1 %finish.1 = (f32[64,16]{1,0:T(8,128)}, f32[16,16]{1,0:T(8,128)}, f32[1024,128]{1,0:T(8,128)}) custom-call(f32[32,2,16,128]{3,2,1,0:T(8,128)} %all-to-all-done.1.sums_ref, bf16[240,8192]{1,0:T(8,128)(2,1)S(1)} %copy-done.3), custom_call_target="tpu_custom_call" | custom-call | tf_op jit(solution)/shard_map/finish/pallas_call | solution.py:312
  (10 shorter events, 0.0 us)
Async XLA Ops:
  0.6 1.6 %copy-start = (f32[4,16,4,2,8,128]{5,4,3,2,1,0:T(8,128)S(1)}, f32[4,16,4,2,8,128]{5,4,3,2,1,0:T(8,128)}, u32[]{:S(2)}) copy-start(f32[4,16,4,2,8,128]{5,4,3,2,1,0:T(8,128)} %basis_ref.1) | copy-start | bytes 6291460
  2.2 0.7 copy-start.5
  2.9 0.7 copy-start.7
  3.5 19.5 %copy-start.2 = (f32[4,16,4,2,8,128]{5,4,3,2,1,0:T(8,128)S(1)}, f32[4,16,4,2,8,128]{5,4,3,2,1,0:T(8,128)}, u32[]{:S(2)}) copy-start(f32[4,16,4,2,8,128]{5,4,3,2,1,0:T(8,128)} %basis_ref.1) | copy-start | bytes 6291460
  3.5 19.5 %copy-start.6 = (s32[4]{0:T(128)S(1)}, s32[4]{0:T(128)}, u32[]{:S(2)}) copy-start(s32[4]{0:T(128)} %num_ref.3) | copy-start | bytes 52
  3.5 19.5 %copy-start.8 = (s32[4]{0:T(128)S(1)}, s32[4]{0:T(128)}, u32[]{:S(2)}) copy-start(s32[4]{0:T(128)} %den_ref.3) | copy-start | bytes 52
  4.2 18.8 %collective-permute-start.2 = (f32[17,2,2,8,128]{4,3,2,1,0:T(8,128)S(1)}, f32[17,2,2,8,128]{4,3,2,1,0:T(8,128)S(1)}, u32[]{:S(2)}, u32[]{:S(2)}) collective-permute-start(f32[17,2,2,8,128]{4,3,2,1,0:T(8,128)S(1)} %get-tuple-element.15), channel_id=1, source_target_pairs={{0,32},{32,64},{64,96},{96,128},{128,160},{160,192},{192,224},{224... | collective-permute-start | bytes 835592 | tf_op jit(solution)/shard_map/ppermute | solution.py:340
  8.8 9.8 %collective-permute-start = (f32[16,4,8,128]{3,2,1,0:T(8,128)S(1)}, f32[16,4,8,128]{3,2,1,0:T(8,128)S(1)}, u32[]{:S(2)}, u32[]{:S(2)}) collective-permute-start(f32[16,4,8,128]{3,2,1,0:T(8,128)S(1)} %get-tuple-element.13), channel_id=1, source_target_pairs={{0,1},{1,2},{2,3},{3,4},{4,5},{5,6},{6,7},{7,8},{8,9},{9,10},{10,1... | collective-permute-start | bytes 786440 | tf_op jit(solution)/shard_map/ppermute | solution.py:338
  12.8 10.2 %collective-permute-start.1 = (f32[16,4,8,128]{3,2,1,0:T(8,128)S(1)}, f32[16,4,8,128]{3,2,1,0:T(8,128)S(1)}, u32[]{:S(2)}, u32[]{:S(2)}) collective-permute-start(f32[16,4,8,128]{3,2,1,0:T(8,128)S(1)} %get-tuple-element.14), channel_id=1, source_target_pairs={{1,0},{2,1},{3,2},{4,3},{5,4},{6,5},{7,6},{8,7},{9,8},{10,9},{11,1... | collective-permute-start | bytes 786440 | tf_op jit(solution)/shard_map/ppermute | solution.py:339
  14.1 1.6 %copy-start.1 = (f32[4,16,4,2,8,128]{5,4,3,2,1,0:T(8,128)S(1)}, f32[4,16,4,2,8,128]{5,4,3,2,1,0:T(8,128)}, u32[]{:S(2)}) copy-start(f32[4,16,4,2,8,128]{5,4,3,2,1,0:T(8,128)} %basis_ref.1) | copy-start | bytes 6291460
  26.9 0.9 %copy-start.4 = (bf16[48,8192]{1,0:T(8,128)(2,1)}, bf16[48,8192]{1,0:T(8,128)(2,1)S(1)}, u32[]{:S(2)}) copy-start(bf16[48,8192]{1,0:T(8,128)(2,1)S(1)} %get-tuple-element.19) | copy-start | bytes 2359300
  47.4 28.9 %all-to-all-start.1 = ((f32[32,2,16,128]{3,2,1,0:T(8,128)}), f32[32,2,16,128]{3,2,1,0:T(8,128)}, u32[]{:S(2)}, u32[]{:S(2)}) async-start(f32[32,2,16,128]{3,2,1,0:T(8,128)} %broadcast_in_dim.3), calls=%async_computation.1 | async-start | bytes 1048576 | tf_op jit(solution)/shard_map/all_to_all | solution.py:327
  76.3 2.1 %copy-start.3 = (bf16[240,8192]{1,0:T(8,128)(2,1)S(1)}, bf16[240,8192]{1,0:T(8,128)(2,1)}, u32[]{:S(2)}) copy-start(bf16[240,8192]{1,0:T(8,128)(2,1)} %pad_maximum_fusion.parts_ref) | copy-start | bytes 11796484

commit v3 on v2

--- a/solution.py
+++ b/solution.py
@@ -17,6 +17,8 @@
 CELLS = LINES * 128
 TOTAL = 64 * 64 * 8 * 128
 PARTS = 3
+GROUPS = 16
+SLABS = 32
 FULL = ROWS + COLS
 HIGHEST = lax.Precision.HIGHEST
 F32 = jnp.float32
@@ -29,6 +31,10 @@
     return pltpu.CompilerParams(vmem_limit_bytes=megabytes * 1024 * 1024)
 
 
+def in_hbm(array):
+    return pltpu.with_memory_space_constraint(array, pltpu.HBM)
+
+
 def size_of(axes):
     count = 1
     for axis in axes:
@@ -44,31 +50,33 @@
     return first, second, third
 
 
-def step_sizes(num_ref, den_ref):
-    sizes = []
+def edges_kernel(
+    num_hbm, den_hbm, basis_hbm, up_ref, down_ref, late_ref, sizes_ref, num_ref, den_ref, tail_ref, sems
+):
+    last = BLOCKS - 1
+    counts = [
+        pltpu.make_async_copy(num_hbm, num_ref, sems.at[4]),
+        pltpu.make_async_copy(den_hbm, den_ref, sems.at[5]),
+    ]
+    copies = [
+        pltpu.make_async_copy(basis_hbm.at[last, :, :, PLANES - 1], up_ref, sems.at[0]),
+        pltpu.make_async_copy(basis_hbm.at[last, :, :, 0], down_ref, sems.at[1]),
+        pltpu.make_async_copy(
+            basis_hbm.at[last, :, pl.ds(STEPS - 2, 2)], late_ref.at[pl.ds(0, COLS)], sems.at[2]
+        ),
+    ]
+    for copy in counts + copies:
+        copy.start()
+    for copy in counts:
+        copy.wait()
     for step in range(STEPS):
         top = jnp.full((8, 128), num_ref[step]).astype(F32)
         bottom = jnp.full((8, 128), den_ref[step]).astype(F32)
-        sizes.append(top / bottom)
-    return sizes
-
-
-def edges_kernel(num_ref, den_ref, basis_ref, up_ref, down_ref, late_ref, size_ref, sems):
-    last = BLOCKS - 1
-    copies = [
-        pltpu.make_async_copy(basis_ref.at[last, :, :, PLANES - 1], up_ref, sems.at[0]),
-        pltpu.make_async_copy(basis_ref.at[last, :, :, 0], down_ref, sems.at[1]),
-        pltpu.make_async_copy(
-            basis_ref.at[last, :, pl.ds(STEPS - 2, 2)], late_ref.at[pl.ds(0, COLS)], sems.at[2]
-        ),
-    ]
-    for copy in copies:
-        copy.start()
-    final_size = step_sizes(num_ref, den_ref)[STEPS - 1]
+        sizes_ref[step] = top / bottom
     for step in range(2):
         for plane in range(PLANES):
-            size_ref[step, plane] = final_size
-    tail = pltpu.make_async_copy(size_ref, late_ref.at[COLS], sems.at[3])
+            tail_ref[step, plane] = sizes_ref[STEPS - 1]
+    tail = pltpu.make_async_copy(tail_ref, late_ref.at[COLS], sems.at[3])
     tail.start()
     for copy in copies:
         copy.wait()
@@ -76,7 +84,8 @@
 
 
 def edges(basis, num, den):
-    smem = pl.BlockSpec(memory_space=pltpu.SMEM)
+    hbm = pl.BlockSpec(memory_space=pltpu.HBM)
+    vmem = pl.BlockSpec(memory_space=pltpu.VMEM)
     anywhere = pl.BlockSpec(memory_space=pl.ANY)
     return pl.pallas_call(
         edges_kernel,
@@ -84,24 +93,30 @@
             jax.ShapeDtypeStruct((COLS, STEPS, 8, 128), F32),
             jax.ShapeDtypeStruct((COLS, STEPS, 8, 128), F32),
             jax.ShapeDtypeStruct((COLS + 1, 2, PLANES, 8, 128), F32),
+            jax.ShapeDtypeStruct((STEPS, 8, 128), F32),
         ),
-        in_specs=[smem, smem, anywhere],
-        out_specs=(anywhere, anywhere, anywhere),
-        scratch_shapes=[pltpu.VMEM((2, PLANES, 8, 128), F32), pltpu.SemaphoreType.DMA((4,))],
+        in_specs=[hbm, hbm, hbm],
+        out_specs=(anywhere, anywhere, anywhere, vmem),
+        scratch_shapes=[
+            pltpu.SMEM((STEPS,), jnp.int32),
+            pltpu.SMEM((STEPS,), jnp.int32),
+            pltpu.VMEM((2, PLANES, 8, 128), F32),
+            pltpu.SemaphoreType.DMA((6,)),
+        ],
         compiler_params=params(4),
         name="edges",
-    )(num, den, basis)
-
-
-def gathered_rows(field_ref, parts_ref, count):
+    )(in_hbm(num), in_hbm(den), in_hbm(basis))
+
+
+def gather_block(field_ref, parts_ref, row, stride):
     @pl.loop(0, TILES)
     def _(tile):
         for line in range(8):
             place = tile * 8 + line
-            value = field_ref[pl.ds(place, count, stride=LINES), :]
+            value = field_ref[pl.ds(place, COLS, stride=LINES), :]
             lanes = pl.ds(pl.multiple_of(place * 128, 128), 128)
             for part, piece in enumerate(split(value)):
-                parts_ref[pl.ds(part * count, count), lanes] = piece
+                parts_ref[pl.ds(row + part * stride, COLS), lanes] = piece
 
 
 def part_products(products, count, offset, width):
@@ -115,39 +130,51 @@
     return total
 
 
-def basis_kernel(field_ref, parts_ref, packed_ref):
-    gathered_rows(field_ref, parts_ref, ROWS)
-    whole = parts_ref[...]
+def basis_kernel(flat_hbm, parts_ref, gram_ref, last_ref, field_ref, sems):
+    per_block = COLS * LINES
+    copies = []
+    for block in range(BLOCKS):
+        rows = pl.ds(block * per_block, per_block)
+        target = last_ref if block == BLOCKS - 1 else field_ref.at[block]
+        copies.append(pltpu.make_async_copy(flat_hbm.at[rows], target, sems.at[block]))
+        copies[-1].start()
+    for block in range(BLOCKS):
+        copies[block].wait()
+        source = last_ref if block == BLOCKS - 1 else field_ref.at[block]
+        gather_block(source, parts_ref, block * COLS, ROWS)
+    whole = parts_ref[: PARTS * ROWS]
     products = lax.dot_general(whole, whole, NT, preferred_element_type=F32)
     gram = part_products(products, ROWS, 0, ROWS)
-    pieces = [jnp.zeros((COLS, FULL), F32)]
-    for block in range(BLOCKS):
-        pieces.append(gram[block * COLS : (block + 1) * COLS, block * COLS :])
-    used = FULL + sum(ROWS - block * COLS for block in range(BLOCKS))
-    pieces.append(jnp.zeros((COLS, 256 - used), F32))
-    packed_ref[...] = jnp.concatenate(pieces, axis=1)
+    packed = jnp.concatenate([gram[: ROWS // 2], gram[ROWS // 2 :]], axis=1)
+    for piece in range(GROUPS):
+        gram_ref[piece] = packed[piece * 2 : piece * 2 + 2]
 
 
 def basis_products(flat):
     vmem = pl.BlockSpec(memory_space=pltpu.VMEM)
+    per_block = COLS * LINES
     return pl.pallas_call(
         basis_kernel,
         out_shape=(
-            jax.ShapeDtypeStruct((PARTS * ROWS, CELLS), BF16),
-            jax.ShapeDtypeStruct((COLS, 256), F32),
+            jax.ShapeDtypeStruct((PARTS * FULL, CELLS), BF16),
+            jax.ShapeDtypeStruct((GROUPS, 2, 128), F32),
+            jax.ShapeDtypeStruct((per_block, 128), F32),
         ),
-        in_specs=[vmem],
-        out_specs=(vmem, vmem),
+        in_specs=[pl.BlockSpec(memory_space=pltpu.HBM)],
+        out_specs=(vmem, vmem, vmem),
+        scratch_shapes=[
+            pltpu.VMEM((BLOCKS - 1, per_block, 128), F32),
+            pltpu.SemaphoreType.DMA((BLOCKS,)),
+        ],
         compiler_params=params(20),
         name="basis_products",
-    )(flat)
+    )(in_hbm(flat))
 
 
 def image_kernel(
-    num_ref, den_ref, field_ref, low_ref, high_ref, late_ref, basis_ref, packed_ref,
-    parts_ref, copies_ref, image_ref,
+    sizes_ref, field_ref, low_ref, high_ref, late_ref, parts_in_ref, parts_ref, main_ref, image_ref
 ):
-    sizes = step_sizes(num_ref, den_ref)
+    sizes = [sizes_ref[step] for step in range(STEPS)]
     first = (lax.axis_index("y") == 0) & (lax.axis_index("core") == 0)
     start = jnp.full((8, 128), first.astype(jnp.int32)) == 1
     weights = []
@@ -197,80 +224,89 @@
                 place = pl.multiple_of(col * LINES + (step * PLANES + plane) * 8, 8)
                 image_ref[pl.ds(place, 8), :] = result
 
-    gathered_rows(image_ref, parts_ref, COLS)
-    own_parts = parts_ref[...]
-    with_basis = lax.dot_general(own_parts, basis_ref[...], NT, preferred_element_type=F32)
-    with_self = lax.dot_general(own_parts, own_parts, NT, preferred_element_type=F32)
-    main = jnp.concatenate(
-        [
-            part_products(with_basis, COLS, 0, ROWS),
-            part_products(with_self, COLS, 0, COLS),
-            jnp.zeros((COLS, 256 - FULL), F32),
-        ],
-        axis=1,
-    )
-    payload = main + packed_ref[...]
-    for copy in range(copies_ref.shape[0]):
-        copies_ref[copy, 0] = payload[:, :128]
-        copies_ref[copy, 1] = payload[:, 128:]
-
-
-def image_products(num, den, flat, low, high, late, basis_parts, packed, count):
-    smem = pl.BlockSpec(memory_space=pltpu.SMEM)
+    base = PARTS * ROWS
+    gather_block(image_ref, parts_ref, base, COLS)
+    own_parts = parts_ref[base:]
+    products = lax.dot_general(own_parts, parts_ref[...], NT, preferred_element_type=F32)
+    proj = part_products(products, COLS, 0, ROWS)
+    gram = part_products(products, COLS, base, COLS)
+    packed = jnp.concatenate([proj[:8], proj[8:]], axis=1)
+    main_ref[0] = packed[:4]
+    main_ref[1] = packed[4:]
+    for half in range(2):
+        pieces = [gram[half * 8 + row : half * 8 + row + 1] for row in range(8)]
+        main_ref[2, half : half + 1] = jnp.concatenate(pieces, axis=1)
+    main_ref[2, 2:4] = jnp.zeros((2, 128), F32)
+
+
+def image_products(sizes, field, low, high, late, parts):
     vmem = pl.BlockSpec(memory_space=pltpu.VMEM)
-    per_block = COLS * LINES
     return pl.pallas_call(
         image_kernel,
-        grid=(1,),
         out_shape=(
-            jax.ShapeDtypeStruct((PARTS * COLS, CELLS), BF16),
-            jax.ShapeDtypeStruct((count, 2, COLS, 128), F32),
+            jax.ShapeDtypeStruct((PARTS * FULL, CELLS), BF16),
+            jax.ShapeDtypeStruct((3, 4, 128), F32),
         ),
-        in_specs=[
-            smem,
-            smem,
-            pl.BlockSpec((per_block, 128), lambda i: (BLOCKS - 1, 0)),
-            vmem,
-            vmem,
-            vmem,
-            vmem,
-            vmem,
-        ],
+        in_specs=[vmem] * 6,
         out_specs=(vmem, vmem),
-        scratch_shapes=[pltpu.VMEM((per_block, 128), F32)],
+        scratch_shapes=[pltpu.VMEM((COLS * LINES, 128), F32)],
+        input_output_aliases={5: 0},
         compiler_params=params(20),
         name="image_products",
-    )(num, den, flat, low, high, late, basis_parts, packed)
-
-
-def finish_kernel(sums_ref, parts_ref, hess_ref, triangle_ref, next_ref):
+    )(sizes, field, low, high, late, parts)
+
+
+def join_kernel(main_ref, gram_ref, copies_ref):
+    gram = gram_ref[0]
+    for piece in range(1, GROUPS):
+        gram = gram + gram_ref[piece]
+    for copy in range(SLABS):
+        copies_ref[copy, 0] = main_ref[0]
+        copies_ref[copy, 1] = main_ref[1]
+        copies_ref[copy, 2, 0:2] = main_ref[2, 0:2]
+        copies_ref[copy, 2, 2:4] = gram
+
+
+def join(main, gram):
+    vmem = pl.BlockSpec(memory_space=pltpu.VMEM)
+    return pl.pallas_call(
+        join_kernel,
+        out_shape=jax.ShapeDtypeStruct((SLABS, 3, 4, 128), F32),
+        in_specs=[vmem, vmem],
+        out_specs=vmem,
+        compiler_params=params(4),
+        name="join",
+    )(main, gram)
+
+
+def finish_kernel(sums_ref, parts_ref, hess_ref, triangle_ref, next_ref, gram_ref):
     sums = sums_ref[0]
-    for piece in range(1, sums_ref.shape[0]):
+    for piece in range(1, GROUPS):
         sums = sums + sums_ref[piece]
+    for piece in range(GROUPS):
+        gram_ref[piece * 2 : piece * 2 + 2] = sums_ref[piece, 2, 2:4]
     sums = sums * (1.0 / TOTAL)
-    left, right = sums[0], sums[1]
-    packed = jnp.concatenate([left, right], axis=1)
-    proj = packed[:, :ROWS]
-    image_gram = packed[:, ROWS:FULL]
+    proj = jnp.concatenate(
+        [sums[0, :, :ROWS], sums[1, :, :ROWS], sums[0, :, ROWS:], sums[1, :, ROWS:]], axis=0
+    )
+    image_gram = jnp.concatenate(
+        [
+            sums[2, half : half + 1, line * COLS : (line + 1) * COLS]
+            for half in range(2)
+            for line in range(8)
+        ],
+        axis=0,
+    )
     row = lax.broadcasted_iota(jnp.int32, (COLS, COLS), 0)
     col = lax.broadcasted_iota(jnp.int32, (COLS, COLS), 1)
-    upper = []
-    offset = FULL
-    for block in range(BLOCKS):
-        width = ROWS - block * COLS
-        rows = packed[:, offset : offset + width]
-        pieces = [0.5 * rows[:, :COLS]]
-        if block:
-            pieces.insert(0, jnp.zeros((COLS, block * COLS), F32))
-        if width > COLS:
-            pieces.append(rows[:, COLS:])
-        upper.append(jnp.concatenate(pieces, axis=1))
-        offset += width
-    half = jnp.concatenate(upper, axis=0)
-    carried = lax.dot_general(proj, half, NN, precision=HIGHEST, preferred_element_type=F32) - proj
-    cross = lax.dot_general(carried, proj, NT, precision=HIGHEST, preferred_element_type=F32)
-    cross_t = lax.dot_general(proj, carried, NT, precision=HIGHEST, preferred_element_type=F32)
-    gram = image_gram + (cross + cross_t)
+    packed = gram_ref[...] * (1.0 / TOTAL)
+    basis_gram = jnp.concatenate([packed[:, :ROWS], packed[:, ROWS:]], axis=0)
+    carried = lax.dot_general(
+        proj, basis_gram, NN, precision=HIGHEST, preferred_element_type=F32
+    ) - 2.0 * proj
+    gram = image_gram + lax.dot_general(
+        carried, proj, NT, precision=HIGHEST, preferred_element_type=F32
+    )
     eye = jnp.where(row == col, 1.0, 0.0).astype(F32)
     work = jnp.concatenate(
         [gram, -proj, eye, jnp.zeros((COLS, 128 - FULL - COLS), F32)], axis=1
@@ -318,6 +354,7 @@
         ),
         in_specs=[vmem, vmem],
         out_specs=(vmem, vmem, vmem),
+        scratch_shapes=[pltpu.VMEM((ROWS // 2, 128), F32)],
         compiler_params=params(20),
         name="finish",
     )(sums, parts)
@@ -334,17 +371,15 @@
     below = [(i + 1, i) for i in range(slabs - 1)]
     later = [(i, i + 1) for i in range(groups - 1)]
     flat = basis.reshape(ROWS * LINES, 128)
-    up, down, late = edges(basis, num, den)
+    up, down, late, sizes = edges(basis, num, den)
     low = lax.ppermute(up, SPACE, above)
     high = lax.ppermute(down, SPACE, below)
     earlier = lax.ppermute(late, TM, later)
-    basis_parts, packed = basis_products(flat)
-    image_parts, copies = image_products(
-        num, den, flat, low, high, earlier, basis_parts, packed, groups
-    )
-    sums = exchanged(copies, TM).sum(0)
-    sums = exchanged(jnp.broadcast_to(sums, (slabs,) + sums.shape), SPACE)
-    parts = jnp.concatenate([basis_parts, image_parts], axis=0)
+    parts, basis_gram, field = basis_products(flat)
+    basis_gram = exchanged(basis_gram, TM)
+    parts, main = image_products(sizes, field, low, high, earlier, parts)
+    sums = exchanged(join(main, basis_gram), SPACE).sum(0)
+    sums = exchanged(jnp.broadcast_to(sums, (groups,) + sums.shape), TM)
     hess, triangle, following = finish(sums, parts)
     return (
         hess.reshape(BLOCKS, COLS, COLS),

time: 84 us -> 79.8 us (0.950)
  blocking collectives: 18.8 us -> 41.5 us
  waiting for transfers between devices: 17.6 us -> 0.01 us
  starting transfers between devices: 22.3 us -> 16.2 us
  other arithmetic: 3.27 us -> 0.05 us
    all_to_all x1 -> x2, blocking collectives: 18.8 us -> 41.5 us  [exchanged(): return lax.all_to_all(copies, axes, 0, 0)]
    all_to_all x1, waiting for transfers between devices: 13.2 us -> 0.01 us  [exchanged(): return lax.all_to_all(copies, axes, 0, 0)]
    all_to_all x1, starting transfers between devices: 12.4 us -> 6.33 us  [exchanged(): return lax.all_to_all(copies, axes, 0, 0)]
    ppermute x1, waiting for transfers between devices: 4.35 us -> 0.01 us  [per_device(): high = lax.ppermute(down, SPACE, below)]
    concatenate x1 -> x0, other arithmetic: 3.25 us -> none  [per_device(): parts = jnp.concatenate([basis_parts, image_parts], axis=0)]
    pallas_call x1, Pallas kernels: 5.07 us -> 3.85 us  [finish(): pl.pallas_call(finish_kernel, out_shape=(jax.ShapeDtypeStruct((ROWS, COLS...]
    pallas_call x2 -> x3, Pallas kernels: 6.78 us -> 7.95 us  [the longest x1 4.56 us: basis_products(): pl.pallas_call(basis_kernel, out_shape=(jax.ShapeDtypeStruct((PARTS * FUL...]
    unnamed x18 -> x8, local copies, waits for them, and re-layouts: 7.48 us -> 7.95 us
  transfers between devices with their start and end apart: 4 -> 4, of which waited for: 2 -> 0; matrix products, arithmetic and copies ran while one was open for 4% -> 0% of each run, Pallas kernels for 4% -> 10%
where the time goes in v3:
time: 79.8 us; the launch traced here: 79.4 us
  blocking collectives  41.5 us (52%)
  starting transfers between devices  16.2 us (20%)
  Pallas kernels  13 us (16%)
  local copies, waits for them, and re-layouts  7.97 us (10%)
    all_to_all x2, blocking collectives, exchanged(): return lax.all_to_all(copies, axes, 0, 0)  41.5 us
    unnamed x8, local copies, waits for them, and re-layouts  7.95 us
    all_to_all x1, starting transfers between devices, exchanged(): return lax.all_to_all(copies, axes, 0, 0)  6.33 us
    ppermute x1, starting transfers between devices, per_device(): earlier = lax.ppermute(late, TM, later)  4.59 us
    pallas_call x1, Pallas kernels, basis_products(): pl.pallas_call(basis_kernel, out_shape=(jax.ShapeDtypeStruct((PARTS * FUL...  4.56 us
    ppermute x1, starting transfers between devices, per_device(): low = lax.ppermute(up, SPACE, above)  4.01 us
    pallas_call x1, Pallas kernels, finish(): pl.pallas_call(finish_kernel, out_shape=(jax.ShapeDtypeStruct((ROWS, COLS...  3.85 us
    pallas_call x1, Pallas kernels, image_products(): pl.pallas_call(image_kernel, out_shape=(jax.ShapeDtypeStruct((PARTS * FUL...  3.35 us
  transfers between devices with their start and end apart: 4, of which 0 were waited for; matrix products, arithmetic and copies ran while one was open for 0% of the time, Pallas kernels for 10%

profile of v3, /device:TPU:1, one launch (start us, length us, event | category | flops | bytes accessed | tf_op | source)
XLA Modules:
  0.0 79.4 jit_solution(8373980433595202855)
XLA Ops:
  0.6 1.2 %edges.1 = (f32[16,4,8,128]{3,2,1,0:T(8,128)S(1)}, f32[16,4,8,128]{3,2,1,0:T(8,128)S(1)}, f32[17,2,2,8,128]{4,3,2,1,0:T(8,128)S(1)}, f32[4,8,128]{2,1,0:T(8,128)S(1)}) custom-call(s32[4]{0:T(128)} %num_hbm.1, s32[4]{0:T(128)} %den_hbm.1, f32[4,16,4,2,8,128]{5,4,3,2,1,0:T(8,128)} %basis_hbm.1), custom_call_target="tpu_custom_call" | custom-call | tf_op jit(solution)/shard_map/edges/pallas_call | solution.py:90
  1.8 4.6 %collective-permute-start.2 = (f32[17,2,2,8,128]{4,3,2,1,0:T(8,128)S(1)}, f32[17,2,2,8,128]{4,3,2,1,0:T(8,128)S(1)}, u32[]{:S(2)}, u32[]{:S(2)}) collective-permute-start(f32[17,2,2,8,128]{4,3,2,1,0:T(8,128)S(1)} %get-tuple-element.19), channel_id=1, source_target_pairs={{0,32},{32,64},{64,96},{96,128},{128,160},{160,192},{192,224},{224... | collective-permute-start | bytes 835592 | tf_op jit(solution)/shard_map/ppermute | solution.py:377
  6.4 4.0 %collective-permute-start = (f32[16,4,8,128]{3,2,1,0:T(8,128)S(1)}, f32[16,4,8,128]{3,2,1,0:T(8,128)S(1)}, u32[]{:S(2)}, u32[]{:S(2)}) collective-permute-start(f32[16,4,8,128]{3,2,1,0:T(8,128)S(1)} %get-tuple-element.17), channel_id=1, source_target_pairs={{0,1},{1,2},{2,3},{3,4},{4,5},{5,6},{6,7},{7,8},{8,9},{9,10},{10,1... | collective-permute-start | bytes 786440 | tf_op jit(solution)/shard_map/ppermute | solution.py:375
  10.4 1.3 %collective-permute-start.1 = (f32[16,4,8,128]{3,2,1,0:T(8,128)S(1)}, f32[16,4,8,128]{3,2,1,0:T(8,128)S(1)}, u32[]{:S(2)}, u32[]{:S(2)}) collective-permute-start(f32[16,4,8,128]{3,2,1,0:T(8,128)S(1)} %get-tuple-element.18), channel_id=1, source_target_pairs={{1,0},{2,1},{3,2},{4,3},{5,4},{6,5},{7,6},{8,7},{9,8},{10,9},{11,1... | collective-permute-start | bytes 786440 | tf_op jit(solution)/shard_map/ppermute | solution.py:376
  11.7 4.6 %basis_products.1 = (bf16[240,8192]{1,0:T(8,128)(2,1)S(1)}, f32[16,2,128]{2,1,0:T(2,128)}, f32[1024,128]{1,0:T(8,128)S(1)}) custom-call(f32[4096,128]{1,0:T(8,128)} %bitcast.3), custom_call_target="tpu_custom_call" | custom-call | tf_op jit(solution)/shard_map/basis_products/pallas_call | solution.py:156
  16.3 0.0 copy-start
  16.3 1.9 %copy-done = bf16[240,8192]{1,0:T(8,128)(2,1)} copy-done((bf16[240,8192]{1,0:T(8,128)(2,1)}, bf16[240,8192]{1,0:T(8,128)(2,1)S(1)}, u32[]{:S(2)}) %copy-start) | copy-done | bytes 3932184
  18.2 6.3 %all-to-all-start = ((f32[16,2,128]{2,1,0:T(2,128)}), f32[16,2,128]{2,1,0:T(2,128)S(1)}, u32[]{:S(2)}, u32[]{:S(2)}) async-start(f32[16,2,128]{2,1,0:T(2,128)} %get-tuple-element.22), calls=%async_computation | async-start | bytes 32768 | tf_op jit(solution)/shard_map/all_to_all | solution.py:364
  24.5 0.0 collective-permute-done.low_ref
  24.5 0.0 collective-permute-done.1.high_ref
  24.5 0.0 collective-permute-done.2.late_ref
  24.5 0.0 copy-start.1
  24.5 2.1 %copy-done.1 = bf16[240,8192]{1,0:T(8,128)(2,1)S(1)} copy-done((bf16[240,8192]{1,0:T(8,128)(2,1)S(1)}, bf16[240,8192]{1,0:T(8,128)(2,1)}, u32[]{:S(2)}) %copy-start.1) | copy-done | bytes 3932184
  26.6 3.4 %image_products.1 = (bf16[240,8192]{1,0:T(8,128)(2,1)S(1)}, f32[3,4,128]{2,1,0:T(4,128)S(1)}) custom-call(f32[4,8,128]{2,1,0:T(8,128)S(1)} %get-tuple-element.15.sizes_ref, f32[1024,128]{1,0:T(8,128)S(1)} %get-tuple-element.16.field_ref, f32[16,4,8,128]{3,2,1,0:T(8,128)S(1)} %collective-permute-done.low_ref, ...), custom_call_target="tpu_custom_call", output_to_operand_aliasing={{0}: (5, {})} | custom-call | tf_op jit(solution)/shard_map/image_products/pallas_call | solution.py:244
  30.0 0.0 copy-start.2
  30.0 1.9 %copy-done.2 = bf16[240,8192]{1,0:T(8,128)(2,1)} copy-done((bf16[240,8192]{1,0:T(8,128)(2,1)}, bf16[240,8192]{1,0:T(8,128)(2,1)S(1)}, u32[]{:S(2)}) %copy-start.2) | copy-done | bytes 3932184
  31.9 0.0 all-to-all-done.gram_ref
  31.9 23.4 %all_to_all.15 = f32[32,3,4,128]{3,2,1,0:T(4,128)S(1)} all-to-all(f32[32,3,4,128]{3,2,1,0:T(4,128)S(1)} %join.1), channel_id=1, replica_groups=mesh['y'=8,'core'=2,'x'=4,'z'=8] {'x','z'}, dimensions={0} | all-to-all | bytes 393216 | tf_op jit(solution)/shard_map/all_to_all | solution.py:364
  55.3 0.1 reduce_sum.9
  55.4 18.1 %all_to_all.16.sums_ref = f32[16,3,4,128]{3,2,1,0:T(4,128)S(1)} all-to-all(f32[16,3,4,128]{3,2,1,0:T(4,128)S(1)} %broadcast_in_dim.3), channel_id=1, replica_groups=mesh['y'=8,'core'=2,'x'=4,'z'=8] {'y','core'}, dimensions={0} | all-to-all | bytes 196608 | tf_op jit(solution)/shard_map/all_to_all | solution.py:364
  73.5 0.0 copy-start.3
  73.5 2.1 %copy-done.3 = bf16[240,8192]{1,0:T(8,128)(2,1)S(1)} copy-done((bf16[240,8192]{1,0:T(8,128)(2,1)S(1)}, bf16[240,8192]{1,0:T(8,128)(2,1)}, u32[]{:S(2)}) %copy-start.3) | copy-done | bytes 3932184
  75.6 3.8 %finish.1 = (f32[64,16]{1,0:T(8,128)}, f32[16,16]{1,0:T(8,128)}, f32[1024,128]{1,0:T(8,128)}) custom-call(f32[16,3,4,128]{3,2,1,0:T(4,128)S(1)} %all_to_all.16.sums_ref, bf16[240,8192]{1,0:T(8,128)(2,1)S(1)} %copy-done.3), custom_call_target="tpu_custom_call" | custom-call | tf_op jit(solution)/shard_map/finish/pallas_call | solution.py:348
  (2 shorter events, 0.1 us)
Async XLA Ops:
  1.8 22.7 %collective-permute-start.2 = (f32[17,2,2,8,128]{4,3,2,1,0:T(8,128)S(1)}, f32[17,2,2,8,128]{4,3,2,1,0:T(8,128)S(1)}, u32[]{:S(2)}, u32[]{:S(2)}) collective-permute-start(f32[17,2,2,8,128]{4,3,2,1,0:T(8,128)S(1)} %get-tuple-element.19), channel_id=1, source_target_pairs={{0,32},{32,64},{64,96},{96,128},{128,160},{160,192},{192,224},{224... | collective-permute-start | bytes 835592 | tf_op jit(solution)/shard_map/ppermute | solution.py:377
  6.4 18.1 %collective-permute-start = (f32[16,4,8,128]{3,2,1,0:T(8,128)S(1)}, f32[16,4,8,128]{3,2,1,0:T(8,128)S(1)}, u32[]{:S(2)}, u32[]{:S(2)}) collective-permute-start(f32[16,4,8,128]{3,2,1,0:T(8,128)S(1)} %get-tuple-element.17), channel_id=1, source_target_pairs={{0,1},{1,2},{2,3},{3,4},{4,5},{5,6},{6,7},{7,8},{8,9},{9,10},{10,1... | collective-permute-start | bytes 786440 | tf_op jit(solution)/shard_map/ppermute | solution.py:375
  10.4 14.1 %collective-permute-start.1 = (f32[16,4,8,128]{3,2,1,0:T(8,128)S(1)}, f32[16,4,8,128]{3,2,1,0:T(8,128)S(1)}, u32[]{:S(2)}, u32[]{:S(2)}) collective-permute-start(f32[16,4,8,128]{3,2,1,0:T(8,128)S(1)} %get-tuple-element.18), channel_id=1, source_target_pairs={{1,0},{2,1},{3,2},{4,3},{5,4},{6,5},{7,6},{8,7},{9,8},{10,9},{11,1... | collective-permute-start | bytes 786440 | tf_op jit(solution)/shard_map/ppermute | solution.py:376
  16.3 1.9 %copy-start = (bf16[240,8192]{1,0:T(8,128)(2,1)}, bf16[240,8192]{1,0:T(8,128)(2,1)S(1)}, u32[]{:S(2)}) copy-start(bf16[240,8192]{1,0:T(8,128)(2,1)S(1)} %get-tuple-element.20.parts_in_ref) | copy-start | bytes 11796484
  18.2 13.7 %all-to-all-start = ((f32[16,2,128]{2,1,0:T(2,128)}), f32[16,2,128]{2,1,0:T(2,128)S(1)}, u32[]{:S(2)}, u32[]{:S(2)}) async-start(f32[16,2,128]{2,1,0:T(2,128)} %get-tuple-element.22), calls=%async_computation | async-start | bytes 32768 | tf_op jit(solution)/shard_map/all_to_all | solution.py:364
  24.5 2.1 %copy-start.1 = (bf16[240,8192]{1,0:T(8,128)(2,1)S(1)}, bf16[240,8192]{1,0:T(8,128)(2,1)}, u32[]{:S(2)}) copy-start(bf16[240,8192]{1,0:T(8,128)(2,1)} %copy-done) | copy-start | bytes 11796484
  30.0 1.9 %copy-start.2 = (bf16[240,8192]{1,0:T(8,128)(2,1)}, bf16[240,8192]{1,0:T(8,128)(2,1)S(1)}, u32[]{:S(2)}) copy-start(bf16[240,8192]{1,0:T(8,128)(2,1)S(1)} %get-tuple-element.23.parts_ref) | copy-start | bytes 11796484
  73.5 2.1 %copy-start.3 = (bf16[240,8192]{1,0:T(8,128)(2,1)S(1)}, bf16[240,8192]{1,0:T(8,128)(2,1)}, u32[]{:S(2)}) copy-start(bf16[240,8192]{1,0:T(8,128)(2,1)} %copy-done.2) | copy-start | bytes 11796484

commit v4 on v3

v4 whole, which is shorter than its diff:
```python
import jax
import jax.numpy as jnp
from jax import lax
from jax.experimental import pallas as pl
from jax.experimental.pallas import tpu as pltpu
from jax.sharding import Mesh, PartitionSpec as P

TM = ("y", "core")
SPACE = ("x", "z")
GROUPS = 16
SLABS = 32
COLS = 16
BLOCKS = 4
ROWS = BLOCKS * COLS
FULL = ROWS + COLS
STEPS = 4
PLANES = 2
LINES = 8
PLACES = STEPS * PLANES * LINES
CELLS = PLACES * 128
TOTAL = 64 * 64 * 8 * 128
PARTS = 3
CHUNKS = 4
HIGHEST = lax.Precision.HIGHEST
F32 = jnp.float32
BF16 = jnp.bfloat16
NT = (((1,), (1,)), ((), ()))
NN = (((1,), (0,)), ((), ()))
VMEM = pl.BlockSpec(memory_space=pltpu.VMEM)
HBM = pl.BlockSpec(memory_space=pltpu.HBM)


def params(megabytes):
    return pltpu.CompilerParams(vmem_limit_bytes=megabytes * 1024 * 1024)


def in_hbm(array):
    return pltpu.with_memory_space_constraint(array, pltpu.HBM)


def size_of(axes):
    count = 1
    for axis in axes:
        count *= lax.axis_size(axis)
    return count


def place_of(step, plane, line):
    return (step * PLANES + plane) * LINES + line


def split(value):
    first = value.astype(BF16)
    rest = value - first.astype(F32)
    second = rest.astype(BF16)
    third = (rest - second.astype(F32)).astype(BF16)
    return first, second, third


def faces_kernel(basis_hbm, up_ref, down_ref, sems):
    copies = []
    columns = pl.ds(ROWS - COLS, COLS)
    for step in range(STEPS):
        for line in range(LINES):
            for plane, target in ((PLANES - 1, up_ref), (0, down_ref)):
                source = basis_hbm.at[columns, place_of(step, plane, line), 0]
                copies.append(
                    pltpu.make_async_copy(
                        source, target.at[step * LINES + line], sems.at[len(copies)]
                    )
                )
    for copy in copies:
        copy.start()
    for copy in copies:
        copy.wait()


def faces(basis):
    face = jax.ShapeDtypeStruct((STEPS * LINES, COLS, 128), F32)
    return pl.pallas_call(
        faces_kernel,
        out_shape=(face, face),
        in_specs=[HBM],
        out_specs=(VMEM, VMEM),
        scratch_shapes=[pltpu.SemaphoreType.DMA((2 * STEPS * LINES,))],
        compiler_params=params(4),
        name="faces",
    )(in_hbm(basis))


def ending_kernel(
    num_hbm, den_hbm, basis_hbm, after_ref, late_ref, sizes_ref, num_ref, den_ref, sems
):
    counts = [
        pltpu.make_async_copy(num_hbm, num_ref, sems.at[0]),
        pltpu.make_async_copy(den_hbm, den_ref, sems.at[1]),
    ]
    copies = []
    columns = pl.ds(ROWS - COLS, COLS)
    first = place_of(STEPS - 2, 0, 0)
    for place in range(first, PLACES):
        copies.append(
            pltpu.make_async_copy(
                basis_hbm.at[columns, place, 0], late_ref.at[place - first], sems.at[2 + len(copies)]
            )
        )
    for copy in counts + copies:
        copy.start()
    for copy in counts:
        copy.wait()
    for step in range(STEPS):
        top = jnp.full((COLS, 128), num_ref[step]).astype(F32)
        bottom = jnp.full((COLS, 128), den_ref[step]).astype(F32)
        sizes_ref[step] = top / bottom
    late_ref[PLACES - first] = sizes_ref[STEPS - 1]
    for copy in copies:
        copy.wait()


def ending(num, den, basis, after):
    kept = 2 * PLANES * LINES
    return pl.pallas_call(
        ending_kernel,
        out_shape=(
            jax.ShapeDtypeStruct((kept + 1, COLS, 128), F32),
            jax.ShapeDtypeStruct((STEPS, COLS, 128), F32),
        ),
        in_specs=[HBM, HBM, HBM, pl.BlockSpec(memory_space=pl.ANY)],
        out_specs=(VMEM, VMEM),
        scratch_shapes=[
            pltpu.SMEM((STEPS,), jnp.int32),
            pltpu.SMEM((STEPS,), jnp.int32),
            pltpu.SemaphoreType.DMA((2 + kept,)),
        ],
        compiler_params=params(4),
        name="ending",
    )(in_hbm(num), in_hbm(den), in_hbm(basis), after)


def part_products(products, count, offset, width):
    total = None
    for b in range(PARTS):
        group = None
        for a in range(PARTS - b):
            piece = products[a * count : (a + 1) * count, offset + b * width : offset + (b + 1) * width]
            group = piece if group is None else group + piece
        total = group if total is None else total + group
    return total


def basis_kernel(basis_hbm, parts_ref, last_ref, keep_ref, give_ref, field_ref, sems):
    copies = [
        pltpu.make_async_copy(basis_hbm.at[:, place, 0], field_ref.at[place], sems.at[place])
        for place in range(PLACES)
    ]
    for copy in copies:
        copy.start()
    products = None
    per_chunk = PLACES // CHUNKS
    for chunk in range(CHUNKS):
        for place in range(chunk * per_chunk, (chunk + 1) * per_chunk):
            copies[place].wait()
            value = field_ref[place]
            last_ref[place] = value[ROWS - COLS :]
            for part, piece in enumerate(split(value)):
                parts_ref[part * ROWS : (part + 1) * ROWS, place * 128 : (place + 1) * 128] = piece
        lanes = slice(chunk * per_chunk * 128, (chunk + 1) * per_chunk * 128)
        piece = parts_ref[: PARTS * ROWS, lanes]
        product = lax.dot_general(piece, piece, NT, preferred_element_type=F32)
        products = product if products is None else products + product
    gram = part_products(products, ROWS, 0, ROWS)
    rows = [gram[block * COLS : (block + 1) * COLS, block * COLS :] for block in range(BLOCKS)]
    packed = jnp.concatenate([rows[0], rows[1], rows[3]], axis=1)
    halves = []
    for half in range(2):
        rest = rows[2][half * 8 : half * 8 + 8]
        rest = jnp.concatenate([rest[2 * i : 2 * i + 2] for i in range(4)], axis=1)
        halves.append((packed[half * 8 : half * 8 + 8], rest))
    own = lax.axis_index("core")
    first = jnp.full((8, 128), own) == 0
    for target, flip in ((keep_ref, False), (give_ref, True)):
        one, two = (halves[1], halves[0]) if flip else (halves[0], halves[1])
        target[0:8] = jnp.where(first, one[0], two[0])
        target[8:10] = jnp.where(first[:2], one[1], two[1])
        target[10:16] = jnp.zeros((6, 128), F32)


def basis_products(basis):
    return pl.pallas_call(
        basis_kernel,
        out_shape=(
            jax.ShapeDtypeStruct((PARTS * FULL, CELLS), BF16),
            jax.ShapeDtypeStruct((PLACES, COLS, 128), F32),
            jax.ShapeDtypeStruct((16, 128), F32),
            jax.ShapeDtypeStruct((16, 128), F32),
        ),
        in_specs=[HBM],
        out_specs=(VMEM, VMEM, VMEM, VMEM),
        scratch_shapes=[
            pltpu.VMEM((PLACES, ROWS, 128), F32),
            pltpu.SemaphoreType.DMA((PLACES,)),
        ],
        compiler_params=params(20),
        name="basis_products",
    )(in_hbm(basis))


def image_kernel(
    sizes_ref, field_ref, low_ref, high_ref, late_ref, keep_ref, got_ref, parts_in_ref,
    parts_ref, copies_ref,
):
    sizes = [sizes_ref[step] for step in range(STEPS)]
    first = (lax.axis_index("y") == 0) & (lax.axis_index("core") == 0)
    start = jnp.full((COLS, 128), first.astype(jnp.int32)) == 1
    weights = []
    for step in range(STEPS):
        if step == 0:
            before = jnp.where(start, sizes[0], late_ref[2 * PLANES * LINES])
        else:
            before = sizes[step - 1]
        ratio = sizes[step] / before
        now = (1.0 + 2.0 * ratio) / (1.0 + ratio)
        one = 1.0 + ratio
        two = ratio * ratio / (1.0 + ratio)
        if step == 0:
            now = jnp.where(start, 1.0, now)
            one = jnp.where(start, 1.0, one)
            two = jnp.where(start, 0.0, two)
        weights.append((now, one, two, 0.5 * sizes[step]))
    lane = lax.broadcasted_iota(jnp.int32, (COLS, 128), 1)
    base = PARTS * ROWS

    def at(step, plane, line):
        if step < 0:
            return late_ref[place_of(step + 2, plane, line)]
        return field_ref[place_of(step, plane, line)]

    for step in range(STEPS):
        now, one, two, kappa = weights[step]
        for plane in range(PLANES):
            for line in range(LINES):
                value = at(step, plane, line)
                side = step * LINES + line
                beside = low_ref[side] if plane == 0 else at(step, plane - 1, line)
                beside += high_ref[side] if plane == PLANES - 1 else at(step, plane + 1, line)
                if line > 0:
                    beside += at(step, plane, line - 1)
                if line < LINES - 1:
                    beside += at(step, plane, line + 1)
                beside += jnp.where(lane < 127, pltpu.roll(value, 127, 1), 0.0)
                beside += jnp.where(lane > 0, pltpu.roll(value, 1, 1), 0.0)
                result = (
                    now * value
                    - one * at(step - 1, plane, line)
                    + two * at(step - 2, plane, line)
                    + kappa * (6.0 * value - beside)
                )
                place = place_of(step, plane, line)
                for part, piece in enumerate(split(result)):
                    parts_ref[
                        base + part * COLS : base + (part + 1) * COLS, place * 128 : (place + 1) * 128
                    ] = piece
    own_parts = parts_ref[base:]
    products = lax.dot_general(own_parts, parts_ref[...], NT, preferred_element_type=F32)
    proj = part_products(products, COLS, 0, ROWS)
    gram = part_products(products, COLS, base, COLS)
    packed = jnp.concatenate([proj[:8], proj[8:]], axis=1)
    pieces = []
    for half in range(2):
        lines = [gram[half * 8 + row : half * 8 + row + 1] for row in range(8)]
        pieces.append(jnp.concatenate(lines, axis=1))
    chip = keep_ref[...] + got_ref[...]
    last = jnp.concatenate(pieces + [chip[8:10]], axis=0)
    for copy in range(SLABS):
        copies_ref[copy, 0] = packed[:4]
        copies_ref[copy, 1] = packed[4:]
        copies_ref[copy, 2] = chip[0:4]
        copies_ref[copy, 3] = chip[4:8]
        copies_ref[copy, 4] = last


def image_products(sizes, field, low, high, late, keep, got, parts):
    return pl.pallas_call(
        image_kernel,
        out_shape=(
            jax.ShapeDtypeStruct((PARTS * FULL, CELLS), BF16),
            jax.ShapeDtypeStruct((SLABS, 5, 4, 128), F32),
        ),
        in_specs=[VMEM] * 8,
        out_specs=(VMEM, VMEM),
        input_output_aliases={7: 0},
        compiler_params=params(20),
        name="image_products",
    )(sizes, field, low, high, late, keep, got, parts)


def finish_kernel(sums_ref, parts_ref, hess_ref, triangle_ref, next_hbm, next_ref, sems):
    cores = []
    for core in range(2):
        total = sums_ref[core]
        for piece in range(core + 2, GROUPS, 2):
            total = total + sums_ref[piece]
        cores.append(total * (1.0 / TOTAL))
    sums = cores[0] + cores[1]
    proj = jnp.concatenate(
        [sums[0, :, :ROWS], sums[1, :, :ROWS], sums[0, :, ROWS:], sums[1, :, ROWS:]], axis=0
    )
    image_gram = jnp.concatenate(
        [
            sums[4, half : half + 1, line * COLS : (line + 1) * COLS]
            for half in range(2)
            for line in range(8)
        ],
        axis=0,
    )
    packed = jnp.concatenate([cores[0][2], cores[0][3], cores[1][2], cores[1][3]], axis=0)
    rest = jnp.concatenate(
        [cores[core][4, 2:4, 32 * i : 32 * i + 32] for core in range(2) for i in range(4)], axis=0
    )
    kept = [packed[:, :64], packed[:, 64:112], rest, packed[:, 112:]]
    upper = []
    for block in range(BLOCKS):
        pieces = [0.5 * kept[block][:, :COLS]]
        if block:
            pieces.insert(0, jnp.zeros((COLS, block * COLS), F32))
        if block < BLOCKS - 1:
            pieces.append(kept[block][:, COLS:])
        upper.append(jnp.concatenate(pieces, axis=1))
    half = jnp.concatenate(upper, axis=0)
    carried = lax.dot_general(proj, half, NN, precision=HIGHEST, preferred_element_type=F32) - proj
    cross = lax.dot_general(carried, proj, NT, precision=HIGHEST, preferred_element_type=F32)
    cross_t = lax.dot_general(proj, carried, NT, precision=HIGHEST, preferred_element_type=F32)
    gram = image_gram + (cross + cross_t)
    row = lax.broadcasted_iota(jnp.int32, (COLS, COLS), 0)
    col = lax.broadcasted_iota(jnp.int32, (COLS, COLS), 1)
    eye = jnp.where(row == col, 1.0, 0.0).astype(F32)
    work = jnp.concatenate(
        [gram, -proj, eye, jnp.zeros((COLS, 128 - FULL - COLS), F32)], axis=1
    )
    wide_row = lax.broadcasted_iota(jnp.int32, (COLS, 128), 0)
    scale = jnp.zeros((COLS, 128), F32)
    for step in range(COLS):
        column = jnp.broadcast_to(work[:, step : step + 1], (COLS, 128))
        pivot = jnp.broadcast_to(column[step : step + 1], (COLS, 128))
        pivot_row = jnp.broadcast_to(work[step : step + 1], (COLS, 128))
        work = work - jnp.where(wide_row > step, column / pivot, 0.0) * pivot_row
        scale = jnp.where(wide_row == step, lax.rsqrt(pivot), scale)
    work = work * scale
    hess_ref[...] = proj.T
    triangle_ref[...] = jnp.where(row <= col, work[:, :COLS], 0.0)
    factors = split(work[:, COLS : COLS + FULL])
    stacked = []
    for part in range(PARTS):
        pieces = []
        for piece in (factors[part][:, :ROWS], factors[part][:, ROWS:]):
            for other in range(PARTS):
                pieces.append(piece if other < PARTS - part else jnp.zeros_like(piece))
        stacked.append(jnp.concatenate(pieces, axis=1))
    factor = jnp.concatenate(stacked, axis=0)
    copies = []
    for tile in range(PLACES // 8):
        lanes = slice(tile * 1024, (tile + 1) * 1024)
        product = lax.dot_general(factor, parts_ref[:, lanes], NN, preferred_element_type=F32)
        value = product[:COLS] + (product[COLS : 2 * COLS] + product[2 * COLS :])
        for line in range(8):
            place = tile * 8 + line
            next_ref[place] = value[:, line * 128 : (line + 1) * 128]
            copies.append(
                pltpu.make_async_copy(next_ref.at[place], next_hbm.at[:, place, 0], sems.at[place])
            )
            copies[-1].start()
    for copy in copies:
        copy.wait()


def finish(sums, parts):
    return pl.pallas_call(
        finish_kernel,
        out_shape=(
            jax.ShapeDtypeStruct((ROWS, COLS), F32),
            jax.ShapeDtypeStruct((COLS, COLS), F32),
            jax.ShapeDtypeStruct((COLS, PLACES, 1, 128), F32),
        ),
        in_specs=[VMEM, VMEM],
        out_specs=(VMEM, VMEM, HBM),
        scratch_shapes=[
            pltpu.VMEM((PLACES, COLS, 128), F32),
            pltpu.SemaphoreType.DMA((PLACES,)),
        ],
        compiler_params=params(20),
        name="finish",
    )(sums, parts)


def exchanged(copies, axes):
    return lax.all_to_all(copies, axes, 0, 0)


def per_device(basis, num, den):
    slabs = size_of(SPACE)
    groups = size_of(TM)
    above = [(i, i + 1) for i in range(slabs - 1)]
    below = [(i + 1, i) for i in range(slabs - 1)]
    later = [(i, i + 1) for i in range(groups - 1)]
    flat = basis.reshape(ROWS, PLACES, 1, 128)
    up, down = faces(flat)
    low = lax.ppermute(up, SPACE, above)
    high = lax.ppermute(down, SPACE, below)
    late, sizes = ending(num, den, flat, up)
    late = lax.ppermute(late, TM, later)
    parts, field, keep, give = basis_products(flat)
    got = lax.ppermute(give, "core", [(0, 1), (1, 0)])
    parts, copies = image_products(sizes, field, low, high, late, keep, got, parts)
    sums = exchanged(copies, SPACE).sum(0)
    sums = exchanged(jnp.broadcast_to(sums, (groups,) + sums.shape), TM)
    hess, triangle, following = finish(sums, parts)
    return (
        hess.reshape(BLOCKS, COLS, COLS),
        triangle,
        following.reshape(COLS, STEPS, PLANES, LINES, 128),
    )


def solution(mesh):
    fine = Mesh(mesh.devices.reshape(8, 2, 4, 8), ("y", "core", "x", "z"))
    placed = (P(None, None, TM, SPACE, None, None), P(TM), P(TM))
    return jax.shard_map(
        per_device,
        mesh=fine,
        in_specs=placed,
        out_specs=(P(), P(), P(None, TM, SPACE, None, None)),
        check_vma=False,
    )
```

time: 79.8 us -> 76.9 us (0.964)
  local copies, waits for them, and re-layouts: 7.97 us -> 3.99 us
  Pallas kernels: 13 us -> 14.1 us
  waiting for transfers between devices: 0.01 us -> 0.81 us
    all_to_all x1 -> x0, starting transfers between devices: 6.33 us -> none  [exchanged(): return lax.all_to_all(copies, axes, 0, 0)]
    ppermute x1 -> x2, starting transfers between devices: 4.59 us -> 10 us  [the longest x1 5.42 us: per_device(): got = lax.ppermute(give, 'core', [(0, 1), (1, 0)])]
    unnamed x8 -> x4, local copies, waits for them, and re-layouts: 7.95 us -> 3.97 us
    pallas_call x1, Pallas kernels: 3.35 us -> 1.67 us  [image_products(): pl.pallas_call(image_kernel, out_shape=(jax.ShapeDtypeStruct((PARTS * FUL...]
    pallas_call x2, Pallas kernels: 1.2 us -> 2.88 us  [the longest x1 1.65 us: faces(): pl.pallas_call(faces_kernel, out_shape=(face, face), in_specs=[HBM], out_...]
    pallas_call x1, Pallas kernels: 3.85 us -> 4.89 us  [finish(): pl.pallas_call(finish_kernel, out_shape=(jax.ShapeDtypeStruct((ROWS, COLS...]
    ppermute x1 -> x2, waiting for transfers between devices: 0.01 us -> 0.81 us  [the longest x1 0.81 us: per_device(): got = lax.ppermute(give, 'core', [(0, 1), (1, 0)])]
  transfers between devices with their start and end apart: 4 -> 4, of which waited for: 0 -> 1; matrix products, arithmetic and copies ran while one was open for 0% -> 0% of each run, Pallas kernels for 10% -> 6%
where the time goes in v4:
time: 76.9 us; the launch traced here: 76.4 us
  blocking collectives  40.8 us (53%)
  starting transfers between devices  15.9 us (21%)
  Pallas kernels  14.1 us (18%)
  local copies, waits for them, and re-layouts  3.99 us (5%)
  waiting for transfers between devices  0.81 us (1%)
    all_to_all x2, blocking collectives, exchanged(): return lax.all_to_all(copies, axes, 0, 0)  40.8 us
    ppermute x1, starting transfers between devices, per_device(): got = lax.ppermute(give, 'core', [(0, 1), (1, 0)])  5.42 us
    pallas_call x1, Pallas kernels, finish(): pl.pallas_call(finish_kernel, out_shape=(jax.ShapeDtypeStruct((ROWS, COLS...  4.89 us
    ppermute x1, starting transfers between devices, per_device(): low = lax.ppermute(up, SPACE, above)  4.64 us
    pallas_call x1, Pallas kernels, basis_products(): pl.pallas_call(basis_kernel, out_shape=(jax.ShapeDtypeStruct((PARTS * FUL...  4.64 us
    ppermute x1, starting transfers between devices, per_device(): late = lax.ppermute(late, TM, later)  4.59 us
    unnamed x4, local copies, waits for them, and re-layouts  3.97 us
    pallas_call x1, Pallas kernels, image_products(): pl.pallas_call(image_kernel, out_shape=(jax.ShapeDtypeStruct((PARTS * FUL...  1.67 us
  transfers between devices with their start and end apart: 4, of which 1 were waited for; matrix products, arithmetic and copies ran while one was open for 0% of the time, Pallas kernels for 6%

profile of v4, /device:TPU:1, one launch (start us, length us, event | category | flops | bytes accessed | tf_op | source)
XLA Modules:
  0.0 76.4 jit_solution(7775151697288388654)
XLA Ops:
  0.6 1.6 %faces.1 = (f32[32,16,128]{2,1,0:T(8,128)S(1)}, f32[32,16,128]{2,1,0:T(8,128)S(1)}) custom-call(f32[64,64,1,128]{3,2,1,0:T(1,128)} %bitcast.3), custom_call_target="tpu_custom_call" | custom-call | tf_op jit(solution)/shard_map/faces/pallas_call | solution.py:80
  2.3 1.2 %ending.1 = (f32[33,16,128]{2,1,0:T(8,128)S(1)}, f32[4,16,128]{2,1,0:T(8,128)S(1)}) custom-call(s32[4]{0:T(128)} %num_hbm.1, s32[4]{0:T(128)} %den_hbm.1, f32[64,64,1,128]{3,2,1,0:T(1,128)} %bitcast.4, f32[32,16,128]{2,1,0:T(8,128)S(1)} %get-tuple-element.16.after_ref), custom_call_target="tpu_custom_call" | custom-call | tf_op jit(solution)/shard_map/ending/pallas_call | solution.py:122
  3.5 4.6 %collective-permute-start.2 = (f32[33,16,128]{2,1,0:T(8,128)S(1)}, f32[33,16,128]{2,1,0:T(8,128)S(1)}, u32[]{:S(2)}, u32[]{:S(2)}) collective-permute-start(f32[33,16,128]{2,1,0:T(8,128)S(1)} %get-tuple-element.20), channel_id=1, source_target_pairs={{0,32},{32,64},{64,96},{96,128},{128,160},{160,192},{192,224},{224... | collective-permute-start | bytes 811016 | tf_op jit(solution)/shard_map/ppermute | solution.py:410
  8.1 1.3 %collective-permute-start.1 = (f32[32,16,128]{2,1,0:T(8,128)S(1)}, f32[32,16,128]{2,1,0:T(8,128)S(1)}, u32[]{:S(2)}, u32[]{:S(2)}) collective-permute-start(f32[32,16,128]{2,1,0:T(8,128)S(1)} %get-tuple-element.19), channel_id=1, source_target_pairs={{1,0},{2,1},{3,2},{4,3},{5,4},{6,5},{7,6},{8,7},{9,8},{10,9},{11,1... | collective-permute-start | bytes 786440 | tf_op jit(solution)/shard_map/ppermute | solution.py:408
  9.4 4.6 %collective-permute-start = (f32[32,16,128]{2,1,0:T(8,128)S(1)}, f32[32,16,128]{2,1,0:T(8,128)S(1)}, u32[]{:S(2)}, u32[]{:S(2)}) collective-permute-start(f32[32,16,128]{2,1,0:T(8,128)S(1)} %get-tuple-element.16.after_ref), channel_id=1, source_target_pairs={{0,1},{1,2},{2,3},{3,4},{4,5},{5,6},{6,7},{7,8},{8,9},{9,10},{10,1... | collective-permute-start | bytes 786440 | tf_op jit(solution)/shard_map/ppermute | solution.py:407
  14.1 4.6 %basis_products.1 = (bf16[240,8192]{1,0:T(8,128)(2,1)S(1)}, f32[64,16,128]{2,1,0:T(8,128)S(1)}, f32[16,128]{1,0:T(8,128)S(1)}, f32[16,128]{1,0:T(8,128)S(1)}) custom-call(f32[64,64,1,128]{3,2,1,0:T(1,128)} %bitcast.5), custom_call_target="tpu_custom_call" | custom-call | tf_op jit(solution)/shard_map/basis_products/pallas_call | solution.py:189
  18.7 5.4 %collective-permute-start.3 = (f32[16,128]{1,0:T(8,128)S(1)}, f32[16,128]{1,0:T(8,128)S(1)}, u32[]{:S(2)}, u32[]{:S(2)}) collective-permute-start(f32[16,128]{1,0:T(8,128)S(1)} %get-tuple-element.22), channel_id=1, source_target_pairs={{0,32},{32,0},{1,33},{33,1},{2,34},{34,2},{3,35},{35,3},{4,36},{36... | collective-permute-start | bytes 24584 | tf_op jit(solution)/shard_map/ppermute | solution.py:412
  24.2 0.8 %collective-permute-done.3.got_ref = f32[16,128]{1,0:T(8,128)S(1)} collective-permute-done((f32[16,128]{1,0:T(8,128)S(1)}, f32[16,128]{1,0:T(8,128)S(1)}, u32[]{:S(2)}, u32[]{:S(2)}) %collective-permute-start.3) | collective-permute-done | bytes 8224 | tf_op jit(solution)/shard_map/ppermute | solution.py:412
  25.0 0.0 collective-permute-done.1.high_ref
  25.0 0.0 collective-permute-done.low_ref
  25.0 0.0 collective-permute-done.2.late_ref
  25.0 1.7 %image_products.1 = (bf16[240,8192]{1,0:T(8,128)(2,1)S(1)}, f32[32,5,4,128]{3,2,1,0:T(4,128)S(1)}) custom-call(f32[4,16,128]{2,1,0:T(8,128)S(1)} %get-tuple-element.17.sizes_ref, f32[64,16,128]{2,1,0:T(8,128)S(1)} %get-tuple-element.18.field_ref, f32[32,16,128]{2,1,0:T(8,128)S(1)} %collective-permute-done.low_ref, ...), custom_call_target="tpu_custom_call", output_to_operand_aliasing={{0}: (7, {})} | custom-call | tf_op jit(solution)/shard_map/image_products/pallas_call | solution.py:283
  26.6 0.0 copy-start
  26.7 1.9 %copy-done = bf16[240,8192]{1,0:T(8,128)(2,1)} copy-done((bf16[240,8192]{1,0:T(8,128)(2,1)}, bf16[240,8192]{1,0:T(8,128)(2,1)S(1)}, u32[]{:S(2)}) %copy-start) | copy-done | bytes 3932184
  28.5 21.7 %all_to_all.10 = f32[32,5,4,128]{3,2,1,0:T(4,128)S(1)} all-to-all(f32[32,5,4,128]{3,2,1,0:T(4,128)S(1)} %get-tuple-element.24), channel_id=1, replica_groups=mesh['y'=8,'core'=2,'x'=4,'z'=8] {'x','z'}, dimensions={0} | all-to-all | bytes 655360 | tf_op jit(solution)/shard_map/all_to_all | solution.py:396
  50.2 0.1 reduce_sum.9
  50.3 19.1 %all_to_all.11.sums_ref = f32[16,5,4,128]{3,2,1,0:T(4,128)S(1)} all-to-all(f32[16,5,4,128]{3,2,1,0:T(4,128)S(1)} %broadcast_in_dim.3), channel_id=1, replica_groups=mesh['y'=8,'core'=2,'x'=4,'z'=8] {'y','core'}, dimensions={0} | all-to-all | bytes 327680 | tf_op jit(solution)/shard_map/all_to_all | solution.py:396
  69.4 0.0 copy-start.1
  69.4 2.1 %copy-done.1 = bf16[240,8192]{1,0:T(8,128)(2,1)S(1)} copy-done((bf16[240,8192]{1,0:T(8,128)(2,1)S(1)}, bf16[240,8192]{1,0:T(8,128)(2,1)}, u32[]{:S(2)}) %copy-start.1) | copy-done | bytes 3932184
  71.5 4.9 %finish.1 = (f32[64,16]{1,0:T(8,128)}, f32[16,16]{1,0:T(8,128)}, f32[16,64,1,128]{3,2,1,0:T(1,128)}) custom-call(f32[16,5,4,128]{3,2,1,0:T(4,128)S(1)} %all_to_all.11.sums_ref, bf16[240,8192]{1,0:T(8,128)(2,1)S(1)} %copy-done.1), custom_call_target="tpu_custom_call" | custom-call | tf_op jit(solution)/shard_map/finish/pallas_call | solution.py:377
  (1 shorter events, 0.0 us)
Async XLA Ops:
  3.5 21.4 %collective-permute-start.2 = (f32[33,16,128]{2,1,0:T(8,128)S(1)}, f32[33,16,128]{2,1,0:T(8,128)S(1)}, u32[]{:S(2)}, u32[]{:S(2)}) collective-permute-start(f32[33,16,128]{2,1,0:T(8,128)S(1)} %get-tuple-element.20), channel_id=1, source_target_pairs={{0,32},{32,64},{64,96},{96,128},{128,160},{160,192},{192,224},{224... | collective-permute-start | bytes 811016 | tf_op jit(solution)/shard_map/ppermute | solution.py:410
  8.1 16.8 %collective-permute-start.1 = (f32[32,16,128]{2,1,0:T(8,128)S(1)}, f32[32,16,128]{2,1,0:T(8,128)S(1)}, u32[]{:S(2)}, u32[]{:S(2)}) collective-permute-start(f32[32,16,128]{2,1,0:T(8,128)S(1)} %get-tuple-element.19), channel_id=1, source_target_pairs={{1,0},{2,1},{3,2},{4,3},{5,4},{6,5},{7,6},{8,7},{9,8},{10,9},{11,1... | collective-permute-start | bytes 786440 | tf_op jit(solution)/shard_map/ppermute | solution.py:408
  9.4 15.5 %collective-permute-start = (f32[32,16,128]{2,1,0:T(8,128)S(1)}, f32[32,16,128]{2,1,0:T(8,128)S(1)}, u32[]{:S(2)}, u32[]{:S(2)}) collective-permute-start(f32[32,16,128]{2,1,0:T(8,128)S(1)} %get-tuple-element.16.after_ref), channel_id=1, source_target_pairs={{0,1},{1,2},{2,3},{3,4},{4,5},{5,6},{6,7},{7,8},{8,9},{9,10},{10,1... | collective-permute-start | bytes 786440 | tf_op jit(solution)/shard_map/ppermute | solution.py:407
  18.7 6.2 %collective-permute-start.3 = (f32[16,128]{1,0:T(8,128)S(1)}, f32[16,128]{1,0:T(8,128)S(1)}, u32[]{:S(2)}, u32[]{:S(2)}) collective-permute-start(f32[16,128]{1,0:T(8,128)S(1)} %get-tuple-element.22), channel_id=1, source_target_pairs={{0,32},{32,0},{1,33},{33,1},{2,34},{34,2},{3,35},{35,3},{4,36},{36... | collective-permute-start | bytes 24584 | tf_op jit(solution)/shard_map/ppermute | solution.py:412
  26.6 1.9 %copy-start = (bf16[240,8192]{1,0:T(8,128)(2,1)}, bf16[240,8192]{1,0:T(8,128)(2,1)S(1)}, u32[]{:S(2)}) copy-start(bf16[240,8192]{1,0:T(8,128)(2,1)S(1)} %get-tuple-element.25.parts_ref) | copy-start | bytes 11796484
  69.4 2.1 %copy-start.1 = (bf16[240,8192]{1,0:T(8,128)(2,1)S(1)}, bf16[240,8192]{1,0:T(8,128)(2,1)}, u32[]{:S(2)}) copy-start(bf16[240,8192]{1,0:T(8,128)(2,1)} %copy-done) | copy-start | bytes 11796484

commit v5 on v4

--- a/solution.py
+++ b/solution.py
@@ -20,7 +20,7 @@
 CELLS = PLACES * 128
 TOTAL = 64 * 64 * 8 * 128
 PARTS = 3
-CHUNKS = 4
+CHUNKS = 1
 HIGHEST = lax.Precision.HIGHEST
 F32 = jnp.float32
 BF16 = jnp.bfloat16
@@ -57,54 +57,22 @@
     return first, second, third
 
 
-def faces_kernel(basis_hbm, up_ref, down_ref, sems):
-    copies = []
-    columns = pl.ds(ROWS - COLS, COLS)
-    for step in range(STEPS):
-        for line in range(LINES):
-            for plane, target in ((PLANES - 1, up_ref), (0, down_ref)):
-                source = basis_hbm.at[columns, place_of(step, plane, line), 0]
-                copies.append(
-                    pltpu.make_async_copy(
-                        source, target.at[step * LINES + line], sems.at[len(copies)]
-                    )
-                )
-    for copy in copies:
-        copy.start()
-    for copy in copies:
-        copy.wait()
-
-
-def faces(basis):
-    face = jax.ShapeDtypeStruct((STEPS * LINES, COLS, 128), F32)
-    return pl.pallas_call(
-        faces_kernel,
-        out_shape=(face, face),
-        in_specs=[HBM],
-        out_specs=(VMEM, VMEM),
-        scratch_shapes=[pltpu.SemaphoreType.DMA((2 * STEPS * LINES,))],
-        compiler_params=params(4),
-        name="faces",
-    )(in_hbm(basis))
-
-
-def ending_kernel(
-    num_hbm, den_hbm, basis_hbm, after_ref, late_ref, sizes_ref, num_ref, den_ref, sems
+def edges_kernel(
+    num_hbm, den_hbm, basis_hbm, up_ref, down_ref, late_ref, sizes_ref, num_ref, den_ref, sems
 ):
+    last = BLOCKS - 1
     counts = [
-        pltpu.make_async_copy(num_hbm, num_ref, sems.at[0]),
-        pltpu.make_async_copy(den_hbm, den_ref, sems.at[1]),
+        pltpu.make_async_copy(num_hbm, num_ref, sems.at[3]),
+        pltpu.make_async_copy(den_hbm, den_ref, sems.at[4]),
     ]
-    copies = []
-    columns = pl.ds(ROWS - COLS, COLS)
-    first = place_of(STEPS - 2, 0, 0)
-    for place in range(first, PLACES):
-        copies.append(
-            pltpu.make_async_copy(
-                basis_hbm.at[columns, place, 0], late_ref.at[place - first], sems.at[2 + len(copies)]
-            )
-        )
-    for copy in counts + copies:
+    copies = [
+        pltpu.make_async_copy(basis_hbm.at[last, :, :, PLANES - 1], up_ref, sems.at[0]),
+        pltpu.make_async_copy(basis_hbm.at[last, :, :, 0], down_ref, sems.at[1]),
+        pltpu.make_async_copy(
+            basis_hbm.at[last, :, pl.ds(STEPS - 2, 2)], late_ref.at[pl.ds(0, COLS)], sems.at[2]
+        ),
+    ]
+    for copy in copies + counts:
         copy.start()
     for copy in counts:
         copy.wait()
@@ -112,29 +80,33 @@
         top = jnp.full((COLS, 128), num_ref[step]).astype(F32)
         bottom = jnp.full((COLS, 128), den_ref[step]).astype(F32)
         sizes_ref[step] = top / bottom
-    late_ref[PLACES - first] = sizes_ref[STEPS - 1]
+    for step in range(2):
+        for plane in range(PLANES):
+            late_ref[COLS, step, plane] = sizes_ref[STEPS - 1, :LINES]
     for copy in copies:
         copy.wait()
 
 
-def ending(num, den, basis, after):
-    kept = 2 * PLANES * LINES
+def edges(num, den, basis):
+    face = jax.ShapeDtypeStruct((COLS, STEPS, LINES, 128), F32)
     return pl.pallas_call(
-        ending_kernel,
+        edges_kernel,
         out_shape=(
-            jax.ShapeDtypeStruct((kept + 1, COLS, 128), F32),
+            face,
+            face,
+            jax.ShapeDtypeStruct((COLS + 1, 2, PLANES, LINES, 128), F32),
             jax.ShapeDtypeStruct((STEPS, COLS, 128), F32),
         ),
-        in_specs=[HBM, HBM, HBM, pl.BlockSpec(memory_space=pl.ANY)],
-        out_specs=(VMEM, VMEM),
+        in_specs=[HBM, HBM, HBM],
+        out_specs=(VMEM, VMEM, VMEM, VMEM),
         scratch_shapes=[
             pltpu.SMEM((STEPS,), jnp.int32),
             pltpu.SMEM((STEPS,), jnp.int32),
-            pltpu.SemaphoreType.DMA((2 + kept,)),
+            pltpu.SemaphoreType.DMA((5,)),
         ],
         compiler_params=params(4),
-        name="ending",
-    )(in_hbm(num), in_hbm(den), in_hbm(basis), after)
+        name="edges",
+    )(in_hbm(num), in_hbm(den), in_hbm(basis))
 
 
 def part_products(products, count, offset, width):
@@ -209,13 +181,15 @@
     sizes_ref, field_ref, low_ref, high_ref, late_ref, keep_ref, got_ref, parts_in_ref,
     parts_ref, copies_ref,
 ):
+    side_rows = 2 * PLANES * LINES
     sizes = [sizes_ref[step] for step in range(STEPS)]
     first = (lax.axis_index("y") == 0) & (lax.axis_index("core") == 0)
     start = jnp.full((COLS, 128), first.astype(jnp.int32)) == 1
     weights = []
     for step in range(STEPS):
         if step == 0:
-            before = jnp.where(start, sizes[0], late_ref[2 * PLANES * LINES])
+            before = late_ref[pl.ds(COLS * side_rows, LINES), :]
+            before = jnp.where(start, sizes[0], jnp.concatenate([before, before], axis=0))
         else:
             before = sizes[step - 1]
         ratio = sizes[step] / before
@@ -230,9 +204,14 @@
     lane = lax.broadcasted_iota(jnp.int32, (COLS, 128), 1)
     base = PARTS * ROWS
 
+    def turned(ref, place):
+        return ref[pl.ds(place, COLS, stride=side_rows), :]
+
+    past = [turned(late_ref, place) for place in range(side_rows)]
+
     def at(step, plane, line):
         if step < 0:
-            return late_ref[place_of(step + 2, plane, line)]
+            return past[place_of(step + 2, plane, line)]
         return field_ref[place_of(step, plane, line)]
 
     for step in range(STEPS):
@@ -241,8 +220,8 @@
             for line in range(LINES):
                 value = at(step, plane, line)
                 side = step * LINES + line
-                beside = low_ref[side] if plane == 0 else at(step, plane - 1, line)
-                beside += high_ref[side] if plane == PLANES - 1 else at(step, plane + 1, line)
+                beside = turned(low_ref, side) if plane == 0 else at(step, plane - 1, line)
+                beside += turned(high_ref, side) if plane == PLANES - 1 else at(step, plane + 1, line)
                 if line > 0:
                     beside += at(step, plane, line - 1)
                 if line < LINES - 1:
@@ -294,7 +273,26 @@
     )(sizes, field, low, high, late, keep, got, parts)
 
 
-def finish_kernel(sums_ref, parts_ref, hess_ref, triangle_ref, next_hbm, next_ref, sems):
+def regroup_kernel(sums_ref, copies_ref):
+    total = sums_ref[0]
+    for piece in range(1, SLABS):
+        total = total + sums_ref[piece]
+    for copy in range(GROUPS):
+        copies_ref[copy] = total
+
+
+def regroup(sums):
+    return pl.pallas_call(
+        regroup_kernel,
+        out_shape=jax.ShapeDtypeStruct((GROUPS, 5, 4, 128), F32),
+        in_specs=[VMEM],
+        out_specs=VMEM,
+        compiler_params=params(4),
+        name="regroup",
+    )(sums)
+
+
+def finish_kernel(sums_ref, parts_ref, hess_ref, triangle_ref, next_ref):
     cores = []
     for core in range(2):
         total = sums_ref[core]
@@ -338,12 +336,14 @@
         [gram, -proj, eye, jnp.zeros((COLS, 128 - FULL - COLS), F32)], axis=1
     )
     wide_row = lax.broadcasted_iota(jnp.int32, (COLS, 128), 0)
+    columns = [jnp.broadcast_to(gram[:, k : k + 1], (COLS, 128)) for k in range(COLS)]
     scale = jnp.zeros((COLS, 128), F32)
     for step in range(COLS):
-        column = jnp.broadcast_to(work[:, step : step + 1], (COLS, 128))
-        pivot = jnp.broadcast_to(column[step : step + 1], (COLS, 128))
-        pivot_row = jnp.broadcast_to(work[step : step + 1], (COLS, 128))
-        work = work - jnp.where(wide_row > step, column / pivot, 0.0) * pivot_row
+        pivot = jnp.broadcast_to(columns[step][step : step + 1], (COLS, 128))
+        factor = jnp.where(wide_row > step, columns[step] * (1.0 / pivot), 0.0)
+        for k in range(step + 1, COLS):
+            columns[k] = columns[k] - factor * columns[k][step : step + 1]
+        work = work - factor * work[step : step + 1]
         scale = jnp.where(wide_row == step, lax.rsqrt(pivot), scale)
     work = work * scale
     hess_ref[...] = proj.T
@@ -357,20 +357,14 @@
                 pieces.append(piece if other < PARTS - part else jnp.zeros_like(piece))
         stacked.append(jnp.concatenate(pieces, axis=1))
     factor = jnp.concatenate(stacked, axis=0)
-    copies = []
     for tile in range(PLACES // 8):
         lanes = slice(tile * 1024, (tile + 1) * 1024)
         product = lax.dot_general(factor, parts_ref[:, lanes], NN, preferred_element_type=F32)
         value = product[:COLS] + (product[COLS : 2 * COLS] + product[2 * COLS :])
         for line in range(8):
-            place = tile * 8 + line
-            next_ref[place] = value[:, line * 128 : (line + 1) * 128]
-            copies.append(
-                pltpu.make_async_copy(next_ref.at[place], next_hbm.at[:, place, 0], sems.at[place])
-            )
-            copies[-1].start()
-    for copy in copies:
-        copy.wait()
+            next_ref[pl.ds(tile * 8 + line, COLS, stride=PLACES), :] = value[
+                :, line * 128 : (line + 1) * 128
+            ]
 
 
 def finish(sums, parts):
@@ -379,14 +373,10 @@
         out_shape=(
             jax.ShapeDtypeStruct((ROWS, COLS), F32),
             jax.ShapeDtypeStruct((COLS, COLS), F32),
-            jax.ShapeDtypeStruct((COLS, PLACES, 1, 128), F32),
+            jax.ShapeDtypeStruct((COLS * PLACES, 128), F32),
         ),
         in_specs=[VMEM, VMEM],
-        out_specs=(VMEM, VMEM, HBM),
-        scratch_shapes=[
-            pltpu.VMEM((PLACES, COLS, 128), F32),
-            pltpu.SemaphoreType.DMA((PLACES,)),
-        ],
+        out_specs=(VMEM, VMEM, VMEM),
         compiler_params=params(20),
         name="finish",
     )(sums, parts)
@@ -403,16 +393,14 @@
     below = [(i + 1, i) for i in range(slabs - 1)]
     later = [(i, i + 1) for i in range(groups - 1)]
     flat = basis.reshape(ROWS, PLACES, 1, 128)
-    up, down = faces(flat)
-    low = lax.ppermute(up, SPACE, above)
-    high = lax.ppermute(down, SPACE, below)
-    late, sizes = ending(num, den, flat, up)
-    late = lax.ppermute(late, TM, later)
+    up, down, late, sizes = edges(num, den, basis)
+    low = lax.ppermute(up, SPACE, above).reshape(-1, 128)
+    high = lax.ppermute(down, SPACE, below).reshape(-1, 128)
+    late = lax.ppermute(late, TM, later).reshape(-1, 128)
     parts, field, keep, give = basis_products(flat)
     got = lax.ppermute(give, "core", [(0, 1), (1, 0)])
     parts, copies = image_products(sizes, field, low, high, late, keep, got, parts)
-    sums = exchanged(copies, SPACE).sum(0)
-    sums = exchanged(jnp.broadcast_to(sums, (groups,) + sums.shape), TM)
+    sums = exchanged(regroup(exchanged(copies, SPACE)), TM)
     hess, triangle, following = finish(sums, parts)
     return (
         hess.reshape(BLOCKS, COLS, COLS),

time: 76.9 us -> 68.1 us (0.89)
  Pallas kernels: 14.1 us -> 8.96 us
  local copies, waits for them, and re-layouts: 3.99 us -> 0 us
  starting transfers between devices: 15.9 us -> 12.7 us
  blocking collectives: 40.8 us -> 42.7 us
  waiting for transfers between devices: 0.81 us -> 2.57 us
    unnamed x4 -> x0, local copies, waits for them, and re-layouts: 3.97 us -> none
    ppermute x1, starting transfers between devices: 5.42 us -> 2.79 us  [per_device(): got = lax.ppermute(give, 'core', [(0, 1), (1, 0)])]
    pallas_call x1, Pallas kernels: 4.89 us -> 2.38 us  [finish(): pl.pallas_call(finish_kernel, out_shape=(jax.ShapeDtypeStruct((ROWS, COLS...]
    all_to_all x2, blocking collectives: 40.8 us -> 42.7 us  [exchanged(): return lax.all_to_all(copies, axes, 0, 0)]
    ppermute x3, waiting for transfers between devices: 0.01 us -> 1.77 us  [the longest x1 1.76 us: per_device(): high = lax.ppermute(down, SPACE, below).reshape(-1, 128)]
    pallas_call x2, Pallas kernels: 2.88 us -> 1.21 us  [the longest x1 1.16 us: edges(): pl.pallas_call(edges_kernel, out_shape=(face, face, jax.ShapeDtypeStruct(...]
    pallas_call x1, Pallas kernels: 4.64 us -> 3.49 us  [basis_products(): pl.pallas_call(basis_kernel, out_shape=(jax.ShapeDtypeStruct((PARTS * FUL...]
  transfers between devices with their start and end apart: 4 -> 4, of which waited for: 1 -> 2; matrix products, arithmetic and copies ran while one was open for 0% -> 0% of each run, Pallas kernels for 6% -> 5%
where the time goes in v5:
time: 68.1 us; the launch traced here: 67.7 us
  blocking collectives  42.7 us (63%)
  starting transfers between devices  12.7 us (19%)
  Pallas kernels  8.96 us (13%)
  waiting for transfers between devices  2.57 us (4%)
  between operations  0.69 us (1%)
    all_to_all x2, blocking collectives, exchanged(): return lax.all_to_all(copies, axes, 0, 0)  42.7 us
    ppermute x1, starting transfers between devices, per_device(): late = lax.ppermute(late, TM, later).reshape(-1, 128)  4.59 us
    ppermute x1, starting transfers between devices, per_device(): low = lax.ppermute(up, SPACE, above).reshape(-1, 128)  4.01 us
    pallas_call x1, Pallas kernels, basis_products(): pl.pallas_call(basis_kernel, out_shape=(jax.ShapeDtypeStruct((PARTS * FUL...  3.49 us
    ppermute x1, starting transfers between devices, per_device(): got = lax.ppermute(give, 'core', [(0, 1), (1, 0)])  2.79 us
    pallas_call x1, Pallas kernels, finish(): pl.pallas_call(finish_kernel, out_shape=(jax.ShapeDtypeStruct((ROWS, COLS...  2.38 us
    pallas_call x1, Pallas kernels, image_products(): pl.pallas_call(image_kernel, out_shape=(jax.ShapeDtypeStruct((PARTS * FUL...  1.87 us
    ppermute x1, waiting for transfers between devices, per_device(): high = lax.ppermute(down, SPACE, below).reshape(-1, 128)  1.76 us
  transfers between devices with their start and end apart: 4, of which 2 were waited for; matrix products, arithmetic and copies ran while one was open for 0% of the time, Pallas kernels for 5%

profile of v5, /device:TPU:1, one launch (start us, length us, event | category | flops | bytes accessed | tf_op | source)
XLA Modules:
  0.0 67.7 jit_solution(12704367628280000509)
XLA Ops:
  0.6 1.2 %edges.1 = (f32[16,4,8,128]{3,2,1,0:T(8,128)S(1)}, f32[16,4,8,128]{3,2,1,0:T(8,128)S(1)}, f32[17,2,2,8,128]{4,3,2,1,0:T(8,128)S(1)}, f32[4,16,128]{2,1,0:T(8,128)S(1)}) custom-call(s32[4]{0:T(128)} %num_hbm.1, s32[4]{0:T(128)} %den_hbm.1, f32[4,16,4,2,8,128]{5,4,3,2,1,0:T(8,128)} %basis_hbm.1), custom_call_target="tpu_custom_call" | custom-call | tf_op jit(solution)/shard_map/edges/pallas_call | solution.py:92
  1.8 4.6 %collective-permute-start.2 = (f32[17,2,2,8,128]{4,3,2,1,0:T(8,128)S(1)}, f32[17,2,2,8,128]{4,3,2,1,0:T(8,128)S(1)}, u32[]{:S(2)}, u32[]{:S(2)}) collective-permute-start(f32[17,2,2,8,128]{4,3,2,1,0:T(8,128)S(1)} %get-tuple-element.20), channel_id=1, source_target_pairs={{0,32},{32,64},{64,96},{96,128},{128,160},{160,192},{192,224},{224... | collective-permute-start | bytes 835592 | tf_op jit(solution)/shard_map/ppermute | solution.py:399
  6.4 4.0 %collective-permute-start = (f32[16,4,8,128]{3,2,1,0:T(8,128)S(1)}, f32[16,4,8,128]{3,2,1,0:T(8,128)S(1)}, u32[]{:S(2)}, u32[]{:S(2)}) collective-permute-start(f32[16,4,8,128]{3,2,1,0:T(8,128)S(1)} %get-tuple-element.18), channel_id=1, source_target_pairs={{0,1},{1,2},{2,3},{3,4},{4,5},{5,6},{6,7},{7,8},{8,9},{9,10},{10,1... | collective-permute-start | bytes 786440 | tf_op jit(solution)/shard_map/ppermute | solution.py:397
  10.4 1.3 %collective-permute-start.1 = (f32[16,4,8,128]{3,2,1,0:T(8,128)S(1)}, f32[16,4,8,128]{3,2,1,0:T(8,128)S(1)}, u32[]{:S(2)}, u32[]{:S(2)}) collective-permute-start(f32[16,4,8,128]{3,2,1,0:T(8,128)S(1)} %get-tuple-element.19), channel_id=1, source_target_pairs={{1,0},{2,1},{3,2},{4,3},{5,4},{6,5},{7,6},{8,7},{9,8},{10,9},{11,1... | collective-permute-start | bytes 786440 | tf_op jit(solution)/shard_map/ppermute | solution.py:398
  11.7 3.5 %basis_products.1 = (bf16[240,8192]{1,0:T(8,128)(2,1)S(1)}, f32[64,16,128]{2,1,0:T(8,128)S(1)}, f32[16,128]{1,0:T(8,128)S(1)}, f32[16,128]{1,0:T(8,128)S(1)}) custom-call(f32[64,64,1,128]{3,2,1,0:T(1,128)} %bitcast.9), custom_call_target="tpu_custom_call" | custom-call | tf_op jit(solution)/shard_map/basis_products/pallas_call | solution.py:161
  15.2 2.8 %collective-permute-start.3 = (f32[16,128]{1,0:T(8,128)S(1)}, f32[16,128]{1,0:T(8,128)S(1)}, u32[]{:S(2)}, u32[]{:S(2)}) collective-permute-start(f32[16,128]{1,0:T(8,128)S(1)} %get-tuple-element.22), channel_id=1, source_target_pairs={{0,32},{32,0},{1,33},{33,1},{2,34},{34,2},{3,35},{35,3},{4,36},{36... | collective-permute-start | bytes 24584 | tf_op jit(solution)/shard_map/ppermute | solution.py:401
  18.0 0.8 %collective-permute-done.3.got_ref = f32[16,128]{1,0:T(8,128)S(1)} collective-permute-done((f32[16,128]{1,0:T(8,128)S(1)}, f32[16,128]{1,0:T(8,128)S(1)}, u32[]{:S(2)}, u32[]{:S(2)}) %collective-permute-start.3) | collective-permute-done | bytes 8224 | tf_op jit(solution)/shard_map/ppermute | solution.py:401
  18.8 0.0 collective-permute-done
  18.8 1.8 %collective-permute-done.1 = f32[16,4,8,128]{3,2,1,0:T(8,128)S(1)} collective-permute-done((f32[16,4,8,128]{3,2,1,0:T(8,128)S(1)}, f32[16,4,8,128]{3,2,1,0:T(8,128)S(1)}, u32[]{:S(2)}, u32[]{:S(2)}) %collective-permute-start.1) | collective-permute-done | bytes 262176 | tf_op jit(solution)/shard_map/ppermute | solution.py:398
  20.6 0.0 collective-permute-done.2
  20.6 1.9 %image_products.1 = (bf16[240,8192]{1,0:T(8,128)(2,1)S(1)}, f32[32,5,4,128]{3,2,1,0:T(4,128)S(1)}) custom-call(f32[4,16,128]{2,1,0:T(8,128)S(1)} %get-tuple-element.16.sizes_ref, f32[64,16,128]{2,1,0:T(8,128)S(1)} %get-tuple-element.17.field_ref, f32[512,128]{1,0:T(8,128)S(1)} %bitcast.7, f32[512,128]{1,0:T(8,128)S(1)} %bitcast.8, ...), custom_call_target="tpu_custom_call", output_to_operand_aliasing={{0}: (7, {})} | custom-call | tf_op jit(solution)/shard_map/image_products/pallas_call | solution.py:262
  22.5 22.4 %all_to_all.10.sums_ref = f32[32,5,4,128]{3,2,1,0:T(4,128)S(1)} all-to-all(f32[32,5,4,128]{3,2,1,0:T(4,128)S(1)} %get-tuple-element.24), channel_id=1, replica_groups=mesh['y'=8,'core'=2,'x'=4,'z'=8] {'x','z'}, dimensions={0} | all-to-all | bytes 655360 | tf_op jit(solution)/shard_map/all_to_all | solution.py:386
  44.9 0.1 regroup.1
  44.9 20.3 %all_to_all.11.sums_ref = f32[16,5,4,128]{3,2,1,0:T(4,128)S(1)} all-to-all(f32[16,5,4,128]{3,2,1,0:T(4,128)S(1)} %regroup.1), channel_id=1, replica_groups=mesh['y'=8,'core'=2,'x'=4,'z'=8] {'y','core'}, dimensions={0} | all-to-all | bytes 327680 | tf_op jit(solution)/shard_map/all_to_all | solution.py:386
  65.3 2.4 %finish.1 = (f32[64,16]{1,0:T(8,128)}, f32[16,16]{1,0:T(8,128)}, f32[1024,128]{1,0:T(8,128)}) custom-call(f32[16,5,4,128]{3,2,1,0:T(4,128)S(1)} %all_to_all.11.sums_ref, bf16[240,8192]{1,0:T(8,128)(2,1)S(1)} %get-tuple-element.25.parts_ref), custom_call_target="tpu_custom_call" | custom-call | tf_op jit(solution)/shard_map/finish/pallas_call | solution.py:371
Async XLA Ops:
  1.8 18.8 %collective-permute-start.2 = (f32[17,2,2,8,128]{4,3,2,1,0:T(8,128)S(1)}, f32[17,2,2,8,128]{4,3,2,1,0:T(8,128)S(1)}, u32[]{:S(2)}, u32[]{:S(2)}) collective-permute-start(f32[17,2,2,8,128]{4,3,2,1,0:T(8,128)S(1)} %get-tuple-element.20), channel_id=1, source_target_pairs={{0,32},{32,64},{64,96},{96,128},{128,160},{160,192},{192,224},{224... | collective-permute-start | bytes 835592 | tf_op jit(solution)/shard_map/ppermute | solution.py:399
  6.4 12.4 %collective-permute-start = (f32[16,4,8,128]{3,2,1,0:T(8,128)S(1)}, f32[16,4,8,128]{3,2,1,0:T(8,128)S(1)}, u32[]{:S(2)}, u32[]{:S(2)}) collective-permute-start(f32[16,4,8,128]{3,2,1,0:T(8,128)S(1)} %get-tuple-element.18), channel_id=1, source_target_pairs={{0,1},{1,2},{2,3},{3,4},{4,5},{5,6},{6,7},{7,8},{8,9},{9,10},{10,1... | collective-permute-start | bytes 786440 | tf_op jit(solution)/shard_map/ppermute | solution.py:397
  10.4 10.2 %collective-permute-start.1 = (f32[16,4,8,128]{3,2,1,0:T(8,128)S(1)}, f32[16,4,8,128]{3,2,1,0:T(8,128)S(1)}, u32[]{:S(2)}, u32[]{:S(2)}) collective-permute-start(f32[16,4,8,128]{3,2,1,0:T(8,128)S(1)} %get-tuple-element.19), channel_id=1, source_target_pairs={{1,0},{2,1},{3,2},{4,3},{5,4},{6,5},{7,6},{8,7},{9,8},{10,9},{11,1... | collective-permute-start | bytes 786440 | tf_op jit(solution)/shard_map/ppermute | solution.py:398
  15.2 3.6 %collective-permute-start.3 = (f32[16,128]{1,0:T(8,128)S(1)}, f32[16,128]{1,0:T(8,128)S(1)}, u32[]{:S(2)}, u32[]{:S(2)}) collective-permute-start(f32[16,128]{1,0:T(8,128)S(1)} %get-tuple-element.22), channel_id=1, source_target_pairs={{0,32},{32,0},{1,33},{33,1},{2,34},{34,2},{3,35},{35,3},{4,36},{36... | collective-permute-start | bytes 24584 | tf_op jit(solution)/shard_map/ppermute | solution.py:401

commit v6 on v5

--- a/solution.py
+++ b/solution.py
@@ -20,7 +20,6 @@
 CELLS = PLACES * 128
 TOTAL = 64 * 64 * 8 * 128
 PARTS = 3
-CHUNKS = 1
 HIGHEST = lax.Precision.HIGHEST
 F32 = jnp.float32
 BF16 = jnp.bfloat16
@@ -58,19 +57,20 @@
 
 
 def edges_kernel(
-    num_hbm, den_hbm, basis_hbm, up_ref, down_ref, late_ref, sizes_ref, num_ref, den_ref, sems
+    num_hbm, den_hbm, basis_hbm, up_ref, down_ref, one_ref, two_ref, sizes_ref, num_ref, den_ref, sems
 ):
     last = BLOCKS - 1
     counts = [
-        pltpu.make_async_copy(num_hbm, num_ref, sems.at[3]),
-        pltpu.make_async_copy(den_hbm, den_ref, sems.at[4]),
+        pltpu.make_async_copy(num_hbm, num_ref, sems.at[4]),
+        pltpu.make_async_copy(den_hbm, den_ref, sems.at[5]),
     ]
     copies = [
         pltpu.make_async_copy(basis_hbm.at[last, :, :, PLANES - 1], up_ref, sems.at[0]),
         pltpu.make_async_copy(basis_hbm.at[last, :, :, 0], down_ref, sems.at[1]),
         pltpu.make_async_copy(
-            basis_hbm.at[last, :, pl.ds(STEPS - 2, 2)], late_ref.at[pl.ds(0, COLS)], sems.at[2]
+            basis_hbm.at[last, :, STEPS - 1], one_ref.at[pl.ds(0, COLS)], sems.at[2]
         ),
+        pltpu.make_async_copy(basis_hbm.at[last, :, STEPS - 2], two_ref, sems.at[3]),
     ]
     for copy in copies + counts:
         copy.start()
@@ -80,9 +80,8 @@
         top = jnp.full((COLS, 128), num_ref[step]).astype(F32)
         bottom = jnp.full((COLS, 128), den_ref[step]).astype(F32)
         sizes_ref[step] = top / bottom
-    for step in range(2):
-        for plane in range(PLANES):
-            late_ref[COLS, step, plane] = sizes_ref[STEPS - 1, :LINES]
+    for plane in range(PLANES):
+        one_ref[COLS, plane] = sizes_ref[STEPS - 1, :LINES]
     for copy in copies:
         copy.wait()
 
@@ -94,15 +93,16 @@
         out_shape=(
             face,
             face,
-            jax.ShapeDtypeStruct((COLS + 1, 2, PLANES, LINES, 128), F32),
+            jax.ShapeDtypeStruct((COLS + 1, PLANES, LINES, 128), F32),
+            jax.ShapeDtypeStruct((COLS, PLANES, LINES, 128), F32),
             jax.ShapeDtypeStruct((STEPS, COLS, 128), F32),
         ),
         in_specs=[HBM, HBM, HBM],
-        out_specs=(VMEM, VMEM, VMEM, VMEM),
+        out_specs=(VMEM,) * 5,
         scratch_shapes=[
             pltpu.SMEM((STEPS,), jnp.int32),
             pltpu.SMEM((STEPS,), jnp.int32),
-            pltpu.SemaphoreType.DMA((5,)),
+            pltpu.SemaphoreType.DMA((6,)),
         ],
         compiler_params=params(4),
         name="edges",
@@ -127,20 +127,20 @@
     ]
     for copy in copies:
         copy.start()
-    products = None
-    per_chunk = PLACES // CHUNKS
-    for chunk in range(CHUNKS):
-        for place in range(chunk * per_chunk, (chunk + 1) * per_chunk):
-            copies[place].wait()
-            value = field_ref[place]
-            last_ref[place] = value[ROWS - COLS :]
-            for part, piece in enumerate(split(value)):
-                parts_ref[part * ROWS : (part + 1) * ROWS, place * 128 : (place + 1) * 128] = piece
-        lanes = slice(chunk * per_chunk * 128, (chunk + 1) * per_chunk * 128)
-        piece = parts_ref[: PARTS * ROWS, lanes]
-        product = lax.dot_general(piece, piece, NT, preferred_element_type=F32)
-        products = product if products is None else products + product
-    gram = part_products(products, ROWS, 0, ROWS)
+    for place in range(PLACES):
+        copies[place].wait()
+        value = field_ref[place]
+        last_ref[place] = value[ROWS - COLS :]
+        for part, piece in enumerate(split(value)):
+            parts_ref[part * ROWS : (part + 1) * ROWS, place * 128 : (place + 1) * 128] = piece
+    products = lax.dot_general(
+        parts_ref[: 2 * ROWS], parts_ref[: PARTS * ROWS], NT, preferred_element_type=F32
+    )
+
+    def pair(a, b):
+        return products[a * ROWS : (a + 1) * ROWS, b * ROWS : (b + 1) * ROWS]
+
+    gram = pair(0, 0) + ((pair(0, 1) + pair(1, 0)) + (pair(1, 1) + (pair(0, 2) + pair(0, 2).T)))
     rows = [gram[block * COLS : (block + 1) * COLS, block * COLS :] for block in range(BLOCKS)]
     packed = jnp.concatenate([rows[0], rows[1], rows[3]], axis=1)
     halves = []
@@ -178,17 +178,16 @@
 
 
 def image_kernel(
-    sizes_ref, field_ref, low_ref, high_ref, late_ref, keep_ref, got_ref, parts_in_ref,
+    sizes_ref, field_ref, low_ref, high_ref, one_ref, two_ref, keep_ref, got_ref, parts_in_ref,
     parts_ref, copies_ref,
 ):
-    side_rows = 2 * PLANES * LINES
     sizes = [sizes_ref[step] for step in range(STEPS)]
     first = (lax.axis_index("y") == 0) & (lax.axis_index("core") == 0)
     start = jnp.full((COLS, 128), first.astype(jnp.int32)) == 1
     weights = []
     for step in range(STEPS):
         if step == 0:
-            before = late_ref[pl.ds(COLS * side_rows, LINES), :]
+            before = one_ref[pl.ds(COLS * PLANES * LINES, LINES), :]
             before = jnp.where(start, sizes[0], jnp.concatenate([before, before], axis=0))
         else:
             before = sizes[step - 1]
@@ -205,13 +204,18 @@
     base = PARTS * ROWS
 
     def turned(ref, place):
-        return ref[pl.ds(place, COLS, stride=side_rows), :]
-
-    past = [turned(late_ref, place) for place in range(side_rows)]
+        return ref[pl.ds(place, COLS, stride=ref.shape[0] // COLS), :]
+
+    past = {}
+    for plane in range(PLANES):
+        for line in range(LINES):
+            place = plane * LINES + line
+            past[-1, plane, line] = one_ref[pl.ds(place, COLS, stride=PLANES * LINES), :]
+            past[-2, plane, line] = turned(two_ref, place)
 
     def at(step, plane, line):
         if step < 0:
-            return past[place_of(step + 2, plane, line)]
+            return past[step, plane, line]
         return field_ref[place_of(step, plane, line)]
 
     for step in range(STEPS):
@@ -258,19 +262,19 @@
         copies_ref[copy, 4] = last
 
 
-def image_products(sizes, field, low, high, late, keep, got, parts):
+def image_products(sizes, field, low, high, one, two, keep, got, parts):
     return pl.pallas_call(
         image_kernel,
         out_shape=(
             jax.ShapeDtypeStruct((PARTS * FULL, CELLS), BF16),
             jax.ShapeDtypeStruct((SLABS, 5, 4, 128), F32),
         ),
-        in_specs=[VMEM] * 8,
+        in_specs=[VMEM] * 9,
         out_specs=(VMEM, VMEM),
-        input_output_aliases={7: 0},
+        input_output_aliases={8: 0},
         compiler_params=params(20),
         name="image_products",
-    )(sizes, field, low, high, late, keep, got, parts)
+    )(sizes, field, low, high, one, two, keep, got, parts)
 
 
 def regroup_kernel(sums_ref, copies_ref):
@@ -393,13 +397,14 @@
     below = [(i + 1, i) for i in range(slabs - 1)]
     later = [(i, i + 1) for i in range(groups - 1)]
     flat = basis.reshape(ROWS, PLACES, 1, 128)
-    up, down, late, sizes = edges(num, den, basis)
+    up, down, one, two, sizes = edges(num, den, basis)
     low = lax.ppermute(up, SPACE, above).reshape(-1, 128)
     high = lax.ppermute(down, SPACE, below).reshape(-1, 128)
-    late = lax.ppermute(late, TM, later).reshape(-1, 128)
+    one = lax.ppermute(one, TM, later).reshape(-1, 128)
+    two = lax.ppermute(two, TM, later).reshape(-1, 128)
     parts, field, keep, give = basis_products(flat)
     got = lax.ppermute(give, "core", [(0, 1), (1, 0)])
-    parts, copies = image_products(sizes, field, low, high, late, keep, got, parts)
+    parts, copies = image_products(sizes, field, low, high, one, two, keep, got, parts)
     sums = exchanged(regroup(exchanged(copies, SPACE)), TM)
     hess, triangle, following = finish(sums, parts)
     return (

time: 68.1 us -> 69.7 us (1.023)
  starting transfers between devices: 12.7 us -> 14.5 us
  waiting for transfers between devices: 2.57 us -> 0.82 us
  blocking collectives: 42.7 us -> 44.1 us
    ppermute x1, waiting for transfers between devices: 1.76 us -> 0.01 us  [per_device(): high = lax.ppermute(down, SPACE, below).reshape(-1, 128)]
    ppermute x1 -> x2, starting transfers between devices: 4.59 us -> 5.97 us  [the longest x1 4.05 us: per_device(): one = lax.ppermute(one, TM, later).reshape(-1, 128)]
    all_to_all x2, blocking collectives: 42.7 us -> 44.1 us  [exchanged(): return lax.all_to_all(copies, axes, 0, 0)]
    ppermute x1, starting transfers between devices: 4.01 us -> 4.84 us  [per_device(): low = lax.ppermute(up, SPACE, above).reshape(-1, 128)]
  transfers between devices with their start and end apart: 4 -> 5, of which waited for: 2 -> 1; matrix products, arithmetic and copies ran while one was open for 0% -> 0% of each run, Pallas kernels for 5% -> 5%
where the time goes in v6:
time: 69.7 us; the launch traced here: 69.3 us
  blocking collectives  44.1 us (63%)
  starting transfers between devices  14.5 us (21%)
  Pallas kernels  9.16 us (13%)
  waiting for transfers between devices  0.82 us (1%)
  between operations  0.71 us (1%)
    all_to_all x2, blocking collectives, exchanged(): return lax.all_to_all(copies, axes, 0, 0)  44.1 us
    ppermute x1, starting transfers between devices, per_device(): low = lax.ppermute(up, SPACE, above).reshape(-1, 128)  4.84 us
    ppermute x1, starting transfers between devices, per_device(): one = lax.ppermute(one, TM, later).reshape(-1, 128)  4.05 us
    pallas_call x1, Pallas kernels, basis_products(): pl.pallas_call(basis_kernel, out_shape=(jax.ShapeDtypeStruct((PARTS * FUL...  3.74 us
    ppermute x1, starting transfers between devices, per_device(): got = lax.ppermute(give, 'core', [(0, 1), (1, 0)])  2.41 us
    pallas_call x1, Pallas kernels, finish(): pl.pallas_call(finish_kernel, out_shape=(jax.ShapeDtypeStruct((ROWS, COLS...  2.36 us
    ppermute x1, starting transfers between devices, per_device(): two = lax.ppermute(two, TM, later).reshape(-1, 128)  1.92 us
    pallas_call x1, Pallas kernels, image_products(): pl.pallas_call(image_kernel, out_shape=(jax.ShapeDtypeStruct((PARTS * FUL...  1.84 us
  transfers between devices with their start and end apart: 5, of which 1 were waited for; matrix products, arithmetic and copies ran while one was open for 0% of the time, Pallas kernels for 5%

profile of v6, /device:TPU:1, one launch (start us, length us, event | category | flops | bytes accessed | tf_op | source)
XLA Modules:
  0.0 69.3 jit_solution(9234434128367205947)
XLA Ops:
  0.6 1.2 %edges.1 = (f32[16,4,8,128]{3,2,1,0:T(8,128)S(1)}, f32[16,4,8,128]{3,2,1,0:T(8,128)S(1)}, f32[17,2,8,128]{3,2,1,0:T(8,128)S(1)}, f32[16,2,8,128]{3,2,1,0:T(8,128)S(1)}, f32[4,16,128]{2,1,0:T(8,128)S(1)}) custom-call(s32[4]{0:T(128)} %num_hbm.1, s32[4]{0:T(128)} %den_hbm.1, f32[4,16,4,2,8,128]{5,4,3,2,1,0:T(8,128)} %basis_hbm.1), custom_call_target="tpu_custom_call" | custom-call | tf_op jit(solution)/shard_map/edges/pallas_call | solution.py:91
  1.8 4.8 %collective-permute-start = (f32[16,4,8,128]{3,2,1,0:T(8,128)S(1)}, f32[16,4,8,128]{3,2,1,0:T(8,128)S(1)}, u32[]{:S(2)}, u32[]{:S(2)}) collective-permute-start(f32[16,4,8,128]{3,2,1,0:T(8,128)S(1)} %get-tuple-element.19), channel_id=1, source_target_pairs={{0,1},{1,2},{2,3},{3,4},{4,5},{5,6},{6,7},{7,8},{8,9},{9,10},{10,1... | collective-permute-start | bytes 786440 | tf_op jit(solution)/shard_map/ppermute | solution.py:401
  6.6 1.3 %collective-permute-start.1 = (f32[16,4,8,128]{3,2,1,0:T(8,128)S(1)}, f32[16,4,8,128]{3,2,1,0:T(8,128)S(1)}, u32[]{:S(2)}, u32[]{:S(2)}) collective-permute-start(f32[16,4,8,128]{3,2,1,0:T(8,128)S(1)} %get-tuple-element.20), channel_id=1, source_target_pairs={{1,0},{2,1},{3,2},{4,3},{5,4},{6,5},{7,6},{8,7},{9,8},{10,9},{11,1... | collective-permute-start | bytes 786440 | tf_op jit(solution)/shard_map/ppermute | solution.py:402
  7.9 4.0 %collective-permute-start.2 = (f32[17,2,8,128]{3,2,1,0:T(8,128)S(1)}, f32[17,2,8,128]{3,2,1,0:T(8,128)S(1)}, u32[]{:S(2)}, u32[]{:S(2)}) collective-permute-start(f32[17,2,8,128]{3,2,1,0:T(8,128)S(1)} %get-tuple-element.21), channel_id=1, source_target_pairs={{0,32},{32,64},{64,96},{96,128},{128,160},{160,192},{192,224},{224... | collective-permute-start | bytes 417800 | tf_op jit(solution)/shard_map/ppermute | solution.py:403
  12.0 1.9 %collective-permute-start.3 = (f32[16,2,8,128]{3,2,1,0:T(8,128)S(1)}, f32[16,2,8,128]{3,2,1,0:T(8,128)S(1)}, u32[]{:S(2)}, u32[]{:S(2)}) collective-permute-start(f32[16,2,8,128]{3,2,1,0:T(8,128)S(1)} %get-tuple-element.22), channel_id=1, source_target_pairs={{0,32},{32,64},{64,96},{96,128},{128,160},{160,192},{192,224},{224... | collective-permute-start | bytes 393224 | tf_op jit(solution)/shard_map/ppermute | solution.py:404
  13.9 3.7 %basis_products.1 = (bf16[240,8192]{1,0:T(8,128)(2,1)S(1)}, f32[64,16,128]{2,1,0:T(8,128)S(1)}, f32[16,128]{1,0:T(8,128)S(1)}, f32[16,128]{1,0:T(8,128)S(1)}) custom-call(f32[64,64,1,128]{3,2,1,0:T(1,128)} %bitcast.11), custom_call_target="tpu_custom_call" | custom-call | tf_op jit(solution)/shard_map/basis_products/pallas_call | solution.py:161
  17.7 2.4 %collective-permute-start.4 = (f32[16,128]{1,0:T(8,128)S(1)}, f32[16,128]{1,0:T(8,128)S(1)}, u32[]{:S(2)}, u32[]{:S(2)}) collective-permute-start(f32[16,128]{1,0:T(8,128)S(1)} %get-tuple-element.24), channel_id=1, source_target_pairs={{0,32},{32,0},{1,33},{33,1},{2,34},{34,2},{3,35},{35,3},{4,36},{36... | collective-permute-start | bytes 24584 | tf_op jit(solution)/shard_map/ppermute | solution.py:406
  20.1 0.8 %collective-permute-done.4.got_ref = f32[16,128]{1,0:T(8,128)S(1)} collective-permute-done((f32[16,128]{1,0:T(8,128)S(1)}, f32[16,128]{1,0:T(8,128)S(1)}, u32[]{:S(2)}, u32[]{:S(2)}) %collective-permute-start.4) | collective-permute-done | bytes 8224 | tf_op jit(solution)/shard_map/ppermute | solution.py:406
  20.9 0.0 collective-permute-done.3
  20.9 0.0 collective-permute-done.2
  20.9 0.0 collective-permute-done
  20.9 0.0 collective-permute-done.1
  20.9 1.8 %image_products.1 = (bf16[240,8192]{1,0:T(8,128)(2,1)S(1)}, f32[32,5,4,128]{3,2,1,0:T(4,128)S(1)}) custom-call(f32[4,16,128]{2,1,0:T(8,128)S(1)} %get-tuple-element.17.sizes_ref, f32[64,16,128]{2,1,0:T(8,128)S(1)} %get-tuple-element.18.field_ref, f32[512,128]{1,0:T(8,128)S(1)} %bitcast.7, f32[512,128]{1,0:T(8,128)S(1)} %bitcast.8, ...), custom_call_target="tpu_custom_call", output_to_operand_aliasing={{0}: (8, {})} | custom-call | tf_op jit(solution)/shard_map/image_products/pallas_call | solution.py:266
  22.8 24.6 %all_to_all.10.sums_ref = f32[32,5,4,128]{3,2,1,0:T(4,128)S(1)} all-to-all(f32[32,5,4,128]{3,2,1,0:T(4,128)S(1)} %get-tuple-element.26), channel_id=1, replica_groups=mesh['y'=8,'core'=2,'x'=4,'z'=8] {'x','z'}, dimensions={0} | all-to-all | bytes 655360 | tf_op jit(solution)/shard_map/all_to_all | solution.py:390
  47.4 0.1 regroup.1
  47.4 19.5 %all_to_all.11.sums_ref = f32[16,5,4,128]{3,2,1,0:T(4,128)S(1)} all-to-all(f32[16,5,4,128]{3,2,1,0:T(4,128)S(1)} %regroup.1), channel_id=1, replica_groups=mesh['y'=8,'core'=2,'x'=4,'z'=8] {'y','core'}, dimensions={0} | all-to-all | bytes 327680 | tf_op jit(solution)/shard_map/all_to_all | solution.py:390
  66.9 2.4 %finish.1 = (f32[64,16]{1,0:T(8,128)}, f32[16,16]{1,0:T(8,128)}, f32[1024,128]{1,0:T(8,128)}) custom-call(f32[16,5,4,128]{3,2,1,0:T(4,128)S(1)} %all_to_all.11.sums_ref, bf16[240,8192]{1,0:T(8,128)(2,1)S(1)} %get-tuple-element.27.parts_ref), custom_call_target="tpu_custom_call" | custom-call | tf_op jit(solution)/shard_map/finish/pallas_call | solution.py:375
Async XLA Ops:
  1.8 19.1 %collective-permute-start = (f32[16,4,8,128]{3,2,1,0:T(8,128)S(1)}, f32[16,4,8,128]{3,2,1,0:T(8,128)S(1)}, u32[]{:S(2)}, u32[]{:S(2)}) collective-permute-start(f32[16,4,8,128]{3,2,1,0:T(8,128)S(1)} %get-tuple-element.19), channel_id=1, source_target_pairs={{0,1},{1,2},{2,3},{3,4},{4,5},{5,6},{6,7},{7,8},{8,9},{9,10},{10,1... | collective-permute-start | bytes 786440 | tf_op jit(solution)/shard_map/ppermute | solution.py:401
  6.6 14.3 %collective-permute-start.1 = (f32[16,4,8,128]{3,2,1,0:T(8,128)S(1)}, f32[16,4,8,128]{3,2,1,0:T(8,128)S(1)}, u32[]{:S(2)}, u32[]{:S(2)}) collective-permute-start(f32[16,4,8,128]{3,2,1,0:T(8,128)S(1)} %get-tuple-element.20), channel_id=1, source_target_pairs={{1,0},{2,1},{3,2},{4,3},{5,4},{6,5},{7,6},{8,7},{9,8},{10,9},{11,1... | collective-permute-start | bytes 786440 | tf_op jit(solution)/shard_map/ppermute | solution.py:402
  7.9 13.0 %collective-permute-start.2 = (f32[17,2,8,128]{3,2,1,0:T(8,128)S(1)}, f32[17,2,8,128]{3,2,1,0:T(8,128)S(1)}, u32[]{:S(2)}, u32[]{:S(2)}) collective-permute-start(f32[17,2,8,128]{3,2,1,0:T(8,128)S(1)} %get-tuple-element.21), channel_id=1, source_target_pairs={{0,32},{32,64},{64,96},{96,128},{128,160},{160,192},{192,224},{224... | collective-permute-start | bytes 417800 | tf_op jit(solution)/shard_map/ppermute | solution.py:403
  12.0 8.9 %collective-permute-start.3 = (f32[16,2,8,128]{3,2,1,0:T(8,128)S(1)}, f32[16,2,8,128]{3,2,1,0:T(8,128)S(1)}, u32[]{:S(2)}, u32[]{:S(2)}) collective-permute-start(f32[16,2,8,128]{3,2,1,0:T(8,128)S(1)} %get-tuple-element.22), channel_id=1, source_target_pairs={{0,32},{32,64},{64,96},{96,128},{128,160},{160,192},{192,224},{224... | collective-permute-start | bytes 393224 | tf_op jit(solution)/shard_map/ppermute | solution.py:404
  17.7 3.2 %collective-permute-start.4 = (f32[16,128]{1,0:T(8,128)S(1)}, f32[16,128]{1,0:T(8,128)S(1)}, u32[]{:S(2)}, u32[]{:S(2)}) collective-permute-start(f32[16,128]{1,0:T(8,128)S(1)} %get-tuple-element.24), channel_id=1, source_target_pairs={{0,32},{32,0},{1,33},{33,1},{2,34},{34,2},{3,35},{35,3},{4,36},{36... | collective-permute-start | bytes 24584 | tf_op jit(solution)/shard_map/ppermute | solution.py:406

commit v7 on v5

--- a/solution.py
+++ b/solution.py
@@ -18,9 +18,9 @@
 LINES = 8
 PLACES = STEPS * PLANES * LINES
 CELLS = PLACES * 128
+SIDE = 2 * PLANES * LINES
 TOTAL = 64 * 64 * 8 * 128
 PARTS = 3
-CHUNKS = 1
 HIGHEST = lax.Precision.HIGHEST
 F32 = jnp.float32
 BF16 = jnp.bfloat16
@@ -58,16 +58,17 @@
 
 
 def edges_kernel(
-    num_hbm, den_hbm, basis_hbm, up_ref, down_ref, late_ref, sizes_ref, num_ref, den_ref, sems
+    num_hbm, den_hbm, basis_hbm, near_ref, far_ref, late_ref, sizes_ref, num_ref, den_ref, sems
 ):
     last = BLOCKS - 1
+    odd = lax.axis_index("z") % 2
     counts = [
         pltpu.make_async_copy(num_hbm, num_ref, sems.at[3]),
         pltpu.make_async_copy(den_hbm, den_ref, sems.at[4]),
     ]
     copies = [
-        pltpu.make_async_copy(basis_hbm.at[last, :, :, PLANES - 1], up_ref, sems.at[0]),
-        pltpu.make_async_copy(basis_hbm.at[last, :, :, 0], down_ref, sems.at[1]),
+        pltpu.make_async_copy(basis_hbm.at[last, :, :, 1 - odd], near_ref, sems.at[0]),
+        pltpu.make_async_copy(basis_hbm.at[last, :, :, odd], far_ref, sems.at[1]),
         pltpu.make_async_copy(
             basis_hbm.at[last, :, pl.ds(STEPS - 2, 2)], late_ref.at[pl.ds(0, COLS)], sems.at[2]
         ),
@@ -127,19 +128,14 @@
     ]
     for copy in copies:
         copy.start()
-    products = None
-    per_chunk = PLACES // CHUNKS
-    for chunk in range(CHUNKS):
-        for place in range(chunk * per_chunk, (chunk + 1) * per_chunk):
-            copies[place].wait()
-            value = field_ref[place]
-            last_ref[place] = value[ROWS - COLS :]
-            for part, piece in enumerate(split(value)):
-                parts_ref[part * ROWS : (part + 1) * ROWS, place * 128 : (place + 1) * 128] = piece
-        lanes = slice(chunk * per_chunk * 128, (chunk + 1) * per_chunk * 128)
-        piece = parts_ref[: PARTS * ROWS, lanes]
-        product = lax.dot_general(piece, piece, NT, preferred_element_type=F32)
-        products = product if products is None else products + product
+    for place in range(PLACES):
+        copies[place].wait()
+        value = field_ref[place]
+        last_ref[place] = value[ROWS - COLS :]
+        for part, piece in enumerate(split(value)):
+            parts_ref[part * ROWS : (part + 1) * ROWS, place * 128 : (place + 1) * 128] = piece
+    whole = parts_ref[: PARTS * ROWS]
+    products = lax.dot_general(whole, whole, NT, preferred_element_type=F32)
     gram = part_products(products, ROWS, 0, ROWS)
     rows = [gram[block * COLS : (block + 1) * COLS, block * COLS :] for block in range(BLOCKS)]
     packed = jnp.concatenate([rows[0], rows[1], rows[3]], axis=1)
@@ -177,18 +173,14 @@
     )(in_hbm(basis))
 
 
-def image_kernel(
-    sizes_ref, field_ref, low_ref, high_ref, late_ref, keep_ref, got_ref, parts_in_ref,
-    parts_ref, copies_ref,
-):
-    side_rows = 2 * PLANES * LINES
+def inner_kernel(sizes_ref, field_ref, late_ref, inner_ref):
     sizes = [sizes_ref[step] for step in range(STEPS)]
     first = (lax.axis_index("y") == 0) & (lax.axis_index("core") == 0)
     start = jnp.full((COLS, 128), first.astype(jnp.int32)) == 1
     weights = []
     for step in range(STEPS):
         if step == 0:
-            before = late_ref[pl.ds(COLS * side_rows, LINES), :]
+            before = late_ref[pl.ds(COLS * SIDE, LINES), :]
             before = jnp.where(start, sizes[0], jnp.concatenate([before, before], axis=0))
         else:
             before = sizes[step - 1]
@@ -202,12 +194,8 @@
             two = jnp.where(start, 0.0, two)
         weights.append((now, one, two, 0.5 * sizes[step]))
     lane = lax.broadcasted_iota(jnp.int32, (COLS, 128), 1)
-    base = PARTS * ROWS
-
-    def turned(ref, place):
-        return ref[pl.ds(place, COLS, stride=side_rows), :]
-
-    past = [turned(late_ref, place) for place in range(side_rows)]
+
+    past = [late_ref[pl.ds(place, COLS, stride=SIDE), :] for place in range(SIDE)]
 
     def at(step, plane, line):
         if step < 0:
@@ -219,9 +207,7 @@
         for plane in range(PLANES):
             for line in range(LINES):
                 value = at(step, plane, line)
-                side = step * LINES + line
-                beside = turned(low_ref, side) if plane == 0 else at(step, plane - 1, line)
-                beside += turned(high_ref, side) if plane == PLANES - 1 else at(step, plane + 1, line)
+                beside = at(step, PLANES - 1 - plane, line)
                 if line > 0:
                     beside += at(step, plane, line - 1)
                 if line < LINES - 1:
@@ -234,8 +220,34 @@
                     + two * at(step - 2, plane, line)
                     + kappa * (6.0 * value - beside)
                 )
+                inner_ref[place_of(step, plane, line)] = result
+
+
+def inner(sizes, field, late):
+    return pl.pallas_call(
+        inner_kernel,
+        out_shape=jax.ShapeDtypeStruct((PLACES, COLS, 128), F32),
+        in_specs=[VMEM] * 3,
+        out_specs=VMEM,
+        compiler_params=params(8),
+        name="inner",
+    )(sizes, field, late)
+
+
+def image_kernel(
+    sizes_ref, inner_ref, near_ref, far_ref, keep_ref, got_ref, parts_in_ref, parts_ref, copies_ref
+):
+    base = PARTS * ROWS
+    odd = jnp.full((COLS, 128), lax.axis_index("z") % 2) == 1
+    for step in range(STEPS):
+        kappa = 0.5 * sizes_ref[step]
+        for line in range(LINES):
+            side = pl.ds(step * LINES + line, COLS, stride=STEPS * LINES)
+            near = near_ref[side, :]
+            far = far_ref[side, :]
+            for plane, halo in ((0, jnp.where(odd, near, far)), (1, jnp.where(odd, far, near))):
                 place = place_of(step, plane, line)
-                for part, piece in enumerate(split(result)):
+                for part, piece in enumerate(split(inner_ref[place] - kappa * halo)):
                     parts_ref[
                         base + part * COLS : base + (part + 1) * COLS, place * 128 : (place + 1) * 128
                     ] = piece
@@ -258,19 +270,19 @@
         copies_ref[copy, 4] = last
 
 
-def image_products(sizes, field, low, high, late, keep, got, parts):
+def image_products(sizes, inside, near, far, keep, got, parts):
     return pl.pallas_call(
         image_kernel,
         out_shape=(
             jax.ShapeDtypeStruct((PARTS * FULL, CELLS), BF16),
             jax.ShapeDtypeStruct((SLABS, 5, 4, 128), F32),
         ),
-        in_specs=[VMEM] * 8,
+        in_specs=[VMEM] * 7,
         out_specs=(VMEM, VMEM),
-        input_output_aliases={7: 0},
+        input_output_aliases={6: 0},
         compiler_params=params(20),
         name="image_products",
-    )(sizes, field, low, high, late, keep, got, parts)
+    )(sizes, inside, near, far, keep, got, parts)
 
 
 def regroup_kernel(sums_ref, copies_ref):
@@ -389,17 +401,18 @@
 def per_device(basis, num, den):
     slabs = size_of(SPACE)
     groups = size_of(TM)
-    above = [(i, i + 1) for i in range(slabs - 1)]
-    below = [(i + 1, i) for i in range(slabs - 1)]
+    pairs = [(i, i ^ 1) for i in range(slabs)]
+    others = [(i, ((i + 1) ^ 1) - 1) for i in range(1, slabs - 1)]
     later = [(i, i + 1) for i in range(groups - 1)]
     flat = basis.reshape(ROWS, PLACES, 1, 128)
-    up, down, late, sizes = edges(num, den, basis)
-    low = lax.ppermute(up, SPACE, above).reshape(-1, 128)
-    high = lax.ppermute(down, SPACE, below).reshape(-1, 128)
+    near, far, late, sizes = edges(num, den, basis)
+    near = lax.ppermute(near, SPACE, pairs).reshape(-1, 128)
+    far = lax.ppermute(far, SPACE, others).reshape(-1, 128)
     late = lax.ppermute(late, TM, later).reshape(-1, 128)
     parts, field, keep, give = basis_products(flat)
     got = lax.ppermute(give, "core", [(0, 1), (1, 0)])
-    parts, copies = image_products(sizes, field, low, high, late, keep, got, parts)
+    inside = inner(sizes, field, late)
+    parts, copies = image_products(sizes, inside, near, far, keep, got, parts)
     sums = exchanged(regroup(exchanged(copies, SPACE)), TM)
     hess, triangle, following = finish(sums, parts)
     return (

time: 68.1 us -> 67.6 us (level)
  waiting for transfers between devices: 2.57 us -> 0.32 us
  blocking collectives: 42.7 us -> 44.4 us
    ppermute x2, waiting for transfers between devices: 1.76 us -> 0.01 us  [the longest x1 0.01 us: per_device(): near = lax.ppermute(near, SPACE, pairs).reshape(-1, 128)]
    all_to_all x2, blocking collectives: 42.7 us -> 44.4 us  [exchanged(): return lax.all_to_all(copies, axes, 0, 0)]
  transfers between devices with their start and end apart: 4 -> 4, of which waited for: 2 -> 1; matrix products, arithmetic and copies ran while one was open for 0% -> 0% of each run, Pallas kernels for 5% -> 6%
where the time goes in v7:
time: 67.6 us; the launch traced here: 67.2 us
  blocking collectives  44.4 us (66%)
  starting transfers between devices  12.7 us (19%)
  Pallas kernels  9.12 us (13%)
  between operations  0.7 us (1%)
    all_to_all x2, blocking collectives, exchanged(): return lax.all_to_all(copies, axes, 0, 0)  44.4 us
    ppermute x1, starting transfers between devices, per_device(): late = lax.ppermute(late, TM, later).reshape(-1, 128)  4.59 us
    ppermute x1, starting transfers between devices, per_device(): near = lax.ppermute(near, SPACE, pairs).reshape(-1, 128)  4 us
    pallas_call x1, Pallas kernels, basis_products(): pl.pallas_call(basis_kernel, out_shape=(jax.ShapeDtypeStruct((PARTS * FUL...  3.49 us
    ppermute x1, starting transfers between devices, per_device(): got = lax.ppermute(give, 'core', [(0, 1), (1, 0)])  3.42 us
    pallas_call x1, Pallas kernels, finish(): pl.pallas_call(finish_kernel, out_shape=(jax.ShapeDtypeStruct((ROWS, COLS...  2.37 us
    pallas_call x1, Pallas kernels, image_products(): pl.pallas_call(image_kernel, out_shape=(jax.ShapeDtypeStruct((PARTS * FUL...  1.55 us
  transfers between devices with their start and end apart: 4, of which 1 were waited for; matrix products, arithmetic and copies ran while one was open for 0% of the time, Pallas kernels for 6%

profile of v7, /device:TPU:1, one launch (start us, length us, event | category | flops | bytes accessed | tf_op | source)
XLA Modules:
  0.0 67.2 jit_solution(2237083437194179772)
XLA Ops:
  0.6 1.2 %edges.1 = (f32[16,4,8,128]{3,2,1,0:T(8,128)S(1)}, f32[16,4,8,128]{3,2,1,0:T(8,128)S(1)}, f32[17,2,2,8,128]{4,3,2,1,0:T(8,128)S(1)}, f32[4,16,128]{2,1,0:T(8,128)S(1)}) custom-call(s32[4]{0:T(128)} %num_hbm.1, s32[4]{0:T(128)} %den_hbm.1, f32[4,16,4,2,8,128]{5,4,3,2,1,0:T(8,128)} %basis_hbm.1), custom_call_target="tpu_custom_call" | custom-call | tf_op jit(solution)/shard_map/edges/pallas_call | solution.py:93
  1.8 4.6 %collective-permute-start = (f32[17,2,2,8,128]{4,3,2,1,0:T(8,128)S(1)}, f32[17,2,2,8,128]{4,3,2,1,0:T(8,128)S(1)}, u32[]{:S(2)}, u32[]{:S(2)}) collective-permute-start(f32[17,2,2,8,128]{4,3,2,1,0:T(8,128)S(1)} %get-tuple-element.18), channel_id=1, source_target_pairs={{0,32},{32,64},{64,96},{96,128},{128,160},{160,192},{192,224},{224... | collective-permute-start | bytes 835592 | tf_op jit(solution)/shard_map/ppermute | solution.py:411
  6.4 4.0 %collective-permute-start.1 = (f32[16,4,8,128]{3,2,1,0:T(8,128)S(1)}, f32[16,4,8,128]{3,2,1,0:T(8,128)S(1)}, u32[]{:S(2)}, u32[]{:S(2)}) collective-permute-start(f32[16,4,8,128]{3,2,1,0:T(8,128)S(1)} %get-tuple-element.19), channel_id=1, source_target_pairs={{0,1},{1,0},{2,3},{3,2},{4,5},{5,4},{6,7},{7,6},{8,9},{9,8},{10,11... | collective-permute-start | bytes 786440 | tf_op jit(solution)/shard_map/ppermute | solution.py:409
  10.4 0.7 %collective-permute-start.2 = (f32[16,4,8,128]{3,2,1,0:T(8,128)S(1)}, f32[16,4,8,128]{3,2,1,0:T(8,128)S(1)}, u32[]{:S(2)}, u32[]{:S(2)}) collective-permute-start(f32[16,4,8,128]{3,2,1,0:T(8,128)S(1)} %get-tuple-element.20), channel_id=1, source_target_pairs={{1,2},{2,1},{3,4},{4,3},{5,6},{6,5},{7,8},{8,7},{9,10},{10,9},{11,... | collective-permute-start | bytes 786440 | tf_op jit(solution)/shard_map/ppermute | solution.py:410
  11.1 3.5 %basis_products.1 = (bf16[240,8192]{1,0:T(8,128)(2,1)S(1)}, f32[64,16,128]{2,1,0:T(8,128)S(1)}, f32[16,128]{1,0:T(8,128)S(1)}, f32[16,128]{1,0:T(8,128)S(1)}) custom-call(f32[64,64,1,128]{3,2,1,0:T(1,128)} %bitcast.9), custom_call_target="tpu_custom_call" | custom-call | tf_op jit(solution)/shard_map/basis_products/pallas_call | solution.py:157
  14.6 3.4 %collective-permute-start.3 = (f32[16,128]{1,0:T(8,128)S(1)}, f32[16,128]{1,0:T(8,128)S(1)}, u32[]{:S(2)}, u32[]{:S(2)}) collective-permute-start(f32[16,128]{1,0:T(8,128)S(1)} %get-tuple-element.22), channel_id=1, source_target_pairs={{0,32},{32,0},{1,33},{33,1},{2,34},{34,2},{3,35},{35,3},{4,36},{36... | collective-permute-start | bytes 24584 | tf_op jit(solution)/shard_map/ppermute | solution.py:413
  18.0 0.0 collective-permute-done
  18.0 0.5 inner.1.inner_ref
  18.5 0.3 collective-permute-done.3.got_ref
  18.8 0.0 collective-permute-done.1
  18.8 0.0 collective-permute-done.2
  18.8 1.6 %image_products.1 = (bf16[240,8192]{1,0:T(8,128)(2,1)S(1)}, f32[32,5,4,128]{3,2,1,0:T(4,128)S(1)}) custom-call(f32[4,16,128]{2,1,0:T(8,128)S(1)} %get-tuple-element.16.sizes_ref, f32[64,16,128]{2,1,0:T(8,128)S(1)} %inner.1.inner_ref, f32[512,128]{1,0:T(8,128)S(1)} %bitcast.7, f32[512,128]{1,0:T(8,128)S(1)} %bitcast.8, ...), custom_call_target="tpu_custom_call", output_to_operand_aliasing={{0}: (6, {})} | custom-call | tf_op jit(solution)/shard_map/image_products/pallas_call | solution.py:274
  20.4 24.6 %all_to_all.10.sums_ref = f32[32,5,4,128]{3,2,1,0:T(4,128)S(1)} all-to-all(f32[32,5,4,128]{3,2,1,0:T(4,128)S(1)} %get-tuple-element.24), channel_id=1, replica_groups=mesh['y'=8,'core'=2,'x'=4,'z'=8] {'x','z'}, dimensions={0} | all-to-all | bytes 655360 | tf_op jit(solution)/shard_map/all_to_all | solution.py:398
  45.0 0.1 regroup.1
  45.1 19.8 %all_to_all.11.sums_ref = f32[16,5,4,128]{3,2,1,0:T(4,128)S(1)} all-to-all(f32[16,5,4,128]{3,2,1,0:T(4,128)S(1)} %regroup.1), channel_id=1, replica_groups=mesh['y'=8,'core'=2,'x'=4,'z'=8] {'y','core'}, dimensions={0} | all-to-all | bytes 327680 | tf_op jit(solution)/shard_map/all_to_all | solution.py:398
  64.9 2.4 %finish.1 = (f32[64,16]{1,0:T(8,128)}, f32[16,16]{1,0:T(8,128)}, f32[1024,128]{1,0:T(8,128)}) custom-call(f32[16,5,4,128]{3,2,1,0:T(4,128)S(1)} %all_to_all.11.sums_ref, bf16[240,8192]{1,0:T(8,128)(2,1)S(1)} %get-tuple-element.25.parts_ref), custom_call_target="tpu_custom_call" | custom-call | tf_op jit(solution)/shard_map/finish/pallas_call | solution.py:383
Async XLA Ops:
  1.8 16.2 %collective-permute-start = (f32[17,2,2,8,128]{4,3,2,1,0:T(8,128)S(1)}, f32[17,2,2,8,128]{4,3,2,1,0:T(8,128)S(1)}, u32[]{:S(2)}, u32[]{:S(2)}) collective-permute-start(f32[17,2,2,8,128]{4,3,2,1,0:T(8,128)S(1)} %get-tuple-element.18), channel_id=1, source_target_pairs={{0,32},{32,64},{64,96},{96,128},{128,160},{160,192},{192,224},{224... | collective-permute-start | bytes 835592 | tf_op jit(solution)/shard_map/ppermute | solution.py:411
  6.4 12.4 %collective-permute-start.1 = (f32[16,4,8,128]{3,2,1,0:T(8,128)S(1)}, f32[16,4,8,128]{3,2,1,0:T(8,128)S(1)}, u32[]{:S(2)}, u32[]{:S(2)}) collective-permute-start(f32[16,4,8,128]{3,2,1,0:T(8,128)S(1)} %get-tuple-element.19), channel_id=1, source_target_pairs={{0,1},{1,0},{2,3},{3,2},{4,5},{5,4},{6,7},{7,6},{8,9},{9,8},{10,11... | collective-permute-start | bytes 786440 | tf_op jit(solution)/shard_map/ppermute | solution.py:409
  10.4 8.4 %collective-permute-start.2 = (f32[16,4,8,128]{3,2,1,0:T(8,128)S(1)}, f32[16,4,8,128]{3,2,1,0:T(8,128)S(1)}, u32[]{:S(2)}, u32[]{:S(2)}) collective-permute-start(f32[16,4,8,128]{3,2,1,0:T(8,128)S(1)} %get-tuple-element.20), channel_id=1, source_target_pairs={{1,2},{2,1},{3,4},{4,3},{5,6},{6,5},{7,8},{8,7},{9,10},{10,9},{11,... | collective-permute-start | bytes 786440 | tf_op jit(solution)/shard_map/ppermute | solution.py:410
  14.6 4.2 %collective-permute-start.3 = (f32[16,128]{1,0:T(8,128)S(1)}, f32[16,128]{1,0:T(8,128)S(1)}, u32[]{:S(2)}, u32[]{:S(2)}) collective-permute-start(f32[16,128]{1,0:T(8,128)S(1)} %get-tuple-element.22), channel_id=1, source_target_pairs={{0,32},{32,0},{1,33},{33,1},{2,34},{34,2},{3,35},{35,3},{4,36},{36... | collective-permute-start | bytes 24584 | tf_op jit(solution)/shard_map/ppermute | solution.py:413

commit v8 on v7

--- a/solution.py
+++ b/solution.py
@@ -18,7 +18,7 @@
 LINES = 8
 PLACES = STEPS * PLANES * LINES
 CELLS = PLACES * 128
-SIDE = 2 * PLANES * LINES
+SIDE = PLANES * LINES
 TOTAL = 64 * 64 * 8 * 128
 PARTS = 3
 HIGHEST = lax.Precision.HIGHEST
@@ -70,7 +70,7 @@
         pltpu.make_async_copy(basis_hbm.at[last, :, :, 1 - odd], near_ref, sems.at[0]),
         pltpu.make_async_copy(basis_hbm.at[last, :, :, odd], far_ref, sems.at[1]),
         pltpu.make_async_copy(
-            basis_hbm.at[last, :, pl.ds(STEPS - 2, 2)], late_ref.at[pl.ds(0, COLS)], sems.at[2]
+            basis_hbm.at[last, :, STEPS - 1], late_ref.at[pl.ds(0, COLS)], sems.at[2]
         ),
     ]
     for copy in copies + counts:
@@ -81,9 +81,8 @@
         top = jnp.full((COLS, 128), num_ref[step]).astype(F32)
         bottom = jnp.full((COLS, 128), den_ref[step]).astype(F32)
         sizes_ref[step] = top / bottom
-    for step in range(2):
-        for plane in range(PLANES):
-            late_ref[COLS, step, plane] = sizes_ref[STEPS - 1, :LINES]
+    for plane in range(PLANES):
+        late_ref[COLS, plane] = sizes_ref[STEPS - 1, :LINES]
     for copy in copies:
         copy.wait()
 
@@ -95,7 +94,7 @@
         out_shape=(
             face,
             face,
-            jax.ShapeDtypeStruct((COLS + 1, 2, PLANES, LINES, 128), F32),
+            jax.ShapeDtypeStruct((COLS + 1, PLANES, LINES, 128), F32),
             jax.ShapeDtypeStruct((STEPS, COLS, 128), F32),
         ),
         in_specs=[HBM, HBM, HBM],
@@ -132,6 +131,8 @@
         copies[place].wait()
         value = field_ref[place]
         last_ref[place] = value[ROWS - COLS :]
+        if place_of(STEPS - 2, 0, 0) <= place < place_of(STEPS - 1, 0, 0):
+            give_ref[place - place_of(STEPS - 2, 0, 0)] = value[ROWS - COLS :]
         for part, piece in enumerate(split(value)):
             parts_ref[part * ROWS : (part + 1) * ROWS, place * 128 : (place + 1) * 128] = piece
     whole = parts_ref[: PARTS * ROWS]
@@ -146,11 +147,11 @@
         halves.append((packed[half * 8 : half * 8 + 8], rest))
     own = lax.axis_index("core")
     first = jnp.full((8, 128), own) == 0
-    for target, flip in ((keep_ref, False), (give_ref, True)):
+    for target, flip in ((keep_ref, False), (give_ref.at[SIDE], True)):
         one, two = (halves[1], halves[0]) if flip else (halves[0], halves[1])
         target[0:8] = jnp.where(first, one[0], two[0])
         target[8:10] = jnp.where(first[:2], one[1], two[1])
-        target[10:16] = jnp.zeros((6, 128), F32)
+        target[10:COLS] = jnp.zeros((COLS - 10, 128), F32)
 
 
 def basis_products(basis):
@@ -159,8 +160,8 @@
         out_shape=(
             jax.ShapeDtypeStruct((PARTS * FULL, CELLS), BF16),
             jax.ShapeDtypeStruct((PLACES, COLS, 128), F32),
-            jax.ShapeDtypeStruct((16, 128), F32),
-            jax.ShapeDtypeStruct((16, 128), F32),
+            jax.ShapeDtypeStruct((COLS, 128), F32),
+            jax.ShapeDtypeStruct((SIDE + 1, COLS, 128), F32),
         ),
         in_specs=[HBM],
         out_specs=(VMEM, VMEM, VMEM, VMEM),
@@ -173,12 +174,20 @@
     )(in_hbm(basis))
 
 
-def inner_kernel(sizes_ref, field_ref, late_ref, inner_ref):
+def inner_kernel(sizes_ref, field_ref, late_ref, near_ref, far_ref, inner_ref, weight_ref):
     sizes = [sizes_ref[step] for step in range(STEPS)]
+    odd = jnp.full((COLS, 128), lax.axis_index("z") % 2) == 1
     first = (lax.axis_index("y") == 0) & (lax.axis_index("core") == 0)
     start = jnp.full((COLS, 128), first.astype(jnp.int32)) == 1
-    weights = []
+    lane = lax.broadcasted_iota(jnp.int32, (COLS, 128), 1)
+
+    def at(step, plane, line):
+        if step < 0:
+            return late_ref[pl.ds(plane * LINES + line, COLS, stride=SIDE), :]
+        return field_ref[place_of(step, plane, line)]
+
     for step in range(STEPS):
+        kappa = 0.5 * sizes[step]
         if step == 0:
             before = late_ref[pl.ds(COLS * SIDE, LINES), :]
             before = jnp.where(start, sizes[0], jnp.concatenate([before, before], axis=0))
@@ -191,66 +200,54 @@
         if step == 0:
             now = jnp.where(start, 1.0, now)
             one = jnp.where(start, 1.0, one)
-            two = jnp.where(start, 0.0, two)
-        weights.append((now, one, two, 0.5 * sizes[step]))
-    lane = lax.broadcasted_iota(jnp.int32, (COLS, 128), 1)
-
-    past = [late_ref[pl.ds(place, COLS, stride=SIDE), :] for place in range(SIDE)]
-
-    def at(step, plane, line):
-        if step < 0:
-            return past[place_of(step + 2, plane, line)]
-        return field_ref[place_of(step, plane, line)]
-
-    for step in range(STEPS):
-        now, one, two, kappa = weights[step]
-        for plane in range(PLANES):
-            for line in range(LINES):
+            weight_ref[...] = jnp.where(start, 0.0, two)
+        for line in range(LINES):
+            side = pl.ds(step * LINES + line, COLS, stride=STEPS * LINES)
+            near = near_ref[side, :]
+            far = far_ref[side, :]
+            for plane, halo in ((0, jnp.where(odd, near, far)), (1, jnp.where(odd, far, near))):
                 value = at(step, plane, line)
-                beside = at(step, PLANES - 1 - plane, line)
+                beside = halo + at(step, PLANES - 1 - plane, line)
                 if line > 0:
                     beside += at(step, plane, line - 1)
                 if line < LINES - 1:
                     beside += at(step, plane, line + 1)
                 beside += jnp.where(lane < 127, pltpu.roll(value, 127, 1), 0.0)
                 beside += jnp.where(lane > 0, pltpu.roll(value, 1, 1), 0.0)
-                result = (
-                    now * value
-                    - one * at(step - 1, plane, line)
-                    + two * at(step - 2, plane, line)
-                    + kappa * (6.0 * value - beside)
-                )
+                result = now * value - one * at(step - 1, plane, line)
+                if step > 0:
+                    result += two * at(step - 2, plane, line)
+                result += kappa * (6.0 * value - beside)
                 inner_ref[place_of(step, plane, line)] = result
 
 
-def inner(sizes, field, late):
+def inner(sizes, field, late, near, far):
     return pl.pallas_call(
         inner_kernel,
-        out_shape=jax.ShapeDtypeStruct((PLACES, COLS, 128), F32),
-        in_specs=[VMEM] * 3,
-        out_specs=VMEM,
+        out_shape=(
+            jax.ShapeDtypeStruct((PLACES, COLS, 128), F32),
+            jax.ShapeDtypeStruct((COLS, 128), F32),
+        ),
+        in_specs=[VMEM] * 5,
+        out_specs=(VMEM, VMEM),
         compiler_params=params(8),
         name="inner",
-    )(sizes, field, late)
+    )(sizes, field, late, near, far)
 
 
 def image_kernel(
-    sizes_ref, inner_ref, near_ref, far_ref, keep_ref, got_ref, parts_in_ref, parts_ref, copies_ref
+    weight_ref, inner_ref, keep_ref, got_ref, parts_in_ref, parts_ref, copies_ref
 ):
     base = PARTS * ROWS
-    odd = jnp.full((COLS, 128), lax.axis_index("z") % 2) == 1
-    for step in range(STEPS):
-        kappa = 0.5 * sizes_ref[step]
-        for line in range(LINES):
-            side = pl.ds(step * LINES + line, COLS, stride=STEPS * LINES)
-            near = near_ref[side, :]
-            far = far_ref[side, :]
-            for plane, halo in ((0, jnp.where(odd, near, far)), (1, jnp.where(odd, far, near))):
-                place = place_of(step, plane, line)
-                for part, piece in enumerate(split(inner_ref[place] - kappa * halo)):
-                    parts_ref[
-                        base + part * COLS : base + (part + 1) * COLS, place * 128 : (place + 1) * 128
-                    ] = piece
+    weight = weight_ref[...]
+    for place in range(PLACES):
+        result = inner_ref[place]
+        if place < SIDE:
+            result += weight * got_ref[place]
+        for part, piece in enumerate(split(result)):
+            parts_ref[
+                base + part * COLS : base + (part + 1) * COLS, place * 128 : (place + 1) * 128
+            ] = piece
     own_parts = parts_ref[base:]
     products = lax.dot_general(own_parts, parts_ref[...], NT, preferred_element_type=F32)
     proj = part_products(products, COLS, 0, ROWS)
@@ -260,7 +257,7 @@
     for half in range(2):
         lines = [gram[half * 8 + row : half * 8 + row + 1] for row in range(8)]
         pieces.append(jnp.concatenate(lines, axis=1))
-    chip = keep_ref[...] + got_ref[...]
+    chip = keep_ref[...] + got_ref[SIDE]
     last = jnp.concatenate(pieces + [chip[8:10]], axis=0)
     for copy in range(SLABS):
         copies_ref[copy, 0] = packed[:4]
@@ -270,19 +267,19 @@
         copies_ref[copy, 4] = last
 
 
-def image_products(sizes, inside, near, far, keep, got, parts):
+def image_products(weight, inside, keep, got, parts):
     return pl.pallas_call(
         image_kernel,
         out_shape=(
             jax.ShapeDtypeStruct((PARTS * FULL, CELLS), BF16),
             jax.ShapeDtypeStruct((SLABS, 5, 4, 128), F32),
         ),
-        in_specs=[VMEM] * 7,
+        in_specs=[VMEM] * 5,
         out_specs=(VMEM, VMEM),
-        input_output_aliases={6: 0},
+        input_output_aliases={4: 0},
         compiler_params=params(20),
         name="image_products",
-    )(sizes, inside, near, far, keep, got, parts)
+    )(weight, inside, keep, got, parts)
 
 
 def regroup_kernel(sums_ref, copies_ref):
@@ -410,9 +407,9 @@
     far = lax.ppermute(far, SPACE, others).reshape(-1, 128)
     late = lax.ppermute(late, TM, later).reshape(-1, 128)
     parts, field, keep, give = basis_products(flat)
-    got = lax.ppermute(give, "core", [(0, 1), (1, 0)])
-    inside = inner(sizes, field, late)
-    parts, copies = image_products(sizes, inside, near, far, keep, got, parts)
+    got = lax.ppermute(give, TM, later + [(groups - 1, 0)])
+    inside, weight = inner(sizes, field, late, near, far)
+    parts, copies = image_products(weight, inside, keep, got, parts)
     sums = exchanged(regroup(exchanged(copies, SPACE)), TM)
     hess, triangle, following = finish(sums, parts)
     return (

time: 67.6 us -> 66.3 us (0.981)
  starting transfers between devices: 12.7 us -> 9.58 us
  waiting for transfers between devices: 0.32 us -> 1.35 us
    ppermute x1, starting transfers between devices: 3.42 us -> 0.02 us  [per_device(): got = lax.ppermute(give, TM, later + [(groups - 1, 0)])]
    ppermute x1, waiting for transfers between devices: 0.31 us -> 1.35 us  [per_device(): got = lax.ppermute(give, TM, later + [(groups - 1, 0)])]
    ppermute x1, starting transfers between devices: 4 us -> 4.83 us  [per_device(): near = lax.ppermute(near, SPACE, pairs).reshape(-1, 128)]
where the time goes in v8:
time: 66.3 us; the launch traced here: 65.9 us
  blocking collectives  45 us (68%)
  starting transfers between devices  9.58 us (14%)
  Pallas kernels  9.22 us (14%)
  waiting for transfers between devices  1.35 us (2%)
  between operations  0.71 us (1%)
    all_to_all x2, blocking collectives, exchanged(): return lax.all_to_all(copies, axes, 0, 0)  45 us
    ppermute x1, starting transfers between devices, per_device(): near = lax.ppermute(near, SPACE, pairs).reshape(-1, 128)  4.83 us
    ppermute x1, starting transfers between devices, per_device(): late = lax.ppermute(late, TM, later).reshape(-1, 128)  4.05 us
    pallas_call x1, Pallas kernels, basis_products(): pl.pallas_call(basis_kernel, out_shape=(jax.ShapeDtypeStruct((PARTS * FUL...  3.5 us
    pallas_call x1, Pallas kernels, finish(): pl.pallas_call(finish_kernel, out_shape=(jax.ShapeDtypeStruct((ROWS, COLS...  2.37 us
    pallas_call x1, Pallas kernels, image_products(): pl.pallas_call(image_kernel, out_shape=(jax.ShapeDtypeStruct((PARTS * FUL...  1.49 us
    ppermute x1, waiting for transfers between devices, per_device(): got = lax.ppermute(give, TM, later + [(groups - 1, 0)])  1.35 us
  transfers between devices with their start and end apart: 4, of which 1 were waited for; matrix products, arithmetic and copies ran while one was open for 0% of the time, Pallas kernels for 6%

profile of v8, /device:TPU:1, one launch (start us, length us, event | category | flops | bytes accessed | tf_op | source)
XLA Modules:
  0.0 65.9 jit_solution(14621285108064275489)
XLA Ops:
  0.6 1.1 %edges.1 = (f32[16,4,8,128]{3,2,1,0:T(8,128)S(1)}, f32[16,4,8,128]{3,2,1,0:T(8,128)S(1)}, f32[17,2,8,128]{3,2,1,0:T(8,128)S(1)}, f32[4,16,128]{2,1,0:T(8,128)S(1)}) custom-call(s32[4]{0:T(128)} %num_hbm.1, s32[4]{0:T(128)} %den_hbm.1, f32[4,16,4,2,8,128]{5,4,3,2,1,0:T(8,128)} %basis_hbm.1), custom_call_target="tpu_custom_call" | custom-call | tf_op jit(solution)/shard_map/edges/pallas_call | solution.py:92
  1.8 4.8 %collective-permute-start.1 = (f32[16,4,8,128]{3,2,1,0:T(8,128)S(1)}, f32[16,4,8,128]{3,2,1,0:T(8,128)S(1)}, u32[]{:S(2)}, u32[]{:S(2)}) collective-permute-start(f32[16,4,8,128]{3,2,1,0:T(8,128)S(1)} %get-tuple-element.21), channel_id=1, source_target_pairs={{0,1},{1,0},{2,3},{3,2},{4,5},{5,4},{6,7},{7,6},{8,9},{9,8},{10,11... | collective-permute-start | bytes 786440 | tf_op jit(solution)/shard_map/ppermute | solution.py:406
  6.6 0.7 %collective-permute-start.2 = (f32[16,4,8,128]{3,2,1,0:T(8,128)S(1)}, f32[16,4,8,128]{3,2,1,0:T(8,128)S(1)}, u32[]{:S(2)}, u32[]{:S(2)}) collective-permute-start(f32[16,4,8,128]{3,2,1,0:T(8,128)S(1)} %get-tuple-element.22), channel_id=1, source_target_pairs={{1,2},{2,1},{3,4},{4,3},{5,6},{6,5},{7,8},{8,7},{9,10},{10,9},{11,... | collective-permute-start | bytes 786440 | tf_op jit(solution)/shard_map/ppermute | solution.py:407
  7.3 4.0 %collective-permute-start = (f32[17,2,8,128]{3,2,1,0:T(8,128)S(1)}, f32[17,2,8,128]{3,2,1,0:T(8,128)S(1)}, u32[]{:S(2)}, u32[]{:S(2)}) collective-permute-start(f32[17,2,8,128]{3,2,1,0:T(8,128)S(1)} %get-tuple-element.20), channel_id=1, source_target_pairs={{0,32},{32,64},{64,96},{96,128},{128,160},{160,192},{192,224},{224... | collective-permute-start | bytes 417800 | tf_op jit(solution)/shard_map/ppermute | solution.py:408
  11.3 3.5 %basis_products.1 = (bf16[240,8192]{1,0:T(8,128)(2,1)S(1)}, f32[64,16,128]{2,1,0:T(8,128)S(1)}, f32[16,128]{1,0:T(8,128)S(1)}, f32[17,16,128]{2,1,0:T(8,128)S(1)}) custom-call(f32[64,64,1,128]{3,2,1,0:T(1,128)} %bitcast.9), custom_call_target="tpu_custom_call" | custom-call | tf_op jit(solution)/shard_map/basis_products/pallas_call | solution.py:158
  14.8 0.0 collective-permute-start.3
  14.9 0.0 collective-permute-done
  14.9 0.0 collective-permute-done.1
  14.9 0.0 collective-permute-done.2
  14.9 0.7 %inner.1 = (f32[64,16,128]{2,1,0:T(8,128)S(1)}, f32[16,128]{1,0:T(8,128)S(1)}) custom-call(f32[4,16,128]{2,1,0:T(8,128)S(1)} %get-tuple-element.18.sizes_ref, f32[64,16,128]{2,1,0:T(8,128)S(1)} %get-tuple-element.19.field_ref, f32[272,128]{1,0:T(8,128)S(1)} %bitcast.8, f32[512,128]{1,0:T(8,128)S(1)} %bitcast.6, f32[512,128]{1,0:T(8,128)S(1)} %bitcast.7), custom_call_target="tpu_custom_call" | custom-call | tf_op jit(solution)/shard_map/inner/pallas_call | solution.py:225
  15.6 1.3 %collective-permute-done.3.got_ref = f32[17,16,128]{2,1,0:T(8,128)S(1)} collective-permute-done((f32[17,16,128]{2,1,0:T(8,128)S(1)}, f32[17,16,128]{2,1,0:T(8,128)S(1)}, u32[]{:S(2)}, u32[]{:S(2)}) %collective-permute-start.3) | collective-permute-done | bytes 139296 | tf_op jit(solution)/shard_map/ppermute | solution.py:410
  16.9 1.5 %image_products.1 = (bf16[240,8192]{1,0:T(8,128)(2,1)S(1)}, f32[32,5,4,128]{3,2,1,0:T(4,128)S(1)}) custom-call(f32[16,128]{1,0:T(8,128)S(1)} %get-tuple-element.23.weight_ref, f32[64,16,128]{2,1,0:T(8,128)S(1)} %get-tuple-element.24.inner_ref, f32[16,128]{1,0:T(8,128)S(1)} %get-tuple-element.25.keep_ref, ...), custom_call_target="tpu_custom_call", output_to_operand_aliasing={{0}: (4, {})} | custom-call | tf_op jit(solution)/shard_map/image_products/pallas_call | solution.py:271
  18.4 24.4 %all_to_all.10.sums_ref = f32[32,5,4,128]{3,2,1,0:T(4,128)S(1)} all-to-all(f32[32,5,4,128]{3,2,1,0:T(4,128)S(1)} %get-tuple-element.28), channel_id=1, replica_groups=mesh['y'=8,'core'=2,'x'=4,'z'=8] {'x','z'}, dimensions={0} | all-to-all | bytes 655360 | tf_op jit(solution)/shard_map/all_to_all | solution.py:395
  42.8 0.1 regroup.1
  42.9 20.6 %all_to_all.11.sums_ref = f32[16,5,4,128]{3,2,1,0:T(4,128)S(1)} all-to-all(f32[16,5,4,128]{3,2,1,0:T(4,128)S(1)} %regroup.1), channel_id=1, replica_groups=mesh['y'=8,'core'=2,'x'=4,'z'=8] {'y','core'}, dimensions={0} | all-to-all | bytes 327680 | tf_op jit(solution)/shard_map/all_to_all | solution.py:395
  63.5 2.4 %finish.1 = (f32[64,16]{1,0:T(8,128)}, f32[16,16]{1,0:T(8,128)}, f32[1024,128]{1,0:T(8,128)}) custom-call(f32[16,5,4,128]{3,2,1,0:T(4,128)S(1)} %all_to_all.11.sums_ref, bf16[240,8192]{1,0:T(8,128)(2,1)S(1)} %get-tuple-element.29.parts_ref), custom_call_target="tpu_custom_call" | custom-call | tf_op jit(solution)/shard_map/finish/pallas_call | solution.py:380
Async XLA Ops:
  1.8 13.1 %collective-permute-start.1 = (f32[16,4,8,128]{3,2,1,0:T(8,128)S(1)}, f32[16,4,8,128]{3,2,1,0:T(8,128)S(1)}, u32[]{:S(2)}, u32[]{:S(2)}) collective-permute-start(f32[16,4,8,128]{3,2,1,0:T(8,128)S(1)} %get-tuple-element.21), channel_id=1, source_target_pairs={{0,1},{1,0},{2,3},{3,2},{4,5},{5,4},{6,7},{7,6},{8,9},{9,8},{10,11... | collective-permute-start | bytes 786440 | tf_op jit(solution)/shard_map/ppermute | solution.py:406
  6.6 8.3 %collective-permute-start.2 = (f32[16,4,8,128]{3,2,1,0:T(8,128)S(1)}, f32[16,4,8,128]{3,2,1,0:T(8,128)S(1)}, u32[]{:S(2)}, u32[]{:S(2)}) collective-permute-start(f32[16,4,8,128]{3,2,1,0:T(8,128)S(1)} %get-tuple-element.22), channel_id=1, source_target_pairs={{1,2},{2,1},{3,4},{4,3},{5,6},{6,5},{7,8},{8,7},{9,10},{10,9},{11,... | collective-permute-start | bytes 786440 | tf_op jit(solution)/shard_map/ppermute | solution.py:407
  7.3 7.6 %collective-permute-start = (f32[17,2,8,128]{3,2,1,0:T(8,128)S(1)}, f32[17,2,8,128]{3,2,1,0:T(8,128)S(1)}, u32[]{:S(2)}, u32[]{:S(2)}) collective-permute-start(f32[17,2,8,128]{3,2,1,0:T(8,128)S(1)} %get-tuple-element.20), channel_id=1, source_target_pairs={{0,32},{32,64},{64,96},{96,128},{128,160},{160,192},{192,224},{224... | collective-permute-start | bytes 417800 | tf_op jit(solution)/shard_map/ppermute | solution.py:408
  14.8 2.1 %collective-permute-start.3 = (f32[17,16,128]{2,1,0:T(8,128)S(1)}, f32[17,16,128]{2,1,0:T(8,128)S(1)}, u32[]{:S(2)}, u32[]{:S(2)}) collective-permute-start(f32[17,16,128]{2,1,0:T(8,128)S(1)} %get-tuple-element.26), channel_id=1, source_target_pairs={{0,32},{32,64},{64,96},{96,128},{128,160},{160,192},{192,224},{224... | collective-permute-start | bytes 417800 | tf_op jit(solution)/shard_map/ppermute | solution.py:410

commit v9 on v7

--- a/solution.py
+++ b/solution.py
@@ -58,17 +58,17 @@
 
 
 def edges_kernel(
-    num_hbm, den_hbm, basis_hbm, near_ref, far_ref, late_ref, sizes_ref, num_ref, den_ref, sems
+    num_hbm, den_hbm, basis_hbm, first_ref, second_ref, late_ref, sizes_ref, num_ref, den_ref, sems
 ):
     last = BLOCKS - 1
-    odd = lax.axis_index("z") % 2
+    flip = (lax.axis_index("z") + lax.axis_index("core")) % 2
     counts = [
         pltpu.make_async_copy(num_hbm, num_ref, sems.at[3]),
         pltpu.make_async_copy(den_hbm, den_ref, sems.at[4]),
     ]
     copies = [
-        pltpu.make_async_copy(basis_hbm.at[last, :, :, 1 - odd], near_ref, sems.at[0]),
-        pltpu.make_async_copy(basis_hbm.at[last, :, :, odd], far_ref, sems.at[1]),
+        pltpu.make_async_copy(basis_hbm.at[last, :, :, 1 - flip], first_ref, sems.at[0]),
+        pltpu.make_async_copy(basis_hbm.at[last, :, :, flip], second_ref, sems.at[1]),
         pltpu.make_async_copy(
             basis_hbm.at[last, :, pl.ds(STEPS - 2, 2)], late_ref.at[pl.ds(0, COLS)], sems.at[2]
         ),
@@ -235,17 +235,18 @@
 
 
 def image_kernel(
-    sizes_ref, inner_ref, near_ref, far_ref, keep_ref, got_ref, parts_in_ref, parts_ref, copies_ref
+    sizes_ref, inner_ref, first_ref, second_ref, keep_ref, got_ref, parts_in_ref, parts_ref, copies_ref
 ):
     base = PARTS * ROWS
-    odd = jnp.full((COLS, 128), lax.axis_index("z") % 2) == 1
+    flip = (lax.axis_index("z") + lax.axis_index("core")) % 2
+    flipped = jnp.full((COLS, 128), flip) == 1
     for step in range(STEPS):
         kappa = 0.5 * sizes_ref[step]
         for line in range(LINES):
             side = pl.ds(step * LINES + line, COLS, stride=STEPS * LINES)
-            near = near_ref[side, :]
-            far = far_ref[side, :]
-            for plane, halo in ((0, jnp.where(odd, near, far)), (1, jnp.where(odd, far, near))):
+            one = first_ref[side, :]
+            two = second_ref[side, :]
+            for plane, halo in ((0, jnp.where(flipped, one, two)), (1, jnp.where(flipped, two, one))):
                 place = place_of(step, plane, line)
                 for part, piece in enumerate(split(inner_ref[place] - kappa * halo)):
                     parts_ref[
@@ -270,7 +271,7 @@
         copies_ref[copy, 4] = last
 
 
-def image_products(sizes, inside, near, far, keep, got, parts):
+def image_products(sizes, inside, one, two, keep, got, parts):
     return pl.pallas_call(
         image_kernel,
         out_shape=(
@@ -282,7 +283,7 @@
         input_output_aliases={6: 0},
         compiler_params=params(20),
         name="image_products",
-    )(sizes, inside, near, far, keep, got, parts)
+    )(sizes, inside, one, two, keep, got, parts)
 
 
 def regroup_kernel(sums_ref, copies_ref):
@@ -403,11 +404,13 @@
     groups = size_of(TM)
     pairs = [(i, i ^ 1) for i in range(slabs)]
     others = [(i, ((i + 1) ^ 1) - 1) for i in range(1, slabs - 1)]
+    first = pairs + [(i + slabs, j + slabs) for i, j in others]
+    second = others + [(i + slabs, j + slabs) for i, j in pairs]
     later = [(i, i + 1) for i in range(groups - 1)]
     flat = basis.reshape(ROWS, PLACES, 1, 128)
     near, far, late, sizes = edges(num, den, basis)
-    near = lax.ppermute(near, SPACE, pairs).reshape(-1, 128)
-    far = lax.ppermute(far, SPACE, others).reshape(-1, 128)
+    near = lax.ppermute(near, ("core",) + SPACE, first).reshape(-1, 128)
+    far = lax.ppermute(far, ("core",) + SPACE, second).reshape(-1, 128)
     late = lax.ppermute(late, TM, later).reshape(-1, 128)
     parts, field, keep, give = basis_products(flat)
     got = lax.ppermute(give, "core", [(0, 1), (1, 0)])

time: 67.6 us -> 66.1 us (0.978)
  blocking collectives: 44.4 us -> 40.7 us
  starting transfers between devices: 12.7 us -> 14.5 us
    all_to_all x2, blocking collectives: 44.4 us -> 40.7 us  [exchanged(): return lax.all_to_all(copies, axes, 0, 0)]
    ppermute x2, starting transfers between devices: 4.68 us -> 8 us  [the longest x1 7.32 us: per_device(): far = lax.ppermute(far, ('core',) + SPACE, second).reshape(-1, 128)]
    ppermute x1, starting transfers between devices: 3.42 us -> 1.92 us  [per_device(): got = lax.ppermute(give, 'core', [(0, 1), (1, 0)])]
where the time goes in v9:
time: 66.1 us; the launch traced here: 65.7 us
  blocking collectives  40.7 us (62%)
  starting transfers between devices  14.5 us (22%)
  Pallas kernels  9.12 us (14%)
  between operations  0.7 us (1%)
    all_to_all x2, blocking collectives, exchanged(): return lax.all_to_all(copies, axes, 0, 0)  40.7 us
    ppermute x1, starting transfers between devices, per_device(): far = lax.ppermute(far, ('core',) + SPACE, second).reshape(-1, 128)  7.32 us
    ppermute x1, starting transfers between devices, per_device(): late = lax.ppermute(late, TM, later).reshape(-1, 128)  4.59 us
    pallas_call x1, Pallas kernels, basis_products(): pl.pallas_call(basis_kernel, out_shape=(jax.ShapeDtypeStruct((PARTS * FUL...  3.49 us
    pallas_call x1, Pallas kernels, finish(): pl.pallas_call(finish_kernel, out_shape=(jax.ShapeDtypeStruct((ROWS, COLS...  2.37 us
    ppermute x1, starting transfers between devices, per_device(): got = lax.ppermute(give, 'core', [(0, 1), (1, 0)])  1.92 us
    pallas_call x1, Pallas kernels, image_products(): pl.pallas_call(image_kernel, out_shape=(jax.ShapeDtypeStruct((PARTS * FUL...  1.56 us
  transfers between devices with their start and end apart: 4, of which 1 were waited for; matrix products, arithmetic and copies ran while one was open for 0% of the time, Pallas kernels for 6%

profile of v9, /device:TPU:1, one launch (start us, length us, event | category | flops | bytes accessed | tf_op | source)
XLA Modules:
  0.0 65.7 jit_solution(14688944182036534747)
XLA Ops:
  0.6 1.2 %edges.1 = (f32[16,4,8,128]{3,2,1,0:T(8,128)S(1)}, f32[16,4,8,128]{3,2,1,0:T(8,128)S(1)}, f32[17,2,2,8,128]{4,3,2,1,0:T(8,128)S(1)}, f32[4,16,128]{2,1,0:T(8,128)S(1)}) custom-call(s32[4]{0:T(128)} %num_hbm.1, s32[4]{0:T(128)} %den_hbm.1, f32[4,16,4,2,8,128]{5,4,3,2,1,0:T(8,128)} %basis_hbm.1), custom_call_target="tpu_custom_call" | custom-call | tf_op jit(solution)/shard_map/edges/pallas_call | solution.py:93
  1.8 4.6 %collective-permute-start = (f32[17,2,2,8,128]{4,3,2,1,0:T(8,128)S(1)}, f32[17,2,2,8,128]{4,3,2,1,0:T(8,128)S(1)}, u32[]{:S(2)}, u32[]{:S(2)}) collective-permute-start(f32[17,2,2,8,128]{4,3,2,1,0:T(8,128)S(1)} %get-tuple-element.18), channel_id=1, source_target_pairs={{0,32},{32,64},{64,96},{96,128},{128,160},{160,192},{192,224},{224... | collective-permute-start | bytes 835592 | tf_op jit(solution)/shard_map/ppermute | solution.py:414
  6.4 0.7 %collective-permute-start.1 = (f32[16,4,8,128]{3,2,1,0:T(8,128)S(1)}, f32[16,4,8,128]{3,2,1,0:T(8,128)S(1)}, u32[]{:S(2)}, u32[]{:S(2)}) collective-permute-start(f32[16,4,8,128]{3,2,1,0:T(8,128)S(1)} %get-tuple-element.19), channel_id=1, source_target_pairs={{0,1},{1,0},{2,3},{3,2},{4,5},{5,4},{6,7},{7,6},{8,9},{9,8},{10,11... | collective-permute-start | bytes 786440 | tf_op jit(solution)/shard_map/ppermute | solution.py:412
  7.1 7.3 %collective-permute-start.2 = (f32[16,4,8,128]{3,2,1,0:T(8,128)S(1)}, f32[16,4,8,128]{3,2,1,0:T(8,128)S(1)}, u32[]{:S(2)}, u32[]{:S(2)}) collective-permute-start(f32[16,4,8,128]{3,2,1,0:T(8,128)S(1)} %get-tuple-element.20), channel_id=1, source_target_pairs={{1,2},{2,1},{3,4},{4,3},{5,6},{6,5},{7,8},{8,7},{9,10},{10,9},{11,... | collective-permute-start | bytes 786440 | tf_op jit(solution)/shard_map/ppermute | solution.py:413
  14.4 3.5 %basis_products.1 = (bf16[240,8192]{1,0:T(8,128)(2,1)S(1)}, f32[64,16,128]{2,1,0:T(8,128)S(1)}, f32[16,128]{1,0:T(8,128)S(1)}, f32[16,128]{1,0:T(8,128)S(1)}) custom-call(f32[64,64,1,128]{3,2,1,0:T(1,128)} %bitcast.9), custom_call_target="tpu_custom_call" | custom-call | tf_op jit(solution)/shard_map/basis_products/pallas_call | solution.py:157
  17.9 1.9 %collective-permute-start.3 = (f32[16,128]{1,0:T(8,128)S(1)}, f32[16,128]{1,0:T(8,128)S(1)}, u32[]{:S(2)}, u32[]{:S(2)}) collective-permute-start(f32[16,128]{1,0:T(8,128)S(1)} %get-tuple-element.22), channel_id=1, source_target_pairs={{0,32},{32,0},{1,33},{33,1},{2,34},{34,2},{3,35},{35,3},{4,36},{36... | collective-permute-start | bytes 24584 | tf_op jit(solution)/shard_map/ppermute | solution.py:416
  19.9 0.0 collective-permute-done
  19.9 0.5 inner.1.inner_ref
  20.3 0.6 collective-permute-done.3.got_ref
  21.0 0.0 collective-permute-done.1
  21.0 0.0 collective-permute-done.2
  21.0 1.6 %image_products.1 = (bf16[240,8192]{1,0:T(8,128)(2,1)S(1)}, f32[32,5,4,128]{3,2,1,0:T(4,128)S(1)}) custom-call(f32[4,16,128]{2,1,0:T(8,128)S(1)} %get-tuple-element.16.sizes_ref, f32[64,16,128]{2,1,0:T(8,128)S(1)} %inner.1.inner_ref, f32[512,128]{1,0:T(8,128)S(1)} %bitcast.7, f32[512,128]{1,0:T(8,128)S(1)} %bitcast.8, ...), custom_call_target="tpu_custom_call", output_to_operand_aliasing={{0}: (6, {})} | custom-call | tf_op jit(solution)/shard_map/image_products/pallas_call | solution.py:275
  22.6 21.6 %all_to_all.10.sums_ref = f32[32,5,4,128]{3,2,1,0:T(4,128)S(1)} all-to-all(f32[32,5,4,128]{3,2,1,0:T(4,128)S(1)} %get-tuple-element.24), channel_id=1, replica_groups=mesh['y'=8,'core'=2,'x'=4,'z'=8] {'x','z'}, dimensions={0} | all-to-all | bytes 655360 | tf_op jit(solution)/shard_map/all_to_all | solution.py:399
  44.2 0.1 regroup.1
  44.2 19.1 %all_to_all.11.sums_ref = f32[16,5,4,128]{3,2,1,0:T(4,128)S(1)} all-to-all(f32[16,5,4,128]{3,2,1,0:T(4,128)S(1)} %regroup.1), channel_id=1, replica_groups=mesh['y'=8,'core'=2,'x'=4,'z'=8] {'y','core'}, dimensions={0} | all-to-all | bytes 327680 | tf_op jit(solution)/shard_map/all_to_all | solution.py:399
  63.3 2.4 %finish.1 = (f32[64,16]{1,0:T(8,128)}, f32[16,16]{1,0:T(8,128)}, f32[1024,128]{1,0:T(8,128)}) custom-call(f32[16,5,4,128]{3,2,1,0:T(4,128)S(1)} %all_to_all.11.sums_ref, bf16[240,8192]{1,0:T(8,128)(2,1)S(1)} %get-tuple-element.25.parts_ref), custom_call_target="tpu_custom_call" | custom-call | tf_op jit(solution)/shard_map/finish/pallas_call | solution.py:384
Async XLA Ops:
  1.8 18.1 %collective-permute-start = (f32[17,2,2,8,128]{4,3,2,1,0:T(8,128)S(1)}, f32[17,2,2,8,128]{4,3,2,1,0:T(8,128)S(1)}, u32[]{:S(2)}, u32[]{:S(2)}) collective-permute-start(f32[17,2,2,8,128]{4,3,2,1,0:T(8,128)S(1)} %get-tuple-element.18), channel_id=1, source_target_pairs={{0,32},{32,64},{64,96},{96,128},{128,160},{160,192},{192,224},{224... | collective-permute-start | bytes 835592 | tf_op jit(solution)/shard_map/ppermute | solution.py:414
  6.4 14.6 %collective-permute-start.1 = (f32[16,4,8,128]{3,2,1,0:T(8,128)S(1)}, f32[16,4,8,128]{3,2,1,0:T(8,128)S(1)}, u32[]{:S(2)}, u32[]{:S(2)}) collective-permute-start(f32[16,4,8,128]{3,2,1,0:T(8,128)S(1)} %get-tuple-element.19), channel_id=1, source_target_pairs={{0,1},{1,0},{2,3},{3,2},{4,5},{5,4},{6,7},{7,6},{8,9},{9,8},{10,11... | collective-permute-start | bytes 786440 | tf_op jit(solution)/shard_map/ppermute | solution.py:412
  7.1 13.9 %collective-permute-start.2 = (f32[16,4,8,128]{3,2,1,0:T(8,128)S(1)}, f32[16,4,8,128]{3,2,1,0:T(8,128)S(1)}, u32[]{:S(2)}, u32[]{:S(2)}) collective-permute-start(f32[16,4,8,128]{3,2,1,0:T(8,128)S(1)} %get-tuple-element.20), channel_id=1, source_target_pairs={{1,2},{2,1},{3,4},{4,3},{5,6},{6,5},{7,8},{8,7},{9,10},{10,9},{11,... | collective-permute-start | bytes 786440 | tf_op jit(solution)/shard_map/ppermute | solution.py:413
  17.9 3.1 %collective-permute-start.3 = (f32[16,128]{1,0:T(8,128)S(1)}, f32[16,128]{1,0:T(8,128)S(1)}, u32[]{:S(2)}, u32[]{:S(2)}) collective-permute-start(f32[16,128]{1,0:T(8,128)S(1)} %get-tuple-element.22), channel_id=1, source_target_pairs={{0,32},{32,0},{1,33},{33,1},{2,34},{34,2},{3,35},{35,3},{4,36},{36... | collective-permute-start | bytes 24584 | tf_op jit(solution)/shard_map/ppermute | solution.py:416

commit v10 on v9

--- a/solution.py
+++ b/solution.py
@@ -19,6 +19,7 @@
 PLACES = STEPS * PLANES * LINES
 CELLS = PLACES * 128
 SIDE = 2 * PLANES * LINES
+SPARE = 2
 TOTAL = 64 * 64 * 8 * 128
 PARTS = 3
 HIGHEST = lax.Precision.HIGHEST
@@ -49,6 +50,12 @@
     return (step * PLANES + plane) * LINES + line
 
 
+def step_weights(size, before):
+    ratio = size / before
+    one = 1.0 + ratio
+    return (1.0 + 2.0 * ratio) / one, one, ratio * ratio / one
+
+
 def split(value):
     first = value.astype(BF16)
     rest = value - first.astype(F32)
@@ -61,14 +68,15 @@
     num_hbm, den_hbm, basis_hbm, first_ref, second_ref, late_ref, sizes_ref, num_ref, den_ref, sems
 ):
     last = BLOCKS - 1
+    own = pl.ds(0, COLS)
     flip = (lax.axis_index("z") + lax.axis_index("core")) % 2
     counts = [
         pltpu.make_async_copy(num_hbm, num_ref, sems.at[3]),
         pltpu.make_async_copy(den_hbm, den_ref, sems.at[4]),
     ]
     copies = [
-        pltpu.make_async_copy(basis_hbm.at[last, :, :, 1 - flip], first_ref, sems.at[0]),
-        pltpu.make_async_copy(basis_hbm.at[last, :, :, flip], second_ref, sems.at[1]),
+        pltpu.make_async_copy(basis_hbm.at[last, :, :, 1 - flip], first_ref.at[own], sems.at[0]),
+        pltpu.make_async_copy(basis_hbm.at[last, :, :, flip], second_ref.at[own], sems.at[1]),
         pltpu.make_async_copy(
             basis_hbm.at[last, :, pl.ds(STEPS - 2, 2)], late_ref.at[pl.ds(0, COLS)], sems.at[2]
         ),
@@ -89,7 +97,7 @@
 
 
 def edges(num, den, basis):
-    face = jax.ShapeDtypeStruct((COLS, STEPS, LINES, 128), F32)
+    face = jax.ShapeDtypeStruct((COLS + SPARE, STEPS, LINES, 128), F32)
     return pl.pallas_call(
         edges_kernel,
         out_shape=(
@@ -173,82 +181,82 @@
     )(in_hbm(basis))
 
 
-def inner_kernel(sizes_ref, field_ref, late_ref, inner_ref):
+def inner_kernel(sizes_ref, field_ref, first_ref, second_ref, inner_ref):
     sizes = [sizes_ref[step] for step in range(STEPS)]
-    first = (lax.axis_index("y") == 0) & (lax.axis_index("core") == 0)
-    start = jnp.full((COLS, 128), first.astype(jnp.int32)) == 1
-    weights = []
+    flip = (lax.axis_index("z") + lax.axis_index("core")) % 2
+    flipped = jnp.full((COLS, 128), flip) == 1
+    lane = lax.broadcasted_iota(jnp.int32, (COLS, 128), 1)
+
+    def at(step, plane, line):
+        return field_ref[place_of(step, plane, line)]
+
     for step in range(STEPS):
-        if step == 0:
-            before = late_ref[pl.ds(COLS * SIDE, LINES), :]
-            before = jnp.where(start, sizes[0], jnp.concatenate([before, before], axis=0))
-        else:
-            before = sizes[step - 1]
-        ratio = sizes[step] / before
-        now = (1.0 + 2.0 * ratio) / (1.0 + ratio)
-        one = 1.0 + ratio
-        two = ratio * ratio / (1.0 + ratio)
-        if step == 0:
-            now = jnp.where(start, 1.0, now)
-            one = jnp.where(start, 1.0, one)
-            two = jnp.where(start, 0.0, two)
-        weights.append((now, one, two, 0.5 * sizes[step]))
-    lane = lax.broadcasted_iota(jnp.int32, (COLS, 128), 1)
-
-    past = [late_ref[pl.ds(place, COLS, stride=SIDE), :] for place in range(SIDE)]
-
-    def at(step, plane, line):
-        if step < 0:
-            return past[place_of(step + 2, plane, line)]
-        return field_ref[place_of(step, plane, line)]
-
-    for step in range(STEPS):
-        now, one, two, kappa = weights[step]
-        for plane in range(PLANES):
-            for line in range(LINES):
+        kappa = 0.5 * sizes[step]
+        if step > 0:
+            now, one, two = step_weights(sizes[step], sizes[step - 1])
+        for line in range(LINES):
+            side = pl.ds(step * LINES + line, COLS, stride=STEPS * LINES)
+            near = first_ref[side, :]
+            far = second_ref[side, :]
+            for plane, halo in ((0, jnp.where(flipped, near, far)), (1, jnp.where(flipped, far, near))):
                 value = at(step, plane, line)
-                beside = at(step, PLANES - 1 - plane, line)
+                beside = halo + at(step, PLANES - 1 - plane, line)
                 if line > 0:
                     beside += at(step, plane, line - 1)
                 if line < LINES - 1:
                     beside += at(step, plane, line + 1)
                 beside += jnp.where(lane < 127, pltpu.roll(value, 127, 1), 0.0)
                 beside += jnp.where(lane > 0, pltpu.roll(value, 1, 1), 0.0)
-                result = (
-                    now * value
-                    - one * at(step - 1, plane, line)
-                    + two * at(step - 2, plane, line)
-                    + kappa * (6.0 * value - beside)
-                )
+                result = kappa * (6.0 * value - beside)
+                if step > 0:
+                    result += now * value - one * at(step - 1, plane, line)
+                if step > 1:
+                    result += two * at(step - 2, plane, line)
                 inner_ref[place_of(step, plane, line)] = result
 
 
-def inner(sizes, field, late):
+def inner(sizes, field, near, far):
     return pl.pallas_call(
         inner_kernel,
         out_shape=jax.ShapeDtypeStruct((PLACES, COLS, 128), F32),
-        in_specs=[VMEM] * 3,
+        in_specs=[VMEM] * 4,
         out_specs=VMEM,
         compiler_params=params(8),
         name="inner",
-    )(sizes, field, late)
+    )(sizes, field, near, far)
 
 
 def image_kernel(
-    sizes_ref, inner_ref, first_ref, second_ref, keep_ref, got_ref, parts_in_ref, parts_ref, copies_ref
+    sizes_ref, field_ref, inner_ref, late_ref, keep_ref, got_ref, parts_in_ref, parts_ref, copies_ref
 ):
     base = PARTS * ROWS
-    flip = (lax.axis_index("z") + lax.axis_index("core")) % 2
-    flipped = jnp.full((COLS, 128), flip) == 1
+    first = (lax.axis_index("y") == 0) & (lax.axis_index("core") == 0)
+    start = jnp.full((COLS, 128), first.astype(jnp.int32)) == 1
+    before = late_ref[pl.ds(COLS * SIDE, LINES), :]
+    before = jnp.where(start, sizes_ref[0], jnp.concatenate([before, before], axis=0))
+    now, one, two = step_weights(sizes_ref[0], before)
+    now = jnp.where(start, 1.0, now)
+    one = jnp.where(start, 1.0, one)
+    two = jnp.where(start, 0.0, two)
+    next_two = step_weights(sizes_ref[1], sizes_ref[0])[2]
+
+    def late(step, plane, line):
+        return late_ref[pl.ds(place_of(step, plane, line), COLS, stride=SIDE), :]
+
     for step in range(STEPS):
-        kappa = 0.5 * sizes_ref[step]
-        for line in range(LINES):
-            side = pl.ds(step * LINES + line, COLS, stride=STEPS * LINES)
-            one = first_ref[side, :]
-            two = second_ref[side, :]
-            for plane, halo in ((0, jnp.where(flipped, one, two)), (1, jnp.where(flipped, two, one))):
+        for plane in range(PLANES):
+            for line in range(LINES):
                 place = place_of(step, plane, line)
-                for part, piece in enumerate(split(inner_ref[place] - kappa * halo)):
+                result = inner_ref[place]
+                if step == 0:
+                    result += (
+                        now * field_ref[place]
+                        - one * late(1, plane, line)
+                        + two * late(0, plane, line)
+                    )
+                if step == 1:
+                    result += next_two * late(1, plane, line)
+                for part, piece in enumerate(split(result)):
                     parts_ref[
                         base + part * COLS : base + (part + 1) * COLS, place * 128 : (place + 1) * 128
                     ] = piece
@@ -271,7 +279,7 @@
         copies_ref[copy, 4] = last
 
 
-def image_products(sizes, inside, one, two, keep, got, parts):
+def image_products(sizes, field, inside, late, keep, got, parts):
     return pl.pallas_call(
         image_kernel,
         out_shape=(
@@ -283,7 +291,7 @@
         input_output_aliases={6: 0},
         compiler_params=params(20),
         name="image_products",
-    )(sizes, inside, one, two, keep, got, parts)
+    )(sizes, field, inside, late, keep, got, parts)
 
 
 def regroup_kernel(sums_ref, copies_ref):
@@ -414,8 +422,8 @@
     late = lax.ppermute(late, TM, later).reshape(-1, 128)
     parts, field, keep, give = basis_products(flat)
     got = lax.ppermute(give, "core", [(0, 1), (1, 0)])
-    inside = inner(sizes, field, late)
-    parts, copies = image_products(sizes, inside, near, far, keep, got, parts)
+    inside = inner(sizes, field, near, far)
+    parts, copies = image_products(sizes, field, inside, late, keep, got, parts)
     sums = exchanged(regroup(exchanged(copies, SPACE)), TM)
     hess, triangle, following = finish(sums, parts)
     return (

time: 66.1 us -> 66.7 us (level)
  blocking collectives: 40.7 us -> 43 us
  starting transfers between devices: 14.5 us -> 13.2 us
    ppermute x1, starting transfers between devices: 4.59 us -> 1.92 us  [per_device(): late = lax.ppermute(late, TM, later).reshape(-1, 128)]
    all_to_all x2, blocking collectives: 40.7 us -> 43 us  [exchanged(): return lax.all_to_all(copies, axes, 0, 0)]
    ppermute x1, starting transfers between devices: 7.32 us -> 8.15 us  [per_device(): far = lax.ppermute(far, ('core',) + SPACE, second).reshape(-1, 128)]
where the time goes in v10:
time: 66.7 us; the launch traced here: 66.3 us
  blocking collectives  43 us (64%)
  starting transfers between devices  13.2 us (20%)
  Pallas kernels  9.29 us (14%)
  between operations  0.71 us (1%)
    all_to_all x2, blocking collectives, exchanged(): return lax.all_to_all(copies, axes, 0, 0)  43 us
    ppermute x1, starting transfers between devices, per_device(): far = lax.ppermute(far, ('core',) + SPACE, second).reshape(-1, 128)  8.15 us
    pallas_call x1, Pallas kernels, basis_products(): pl.pallas_call(basis_kernel, out_shape=(jax.ShapeDtypeStruct((PARTS * FUL...  3.49 us
    ppermute x1, starting transfers between devices, per_device(): got = lax.ppermute(give, 'core', [(0, 1), (1, 0)])  2.42 us
    pallas_call x1, Pallas kernels, finish(): pl.pallas_call(finish_kernel, out_shape=(jax.ShapeDtypeStruct((ROWS, COLS...  2.35 us
    ppermute x1, starting transfers between devices, per_device(): late = lax.ppermute(late, TM, later).reshape(-1, 128)  1.92 us
    pallas_call x1, Pallas kernels, image_products(): pl.pallas_call(image_kernel, out_shape=(jax.ShapeDtypeStruct((PARTS * FUL...  1.56 us
  transfers between devices with their start and end apart: 4, of which 1 were waited for; matrix products, arithmetic and copies ran while one was open for 0% of the time, Pallas kernels for 6%

profile of v10, /device:TPU:1, one launch (start us, length us, event | category | flops | bytes accessed | tf_op | source)
XLA Modules:
  0.0 66.3 jit_solution(13317933505653305655)
XLA Ops:
  0.6 1.2 %edges.1 = (f32[18,4,8,128]{3,2,1,0:T(8,128)S(1)}, f32[18,4,8,128]{3,2,1,0:T(8,128)S(1)}, f32[17,2,2,8,128]{4,3,2,1,0:T(8,128)S(1)}, f32[4,16,128]{2,1,0:T(8,128)S(1)}) custom-call(s32[4]{0:T(128)} %num_hbm.1, s32[4]{0:T(128)} %den_hbm.1, f32[4,16,4,2,8,128]{5,4,3,2,1,0:T(8,128)} %basis_hbm.1), custom_call_target="tpu_custom_call" | custom-call | tf_op jit(solution)/shard_map/edges/pallas_call | solution.py:101
  1.8 0.7 %collective-permute-start = (f32[18,4,8,128]{3,2,1,0:T(8,128)S(1)}, f32[18,4,8,128]{3,2,1,0:T(8,128)S(1)}, u32[]{:S(2)}, u32[]{:S(2)}) collective-permute-start(f32[18,4,8,128]{3,2,1,0:T(8,128)S(1)} %get-tuple-element.18), channel_id=1, source_target_pairs={{0,1},{1,0},{2,3},{3,2},{4,5},{5,4},{6,7},{7,6},{8,9},{9,8},{10,11... | collective-permute-start | bytes 884744 | tf_op jit(solution)/shard_map/ppermute | solution.py:420
  2.5 8.2 %collective-permute-start.1 = (f32[18,4,8,128]{3,2,1,0:T(8,128)S(1)}, f32[18,4,8,128]{3,2,1,0:T(8,128)S(1)}, u32[]{:S(2)}, u32[]{:S(2)}) collective-permute-start(f32[18,4,8,128]{3,2,1,0:T(8,128)S(1)} %get-tuple-element.19), channel_id=1, source_target_pairs={{1,2},{2,1},{3,4},{4,3},{5,6},{6,5},{7,8},{8,7},{9,10},{10,9},{11,... | collective-permute-start | bytes 884744 | tf_op jit(solution)/shard_map/ppermute | solution.py:421
  10.7 1.9 %collective-permute-start.2 = (f32[17,2,2,8,128]{4,3,2,1,0:T(8,128)S(1)}, f32[17,2,2,8,128]{4,3,2,1,0:T(8,128)S(1)}, u32[]{:S(2)}, u32[]{:S(2)}) collective-permute-start(f32[17,2,2,8,128]{4,3,2,1,0:T(8,128)S(1)} %get-tuple-element.20), channel_id=1, source_target_pairs={{0,32},{32,64},{64,96},{96,128},{128,160},{160,192},{192,224},{224... | collective-permute-start | bytes 835592 | tf_op jit(solution)/shard_map/ppermute | solution.py:422
  12.6 3.5 %basis_products.1 = (bf16[240,8192]{1,0:T(8,128)(2,1)S(1)}, f32[64,16,128]{2,1,0:T(8,128)S(1)}, f32[16,128]{1,0:T(8,128)S(1)}, f32[16,128]{1,0:T(8,128)S(1)}) custom-call(f32[64,64,1,128]{3,2,1,0:T(1,128)} %bitcast.9), custom_call_target="tpu_custom_call" | custom-call | tf_op jit(solution)/shard_map/basis_products/pallas_call | solution.py:165
  16.1 2.4 %collective-permute-start.3 = (f32[16,128]{1,0:T(8,128)S(1)}, f32[16,128]{1,0:T(8,128)S(1)}, u32[]{:S(2)}, u32[]{:S(2)}) collective-permute-start(f32[16,128]{1,0:T(8,128)S(1)} %get-tuple-element.22), channel_id=1, source_target_pairs={{0,32},{32,0},{1,33},{33,1},{2,34},{34,2},{3,35},{35,3},{4,36},{36... | collective-permute-start | bytes 24584 | tf_op jit(solution)/shard_map/ppermute | solution.py:424
  18.5 0.0 collective-permute-done
  18.5 0.0 collective-permute-done.1
  18.5 0.7 inner.1.inner_ref
  19.2 0.1 collective-permute-done.3.got_ref
  19.3 0.0 collective-permute-done.2
  19.3 1.6 %image_products.1 = (bf16[240,8192]{1,0:T(8,128)(2,1)S(1)}, f32[32,5,4,128]{3,2,1,0:T(4,128)S(1)}) custom-call(f32[4,16,128]{2,1,0:T(8,128)S(1)} %get-tuple-element.16.sizes_ref, f32[64,16,128]{2,1,0:T(8,128)S(1)} %get-tuple-element.17.field_ref, f32[64,16,128]{2,1,0:T(8,128)S(1)} %inner.1.inner_ref, ...), custom_call_target="tpu_custom_call", output_to_operand_aliasing={{0}: (6, {})} | custom-call | tf_op jit(solution)/shard_map/image_products/pallas_call | solution.py:283
  20.9 23.9 %all_to_all.10.sums_ref = f32[32,5,4,128]{3,2,1,0:T(4,128)S(1)} all-to-all(f32[32,5,4,128]{3,2,1,0:T(4,128)S(1)} %get-tuple-element.24), channel_id=1, replica_groups=mesh['y'=8,'core'=2,'x'=4,'z'=8] {'x','z'}, dimensions={0} | all-to-all | bytes 655360 | tf_op jit(solution)/shard_map/all_to_all | solution.py:407
  44.7 0.1 regroup.1
  44.8 19.1 %all_to_all.11.sums_ref = f32[16,5,4,128]{3,2,1,0:T(4,128)S(1)} all-to-all(f32[16,5,4,128]{3,2,1,0:T(4,128)S(1)} %regroup.1), channel_id=1, replica_groups=mesh['y'=8,'core'=2,'x'=4,'z'=8] {'y','core'}, dimensions={0} | all-to-all | bytes 327680 | tf_op jit(solution)/shard_map/all_to_all | solution.py:407
  63.9 2.4 %finish.1 = (f32[64,16]{1,0:T(8,128)}, f32[16,16]{1,0:T(8,128)}, f32[1024,128]{1,0:T(8,128)}) custom-call(f32[16,5,4,128]{3,2,1,0:T(4,128)S(1)} %all_to_all.11.sums_ref, bf16[240,8192]{1,0:T(8,128)(2,1)S(1)} %get-tuple-element.25.parts_ref), custom_call_target="tpu_custom_call" | custom-call | tf_op jit(solution)/shard_map/finish/pallas_call | solution.py:392
Async XLA Ops:
  1.8 16.7 %collective-permute-start = (f32[18,4,8,128]{3,2,1,0:T(8,128)S(1)}, f32[18,4,8,128]{3,2,1,0:T(8,128)S(1)}, u32[]{:S(2)}, u32[]{:S(2)}) collective-permute-start(f32[18,4,8,128]{3,2,1,0:T(8,128)S(1)} %get-tuple-element.18), channel_id=1, source_target_pairs={{0,1},{1,0},{2,3},{3,2},{4,5},{5,4},{6,7},{7,6},{8,9},{9,8},{10,11... | collective-permute-start | bytes 884744 | tf_op jit(solution)/shard_map/ppermute | solution.py:420
  2.5 16.0 %collective-permute-start.1 = (f32[18,4,8,128]{3,2,1,0:T(8,128)S(1)}, f32[18,4,8,128]{3,2,1,0:T(8,128)S(1)}, u32[]{:S(2)}, u32[]{:S(2)}) collective-permute-start(f32[18,4,8,128]{3,2,1,0:T(8,128)S(1)} %get-tuple-element.19), channel_id=1, source_target_pairs={{1,2},{2,1},{3,4},{4,3},{5,6},{6,5},{7,8},{8,7},{9,10},{10,9},{11,... | collective-permute-start | bytes 884744 | tf_op jit(solution)/shard_map/ppermute | solution.py:421
  10.7 8.7 %collective-permute-start.2 = (f32[17,2,2,8,128]{4,3,2,1,0:T(8,128)S(1)}, f32[17,2,2,8,128]{4,3,2,1,0:T(8,128)S(1)}, u32[]{:S(2)}, u32[]{:S(2)}) collective-permute-start(f32[17,2,2,8,128]{4,3,2,1,0:T(8,128)S(1)} %get-tuple-element.20), channel_id=1, source_target_pairs={{0,32},{32,64},{64,96},{96,128},{128,160},{160,192},{192,224},{224... | collective-permute-start | bytes 835592 | tf_op jit(solution)/shard_map/ppermute | solution.py:422
  16.1 3.2 %collective-permute-start.3 = (f32[16,128]{1,0:T(8,128)S(1)}, f32[16,128]{1,0:T(8,128)S(1)}, u32[]{:S(2)}, u32[]{:S(2)}) collective-permute-start(f32[16,128]{1,0:T(8,128)S(1)} %get-tuple-element.22), channel_id=1, source_target_pairs={{0,32},{32,0},{1,33},{33,1},{2,34},{34,2},{3,35},{35,3},{4,36},{36... | collective-permute-start | bytes 24584 | tf_op jit(solution)/shard_map/ppermute | solution.py:424

commit v11 on v8

--- a/solution.py
+++ b/solution.py
@@ -58,17 +58,17 @@
 
 
 def edges_kernel(
-    num_hbm, den_hbm, basis_hbm, near_ref, far_ref, late_ref, sizes_ref, num_ref, den_ref, sems
+    num_hbm, den_hbm, basis_hbm, first_ref, second_ref, late_ref, sizes_ref, num_ref, den_ref, sems
 ):
     last = BLOCKS - 1
-    odd = lax.axis_index("z") % 2
+    flip = (lax.axis_index("z") + lax.axis_index("core")) % 2
     counts = [
         pltpu.make_async_copy(num_hbm, num_ref, sems.at[3]),
         pltpu.make_async_copy(den_hbm, den_ref, sems.at[4]),
     ]
     copies = [
-        pltpu.make_async_copy(basis_hbm.at[last, :, :, 1 - odd], near_ref, sems.at[0]),
-        pltpu.make_async_copy(basis_hbm.at[last, :, :, odd], far_ref, sems.at[1]),
+        pltpu.make_async_copy(basis_hbm.at[last, :, :, 1 - flip], first_ref, sems.at[0]),
+        pltpu.make_async_copy(basis_hbm.at[last, :, :, flip], second_ref, sems.at[1]),
         pltpu.make_async_copy(
             basis_hbm.at[last, :, STEPS - 1], late_ref.at[pl.ds(0, COLS)], sems.at[2]
         ),
@@ -174,9 +174,10 @@
     )(in_hbm(basis))
 
 
-def inner_kernel(sizes_ref, field_ref, late_ref, near_ref, far_ref, inner_ref, weight_ref):
+def inner_kernel(sizes_ref, field_ref, late_ref, first_ref, second_ref, inner_ref, weight_ref):
     sizes = [sizes_ref[step] for step in range(STEPS)]
-    odd = jnp.full((COLS, 128), lax.axis_index("z") % 2) == 1
+    flip = (lax.axis_index("z") + lax.axis_index("core")) % 2
+    flipped = jnp.full((COLS, 128), flip) == 1
     first = (lax.axis_index("y") == 0) & (lax.axis_index("core") == 0)
     start = jnp.full((COLS, 128), first.astype(jnp.int32)) == 1
     lane = lax.broadcasted_iota(jnp.int32, (COLS, 128), 1)
@@ -203,9 +204,9 @@
             weight_ref[...] = jnp.where(start, 0.0, two)
         for line in range(LINES):
             side = pl.ds(step * LINES + line, COLS, stride=STEPS * LINES)
-            near = near_ref[side, :]
-            far = far_ref[side, :]
-            for plane, halo in ((0, jnp.where(odd, near, far)), (1, jnp.where(odd, far, near))):
+            near = first_ref[side, :]
+            far = second_ref[side, :]
+            for plane, halo in ((0, jnp.where(flipped, near, far)), (1, jnp.where(flipped, far, near))):
                 value = at(step, plane, line)
                 beside = halo + at(step, PLANES - 1 - plane, line)
                 if line > 0:
@@ -400,11 +401,13 @@
     groups = size_of(TM)
     pairs = [(i, i ^ 1) for i in range(slabs)]
     others = [(i, ((i + 1) ^ 1) - 1) for i in range(1, slabs - 1)]
+    first = pairs + [(i + slabs, j + slabs) for i, j in others]
+    second = others + [(i + slabs, j + slabs) for i, j in pairs]
     later = [(i, i + 1) for i in range(groups - 1)]
     flat = basis.reshape(ROWS, PLACES, 1, 128)
     near, far, late, sizes = edges(num, den, basis)
-    near = lax.ppermute(near, SPACE, pairs).reshape(-1, 128)
-    far = lax.ppermute(far, SPACE, others).reshape(-1, 128)
+    near = lax.ppermute(near, ("core",) + SPACE, first).reshape(-1, 128)
+    far = lax.ppermute(far, ("core",) + SPACE, second).reshape(-1, 128)
     late = lax.ppermute(late, TM, later).reshape(-1, 128)
     parts, field, keep, give = basis_products(flat)
     got = lax.ppermute(give, TM, later + [(groups - 1, 0)])

time: 66.3 us -> 66.3 us (level)
  starting transfers between devices: 9.58 us -> 12.4 us
  blocking collectives: 45 us -> 42.2 us
    ppermute x2, starting transfers between devices: 5.51 us -> 8.83 us  [the longest x1 8.15 us: per_device(): far = lax.ppermute(far, ('core',) + SPACE, second).reshape(-1, 128)]
    all_to_all x2, blocking collectives: 45 us -> 42.2 us  [exchanged(): return lax.all_to_all(copies, axes, 0, 0)]
    ppermute x1, starting transfers between devices: 4.05 us -> 1.92 us  [per_device(): late = lax.ppermute(late, TM, later).reshape(-1, 128)]
    ppermute x1, starting transfers between devices: 0.02 us -> 1.69 us  [per_device(): got = lax.ppermute(give, TM, later + [(groups - 1, 0)])]
where the time goes in v11:
time: 66.3 us; the launch traced here: 65.9 us
  blocking collectives  42.2 us (64%)
  starting transfers between devices  12.4 us (19%)
  Pallas kernels  9.22 us (14%)
  waiting for transfers between devices  1.33 us (2%)
  between operations  0.69 us (1%)
    all_to_all x2, blocking collectives, exchanged(): return lax.all_to_all(copies, axes, 0, 0)  42.2 us
    ppermute x1, starting transfers between devices, per_device(): far = lax.ppermute(far, ('core',) + SPACE, second).reshape(-1, 128)  8.15 us
    pallas_call x1, Pallas kernels, basis_products(): pl.pallas_call(basis_kernel, out_shape=(jax.ShapeDtypeStruct((PARTS * FUL...  3.5 us
    pallas_call x1, Pallas kernels, finish(): pl.pallas_call(finish_kernel, out_shape=(jax.ShapeDtypeStruct((ROWS, COLS...  2.37 us
    ppermute x1, starting transfers between devices, per_device(): late = lax.ppermute(late, TM, later).reshape(-1, 128)  1.92 us
    ppermute x1, starting transfers between devices, per_device(): got = lax.ppermute(give, TM, later + [(groups - 1, 0)])  1.69 us
    pallas_call x1, Pallas kernels, image_products(): pl.pallas_call(image_kernel, out_shape=(jax.ShapeDtypeStruct((PARTS * FUL...  1.49 us
    ppermute x1, waiting for transfers between devices, per_device(): got = lax.ppermute(give, TM, later + [(groups - 1, 0)])  1.33 us
  transfers between devices with their start and end apart: 4, of which 1 were waited for; matrix products, arithmetic and copies ran while one was open for 0% of the time, Pallas kernels for 6%

profile of v11, /device:TPU:1, one launch (start us, length us, event | category | flops | bytes accessed | tf_op | source)
XLA Modules:
  0.0 65.9 jit_solution(8090451628703329116)
XLA Ops:
  0.6 1.1 %edges.1 = (f32[16,4,8,128]{3,2,1,0:T(8,128)S(1)}, f32[16,4,8,128]{3,2,1,0:T(8,128)S(1)}, f32[17,2,8,128]{3,2,1,0:T(8,128)S(1)}, f32[4,16,128]{2,1,0:T(8,128)S(1)}) custom-call(s32[4]{0:T(128)} %num_hbm.1, s32[4]{0:T(128)} %den_hbm.1, f32[4,16,4,2,8,128]{5,4,3,2,1,0:T(8,128)} %basis_hbm.1), custom_call_target="tpu_custom_call" | custom-call | tf_op jit(solution)/shard_map/edges/pallas_call | solution.py:92
  1.8 0.7 %collective-permute-start.1 = (f32[16,4,8,128]{3,2,1,0:T(8,128)S(1)}, f32[16,4,8,128]{3,2,1,0:T(8,128)S(1)}, u32[]{:S(2)}, u32[]{:S(2)}) collective-permute-start(f32[16,4,8,128]{3,2,1,0:T(8,128)S(1)} %get-tuple-element.21), channel_id=1, source_target_pairs={{0,1},{1,0},{2,3},{3,2},{4,5},{5,4},{6,7},{7,6},{8,9},{9,8},{10,11... | collective-permute-start | bytes 786440 | tf_op jit(solution)/shard_map/ppermute | solution.py:409
  2.4 8.2 %collective-permute-start.2 = (f32[16,4,8,128]{3,2,1,0:T(8,128)S(1)}, f32[16,4,8,128]{3,2,1,0:T(8,128)S(1)}, u32[]{:S(2)}, u32[]{:S(2)}) collective-permute-start(f32[16,4,8,128]{3,2,1,0:T(8,128)S(1)} %get-tuple-element.22), channel_id=1, source_target_pairs={{1,2},{2,1},{3,4},{4,3},{5,6},{6,5},{7,8},{8,7},{9,10},{10,9},{11,... | collective-permute-start | bytes 786440 | tf_op jit(solution)/shard_map/ppermute | solution.py:410
  10.6 1.9 %collective-permute-start = (f32[17,2,8,128]{3,2,1,0:T(8,128)S(1)}, f32[17,2,8,128]{3,2,1,0:T(8,128)S(1)}, u32[]{:S(2)}, u32[]{:S(2)}) collective-permute-start(f32[17,2,8,128]{3,2,1,0:T(8,128)S(1)} %get-tuple-element.20), channel_id=1, source_target_pairs={{0,32},{32,64},{64,96},{96,128},{128,160},{160,192},{192,224},{224... | collective-permute-start | bytes 417800 | tf_op jit(solution)/shard_map/ppermute | solution.py:411
  12.5 3.5 %basis_products.1 = (bf16[240,8192]{1,0:T(8,128)(2,1)S(1)}, f32[64,16,128]{2,1,0:T(8,128)S(1)}, f32[16,128]{1,0:T(8,128)S(1)}, f32[17,16,128]{2,1,0:T(8,128)S(1)}) custom-call(f32[64,64,1,128]{3,2,1,0:T(1,128)} %bitcast.9), custom_call_target="tpu_custom_call" | custom-call | tf_op jit(solution)/shard_map/basis_products/pallas_call | solution.py:158
  16.0 1.7 %collective-permute-start.3 = (f32[17,16,128]{2,1,0:T(8,128)S(1)}, f32[17,16,128]{2,1,0:T(8,128)S(1)}, u32[]{:S(2)}, u32[]{:S(2)}) collective-permute-start(f32[17,16,128]{2,1,0:T(8,128)S(1)} %get-tuple-element.26), channel_id=1, source_target_pairs={{0,32},{32,64},{64,96},{96,128},{128,160},{160,192},{192,224},{224... | collective-permute-start | bytes 417800 | tf_op jit(solution)/shard_map/ppermute | solution.py:413
  17.7 0.0 collective-permute-done
  17.7 0.0 collective-permute-done.1
  17.7 0.0 collective-permute-done.2
  17.7 0.7 %inner.1 = (f32[64,16,128]{2,1,0:T(8,128)S(1)}, f32[16,128]{1,0:T(8,128)S(1)}) custom-call(f32[4,16,128]{2,1,0:T(8,128)S(1)} %get-tuple-element.18.sizes_ref, f32[64,16,128]{2,1,0:T(8,128)S(1)} %get-tuple-element.19.field_ref, f32[272,128]{1,0:T(8,128)S(1)} %bitcast.8, f32[512,128]{1,0:T(8,128)S(1)} %bitcast.6, f32[512,128]{1,0:T(8,128)S(1)} %bitcast.7), custom_call_target="tpu_custom_call" | custom-call | tf_op jit(solution)/shard_map/inner/pallas_call | solution.py:226
  18.4 1.3 %collective-permute-done.3.got_ref = f32[17,16,128]{2,1,0:T(8,128)S(1)} collective-permute-done((f32[17,16,128]{2,1,0:T(8,128)S(1)}, f32[17,16,128]{2,1,0:T(8,128)S(1)}, u32[]{:S(2)}, u32[]{:S(2)}) %collective-permute-start.3) | collective-permute-done | bytes 139296 | tf_op jit(solution)/shard_map/ppermute | solution.py:413
  19.8 1.5 %image_products.1 = (bf16[240,8192]{1,0:T(8,128)(2,1)S(1)}, f32[32,5,4,128]{3,2,1,0:T(4,128)S(1)}) custom-call(f32[16,128]{1,0:T(8,128)S(1)} %get-tuple-element.23.weight_ref, f32[64,16,128]{2,1,0:T(8,128)S(1)} %get-tuple-element.24.inner_ref, f32[16,128]{1,0:T(8,128)S(1)} %get-tuple-element.25.keep_ref, ...), custom_call_target="tpu_custom_call", output_to_operand_aliasing={{0}: (4, {})} | custom-call | tf_op jit(solution)/shard_map/image_products/pallas_call | solution.py:272
  21.3 21.6 %all_to_all.10.sums_ref = f32[32,5,4,128]{3,2,1,0:T(4,128)S(1)} all-to-all(f32[32,5,4,128]{3,2,1,0:T(4,128)S(1)} %get-tuple-element.28), channel_id=1, replica_groups=mesh['y'=8,'core'=2,'x'=4,'z'=8] {'x','z'}, dimensions={0} | all-to-all | bytes 655360 | tf_op jit(solution)/shard_map/all_to_all | solution.py:396
  42.8 0.1 regroup.1
  42.9 20.6 %all_to_all.11.sums_ref = f32[16,5,4,128]{3,2,1,0:T(4,128)S(1)} all-to-all(f32[16,5,4,128]{3,2,1,0:T(4,128)S(1)} %regroup.1), channel_id=1, replica_groups=mesh['y'=8,'core'=2,'x'=4,'z'=8] {'y','core'}, dimensions={0} | all-to-all | bytes 327680 | tf_op jit(solution)/shard_map/all_to_all | solution.py:396
  63.5 2.4 %finish.1 = (f32[64,16]{1,0:T(8,128)}, f32[16,16]{1,0:T(8,128)}, f32[1024,128]{1,0:T(8,128)}) custom-call(f32[16,5,4,128]{3,2,1,0:T(4,128)S(1)} %all_to_all.11.sums_ref, bf16[240,8192]{1,0:T(8,128)(2,1)S(1)} %get-tuple-element.29.parts_ref), custom_call_target="tpu_custom_call" | custom-call | tf_op jit(solution)/shard_map/finish/pallas_call | solution.py:381
Async XLA Ops:
  1.8 16.0 %collective-permute-start.1 = (f32[16,4,8,128]{3,2,1,0:T(8,128)S(1)}, f32[16,4,8,128]{3,2,1,0:T(8,128)S(1)}, u32[]{:S(2)}, u32[]{:S(2)}) collective-permute-start(f32[16,4,8,128]{3,2,1,0:T(8,128)S(1)} %get-tuple-element.21), channel_id=1, source_target_pairs={{0,1},{1,0},{2,3},{3,2},{4,5},{5,4},{6,7},{7,6},{8,9},{9,8},{10,11... | collective-permute-start | bytes 786440 | tf_op jit(solution)/shard_map/ppermute | solution.py:409
  2.4 15.3 %collective-permute-start.2 = (f32[16,4,8,128]{3,2,1,0:T(8,128)S(1)}, f32[16,4,8,128]{3,2,1,0:T(8,128)S(1)}, u32[]{:S(2)}, u32[]{:S(2)}) collective-permute-start(f32[16,4,8,128]{3,2,1,0:T(8,128)S(1)} %get-tuple-element.22), channel_id=1, source_target_pairs={{1,2},{2,1},{3,4},{4,3},{5,6},{6,5},{7,8},{8,7},{9,10},{10,9},{11,... | collective-permute-start | bytes 786440 | tf_op jit(solution)/shard_map/ppermute | solution.py:410
  10.6 7.1 %collective-permute-start = (f32[17,2,8,128]{3,2,1,0:T(8,128)S(1)}, f32[17,2,8,128]{3,2,1,0:T(8,128)S(1)}, u32[]{:S(2)}, u32[]{:S(2)}) collective-permute-start(f32[17,2,8,128]{3,2,1,0:T(8,128)S(1)} %get-tuple-element.20), channel_id=1, source_target_pairs={{0,32},{32,64},{64,96},{96,128},{128,160},{160,192},{192,224},{224... | collective-permute-start | bytes 417800 | tf_op jit(solution)/shard_map/ppermute | solution.py:411
  16.0 3.7 %collective-permute-start.3 = (f32[17,16,128]{2,1,0:T(8,128)S(1)}, f32[17,16,128]{2,1,0:T(8,128)S(1)}, u32[]{:S(2)}, u32[]{:S(2)}) collective-permute-start(f32[17,16,128]{2,1,0:T(8,128)S(1)} %get-tuple-element.26), channel_id=1, source_target_pairs={{0,32},{32,64},{64,96},{96,128},{128,160},{160,192},{192,224},{224... | collective-permute-start | bytes 417800 | tf_op jit(solution)/shard_map/ppermute | solution.py:413

commit v12 on v10

--- a/solution.py
+++ b/solution.py
@@ -64,24 +64,19 @@
     return first, second, third
 
 
-def edges_kernel(
-    num_hbm, den_hbm, basis_hbm, first_ref, second_ref, late_ref, sizes_ref, num_ref, den_ref, sems
+def prepare_kernel(
+    num_hbm, den_hbm, basis_hbm, parts_ref, last_ref, sizes_ref, first_ref, second_ref, late_ref,
+    field_ref, num_ref, den_ref, sems, count_sems,
 ):
-    last = BLOCKS - 1
-    own = pl.ds(0, COLS)
-    flip = (lax.axis_index("z") + lax.axis_index("core")) % 2
     counts = [
-        pltpu.make_async_copy(num_hbm, num_ref, sems.at[3]),
-        pltpu.make_async_copy(den_hbm, den_ref, sems.at[4]),
+        pltpu.make_async_copy(num_hbm, num_ref, count_sems.at[0]),
+        pltpu.make_async_copy(den_hbm, den_ref, count_sems.at[1]),
     ]
     copies = [
-        pltpu.make_async_copy(basis_hbm.at[last, :, :, 1 - flip], first_ref.at[own], sems.at[0]),
-        pltpu.make_async_copy(basis_hbm.at[last, :, :, flip], second_ref.at[own], sems.at[1]),
-        pltpu.make_async_copy(
-            basis_hbm.at[last, :, pl.ds(STEPS - 2, 2)], late_ref.at[pl.ds(0, COLS)], sems.at[2]
-        ),
+        pltpu.make_async_copy(basis_hbm.at[:, place, 0], field_ref.at[place], sems.at[place])
+        for place in range(PLACES)
     ]
-    for copy in copies + counts:
+    for copy in counts + copies:
         copy.start()
     for copy in counts:
         copy.wait()
@@ -89,32 +84,48 @@
         top = jnp.full((COLS, 128), num_ref[step]).astype(F32)
         bottom = jnp.full((COLS, 128), den_ref[step]).astype(F32)
         sizes_ref[step] = top / bottom
-    for step in range(2):
-        for plane in range(PLANES):
-            late_ref[COLS, step, plane] = sizes_ref[STEPS - 1, :LINES]
-    for copy in copies:
-        copy.wait()
-
-
-def edges(num, den, basis):
-    face = jax.ShapeDtypeStruct((COLS + SPARE, STEPS, LINES, 128), F32)
-    return pl.pallas_call(
-        edges_kernel,
+    late_ref[SIDE] = sizes_ref[STEPS - 1]
+    flip = (lax.axis_index("z") + lax.axis_index("core")) % 2
+    flipped = jnp.full((COLS, 128), flip) == 1
+    for place in range(PLACES):
+        copies[place].wait()
+        value = field_ref[place]
+        own = value[ROWS - COLS :]
+        last_ref[place] = own
+        if place >= PLACES - SIDE:
+            late_ref[place - (PLACES - SIDE)] = own
+        step, plane, line = place // (PLANES * LINES), place // LINES % PLANES, place % LINES
+        if plane == PLANES - 1:
+            other = last_ref[place_of(step, 0, line)]
+            first_ref[step * LINES + line] = jnp.where(flipped, other, own)
+            second_ref[step * LINES + line] = jnp.where(flipped, own, other)
+        for part, piece in enumerate(split(value)):
+            parts_ref[part * ROWS : (part + 1) * ROWS, place * 128 : (place + 1) * 128] = piece
+
+
+def prepare(num, den, basis):
+    face = jax.ShapeDtypeStruct((STEPS * LINES + SPARE, COLS, 128), F32)
+    return pl.pallas_call(
+        prepare_kernel,
         out_shape=(
+            jax.ShapeDtypeStruct((PARTS * FULL, CELLS), BF16),
+            jax.ShapeDtypeStruct((PLACES, COLS, 128), F32),
+            jax.ShapeDtypeStruct((STEPS, COLS, 128), F32),
             face,
             face,
-            jax.ShapeDtypeStruct((COLS + 1, 2, PLANES, LINES, 128), F32),
-            jax.ShapeDtypeStruct((STEPS, COLS, 128), F32),
+            jax.ShapeDtypeStruct((SIDE + 1, COLS, 128), F32),
         ),
         in_specs=[HBM, HBM, HBM],
-        out_specs=(VMEM, VMEM, VMEM, VMEM),
+        out_specs=(VMEM,) * 6,
         scratch_shapes=[
+            pltpu.VMEM((PLACES, ROWS, 128), F32),
             pltpu.SMEM((STEPS,), jnp.int32),
             pltpu.SMEM((STEPS,), jnp.int32),
-            pltpu.SemaphoreType.DMA((5,)),
+            pltpu.SemaphoreType.DMA((PLACES,)),
+            pltpu.SemaphoreType.DMA((2,)),
         ],
-        compiler_params=params(4),
-        name="edges",
+        compiler_params=params(20),
+        name="prepare",
     )(in_hbm(num), in_hbm(den), in_hbm(basis))
 
 
@@ -129,19 +140,7 @@
     return total
 
 
-def basis_kernel(basis_hbm, parts_ref, last_ref, keep_ref, give_ref, field_ref, sems):
-    copies = [
-        pltpu.make_async_copy(basis_hbm.at[:, place, 0], field_ref.at[place], sems.at[place])
-        for place in range(PLACES)
-    ]
-    for copy in copies:
-        copy.start()
-    for place in range(PLACES):
-        copies[place].wait()
-        value = field_ref[place]
-        last_ref[place] = value[ROWS - COLS :]
-        for part, piece in enumerate(split(value)):
-            parts_ref[part * ROWS : (part + 1) * ROWS, place * 128 : (place + 1) * 128] = piece
+def basis_kernel(parts_ref, keep_ref, give_ref):
     whole = parts_ref[: PARTS * ROWS]
     products = lax.dot_general(whole, whole, NT, preferred_element_type=F32)
     gram = part_products(products, ROWS, 0, ROWS)
@@ -161,24 +160,16 @@
         target[10:16] = jnp.zeros((6, 128), F32)
 
 
-def basis_products(basis):
+def basis_products(parts):
+    half = jax.ShapeDtypeStruct((COLS, 128), F32)
     return pl.pallas_call(
         basis_kernel,
-        out_shape=(
-            jax.ShapeDtypeStruct((PARTS * FULL, CELLS), BF16),
-            jax.ShapeDtypeStruct((PLACES, COLS, 128), F32),
-            jax.ShapeDtypeStruct((16, 128), F32),
-            jax.ShapeDtypeStruct((16, 128), F32),
-        ),
-        in_specs=[HBM],
-        out_specs=(VMEM, VMEM, VMEM, VMEM),
-        scratch_shapes=[
-            pltpu.VMEM((PLACES, ROWS, 128), F32),
-            pltpu.SemaphoreType.DMA((PLACES,)),
-        ],
+        out_shape=(half, half),
+        in_specs=[VMEM],
+        out_specs=(VMEM, VMEM),
         compiler_params=params(20),
         name="basis_products",
-    )(in_hbm(basis))
+    )(parts)
 
 
 def inner_kernel(sizes_ref, field_ref, first_ref, second_ref, inner_ref):
@@ -195,9 +186,8 @@
         if step > 0:
             now, one, two = step_weights(sizes[step], sizes[step - 1])
         for line in range(LINES):
-            side = pl.ds(step * LINES + line, COLS, stride=STEPS * LINES)
-            near = first_ref[side, :]
-            far = second_ref[side, :]
+            near = first_ref[step * LINES + line]
+            far = second_ref[step * LINES + line]
             for plane, halo in ((0, jnp.where(flipped, near, far)), (1, jnp.where(flipped, far, near))):
                 value = at(step, plane, line)
                 beside = halo + at(step, PLANES - 1 - plane, line)
@@ -232,8 +222,7 @@
     base = PARTS * ROWS
     first = (lax.axis_index("y") == 0) & (lax.axis_index("core") == 0)
     start = jnp.full((COLS, 128), first.astype(jnp.int32)) == 1
-    before = late_ref[pl.ds(COLS * SIDE, LINES), :]
-    before = jnp.where(start, sizes_ref[0], jnp.concatenate([before, before], axis=0))
+    before = jnp.where(start, sizes_ref[0], late_ref[SIDE])
     now, one, two = step_weights(sizes_ref[0], before)
     now = jnp.where(start, 1.0, now)
     one = jnp.where(start, 1.0, one)
@@ -241,7 +230,7 @@
     next_two = step_weights(sizes_ref[1], sizes_ref[0])[2]
 
     def late(step, plane, line):
-        return late_ref[pl.ds(place_of(step, plane, line), COLS, stride=SIDE), :]
+        return late_ref[place_of(step, plane, line)]
 
     for step in range(STEPS):
         for plane in range(PLANES):
@@ -416,11 +405,11 @@
     second = others + [(i + slabs, j + slabs) for i, j in pairs]
     later = [(i, i + 1) for i in range(groups - 1)]
     flat = basis.reshape(ROWS, PLACES, 1, 128)
-    near, far, late, sizes = edges(num, den, basis)
-    near = lax.ppermute(near, ("core",) + SPACE, first).reshape(-1, 128)
-    far = lax.ppermute(far, ("core",) + SPACE, second).reshape(-1, 128)
-    late = lax.ppermute(late, TM, later).reshape(-1, 128)
-    parts, field, keep, give = basis_products(flat)
+    parts, field, sizes, near, far, late = prepare(num, den, flat)
+    near = lax.ppermute(near, ("core",) + SPACE, first)
+    far = lax.ppermute(far, ("core",) + SPACE, second)
+    late = lax.ppermute(late, TM, later)
+    keep, give = basis_products(parts)
     got = lax.ppermute(give, "core", [(0, 1), (1, 0)])
     inside = inner(sizes, field, near, far)
     parts, copies = image_products(sizes, field, inside, late, keep, got, parts)

time: 66.7 us -> 66.7 us (level)
  Pallas kernels: 9.29 us -> 7.93 us
  blocking collectives: 43 us -> 43.7 us
  waiting for transfers between devices: 0.14 us -> 0.83 us
    pallas_call x2, Pallas kernels: 4.66 us -> 3.63 us  [the longest x1 2.51 us: prepare(): pl.pallas_call(prepare_kernel, out_shape=(jax.ShapeDtypeStruct((PARTS * F...]
    ppermute x3, waiting for transfers between devices: 0.01 us -> 0.83 us  [the longest x1 0.83 us: per_device(): far = lax.ppermute(far, ('core',) + SPACE, second)]
    all_to_all x2, blocking collectives: 43 us -> 43.7 us  [exchanged(): return lax.all_to_all(copies, axes, 0, 0)]
  transfers between devices with their start and end apart: 4 -> 4, of which waited for: 1 -> 1; matrix products, arithmetic and copies ran while one was open for 0% -> 0% of each run, Pallas kernels for 6% -> 2%
where the time goes in v12:
time: 66.7 us; the launch traced here: 66.4 us
  blocking collectives  43.7 us (66%)
  starting transfers between devices  13.2 us (20%)
  Pallas kernels  7.93 us (12%)
  waiting for transfers between devices  0.83 us (1%)
  between operations  0.71 us (1%)
    all_to_all x2, blocking collectives, exchanged(): return lax.all_to_all(copies, axes, 0, 0)  43.7 us
    ppermute x1, starting transfers between devices, per_device(): far = lax.ppermute(far, ('core',) + SPACE, second)  8.15 us
    pallas_call x1, Pallas kernels, prepare(): pl.pallas_call(prepare_kernel, out_shape=(jax.ShapeDtypeStruct((PARTS * F...  2.51 us
    ppermute x1, starting transfers between devices, per_device(): got = lax.ppermute(give, 'core', [(0, 1), (1, 0)])  2.42 us
    pallas_call x1, Pallas kernels, finish(): pl.pallas_call(finish_kernel, out_shape=(jax.ShapeDtypeStruct((ROWS, COLS...  2.35 us
    ppermute x1, starting transfers between devices, per_device(): late = lax.ppermute(late, TM, later)  1.92 us
    pallas_call x1, Pallas kernels, image_products(): pl.pallas_call(image_kernel, out_shape=(jax.ShapeDtypeStruct((PARTS * FUL...  1.52 us
  transfers between devices with their start and end apart: 4, of which 1 were waited for; matrix products, arithmetic and copies ran while one was open for 0% of the time, Pallas kernels for 2%

profile of v12, /device:TPU:1, one launch (start us, length us, event | category | flops | bytes accessed | tf_op | source)
XLA Modules:
  0.0 66.4 jit_solution(15856352675595160293)
XLA Ops:
  0.6 2.5 %prepare.1 = (bf16[240,8192]{1,0:T(8,128)(2,1)S(1)}, f32[64,16,128]{2,1,0:T(8,128)S(1)}, f32[4,16,128]{2,1,0:T(8,128)S(1)}, f32[34,16,128]{2,1,0:T(8,128)S(1)}, ...) custom-call(s32[4]{0:T(128)} %num_hbm.1, s32[4]{0:T(128)} %den_hbm.1, f32[64,64,1,128]{3,2,1,0:T(1,128)} %bitcast.3), custom_call_target="tpu_custom_call" | custom-call | tf_op jit(solution)/shard_map/prepare/pallas_call | solution.py:108
  3.1 0.7 %collective-permute-start = (f32[34,16,128]{2,1,0:T(8,128)S(1)}, f32[34,16,128]{2,1,0:T(8,128)S(1)}, u32[]{:S(2)}, u32[]{:S(2)}) collective-permute-start(f32[34,16,128]{2,1,0:T(8,128)S(1)} %get-tuple-element.18), channel_id=1, source_target_pairs={{0,1},{1,0},{2,3},{3,2},{4,5},{5,4},{6,7},{7,6},{8,9},{9,8},{10,11... | collective-permute-start | bytes 835592 | tf_op jit(solution)/shard_map/ppermute | solution.py:409
  3.8 8.2 %collective-permute-start.1 = (f32[34,16,128]{2,1,0:T(8,128)S(1)}, f32[34,16,128]{2,1,0:T(8,128)S(1)}, u32[]{:S(2)}, u32[]{:S(2)}) collective-permute-start(f32[34,16,128]{2,1,0:T(8,128)S(1)} %get-tuple-element.19), channel_id=1, source_target_pairs={{1,2},{2,1},{3,4},{4,3},{5,6},{6,5},{7,8},{8,7},{9,10},{10,9},{11,... | collective-permute-start | bytes 835592 | tf_op jit(solution)/shard_map/ppermute | solution.py:410
  12.0 1.9 %collective-permute-start.2 = (f32[33,16,128]{2,1,0:T(8,128)S(1)}, f32[33,16,128]{2,1,0:T(8,128)S(1)}, u32[]{:S(2)}, u32[]{:S(2)}) collective-permute-start(f32[33,16,128]{2,1,0:T(8,128)S(1)} %get-tuple-element.20), channel_id=1, source_target_pairs={{0,32},{32,64},{64,96},{96,128},{128,160},{160,192},{192,224},{224... | collective-permute-start | bytes 811016 | tf_op jit(solution)/shard_map/ppermute | solution.py:411
  13.9 1.1 %basis_products.1 = (f32[16,128]{1,0:T(8,128)S(1)}, f32[16,128]{1,0:T(8,128)S(1)}) custom-call(bf16[240,8192]{1,0:T(8,128)(2,1)S(1)} %get-tuple-element.21.parts_ref.parts_in_ref), custom_call_target="tpu_custom_call" | custom-call | tf_op jit(solution)/shard_map/basis_products/pallas_call | solution.py:165
  15.0 2.4 %collective-permute-start.3 = (f32[16,128]{1,0:T(8,128)S(1)}, f32[16,128]{1,0:T(8,128)S(1)}, u32[]{:S(2)}, u32[]{:S(2)}) collective-permute-start(f32[16,128]{1,0:T(8,128)S(1)} %get-tuple-element.23), channel_id=1, source_target_pairs={{0,32},{32,0},{1,33},{33,1},{2,34},{34,2},{3,35},{35,3},{4,36},{36... | collective-permute-start | bytes 24584 | tf_op jit(solution)/shard_map/ppermute | solution.py:413
  17.5 0.0 collective-permute-done.first_ref
  17.5 0.8 %collective-permute-done.1.second_ref = f32[34,16,128]{2,1,0:T(8,128)S(1)} collective-permute-done((f32[34,16,128]{2,1,0:T(8,128)S(1)}, f32[34,16,128]{2,1,0:T(8,128)S(1)}, u32[]{:S(2)}, u32[]{:S(2)}) %collective-permute-start.1) | collective-permute-done | bytes 278560 | tf_op jit(solution)/shard_map/ppermute | solution.py:410
  18.3 0.4 inner.1.inner_ref
  18.7 0.0 collective-permute-done.3.got_ref
  18.7 0.0 collective-permute-done.2.late_ref
  18.7 1.5 %image_products.1 = (bf16[240,8192]{1,0:T(8,128)(2,1)S(1)}, f32[32,5,4,128]{3,2,1,0:T(4,128)S(1)}) custom-call(f32[4,16,128]{2,1,0:T(8,128)S(1)} %get-tuple-element.16.sizes_ref, f32[64,16,128]{2,1,0:T(8,128)S(1)} %get-tuple-element.17.field_ref, f32[64,16,128]{2,1,0:T(8,128)S(1)} %inner.1.inner_ref, ...), custom_call_target="tpu_custom_call", output_to_operand_aliasing={{0}: (6, {})} | custom-call | tf_op jit(solution)/shard_map/image_products/pallas_call | solution.py:272
  20.2 23.4 %all_to_all.10.sums_ref = f32[32,5,4,128]{3,2,1,0:T(4,128)S(1)} all-to-all(f32[32,5,4,128]{3,2,1,0:T(4,128)S(1)} %get-tuple-element.24), channel_id=1, replica_groups=mesh['y'=8,'core'=2,'x'=4,'z'=8] {'x','z'}, dimensions={0} | all-to-all | bytes 655360 | tf_op jit(solution)/shard_map/all_to_all | solution.py:396
  43.7 0.1 regroup.1
  43.7 20.3 %all_to_all.11.sums_ref = f32[16,5,4,128]{3,2,1,0:T(4,128)S(1)} all-to-all(f32[16,5,4,128]{3,2,1,0:T(4,128)S(1)} %regroup.1), channel_id=1, replica_groups=mesh['y'=8,'core'=2,'x'=4,'z'=8] {'y','core'}, dimensions={0} | all-to-all | bytes 327680 | tf_op jit(solution)/shard_map/all_to_all | solution.py:396
  64.0 2.4 %finish.1 = (f32[64,16]{1,0:T(8,128)}, f32[16,16]{1,0:T(8,128)}, f32[1024,128]{1,0:T(8,128)}) custom-call(f32[16,5,4,128]{3,2,1,0:T(4,128)S(1)} %all_to_all.11.sums_ref, bf16[240,8192]{1,0:T(8,128)(2,1)S(1)} %get-tuple-element.25.parts_ref), custom_call_target="tpu_custom_call" | custom-call | tf_op jit(solution)/shard_map/finish/pallas_call | solution.py:381
Async XLA Ops:
  3.1 14.3 %collective-permute-start = (f32[34,16,128]{2,1,0:T(8,128)S(1)}, f32[34,16,128]{2,1,0:T(8,128)S(1)}, u32[]{:S(2)}, u32[]{:S(2)}) collective-permute-start(f32[34,16,128]{2,1,0:T(8,128)S(1)} %get-tuple-element.18), channel_id=1, source_target_pairs={{0,1},{1,0},{2,3},{3,2},{4,5},{5,4},{6,7},{7,6},{8,9},{9,8},{10,11... | collective-permute-start | bytes 835592 | tf_op jit(solution)/shard_map/ppermute | solution.py:409
  3.8 14.5 %collective-permute-start.1 = (f32[34,16,128]{2,1,0:T(8,128)S(1)}, f32[34,16,128]{2,1,0:T(8,128)S(1)}, u32[]{:S(2)}, u32[]{:S(2)}) collective-permute-start(f32[34,16,128]{2,1,0:T(8,128)S(1)} %get-tuple-element.19), channel_id=1, source_target_pairs={{1,2},{2,1},{3,4},{4,3},{5,6},{6,5},{7,8},{8,7},{9,10},{10,9},{11,... | collective-permute-start | bytes 835592 | tf_op jit(solution)/shard_map/ppermute | solution.py:410
  12.0 6.7 %collective-permute-start.2 = (f32[33,16,128]{2,1,0:T(8,128)S(1)}, f32[33,16,128]{2,1,0:T(8,128)S(1)}, u32[]{:S(2)}, u32[]{:S(2)}) collective-permute-start(f32[33,16,128]{2,1,0:T(8,128)S(1)} %get-tuple-element.20), channel_id=1, source_target_pairs={{0,32},{32,64},{64,96},{96,128},{128,160},{160,192},{192,224},{224... | collective-permute-start | bytes 811016 | tf_op jit(solution)/shard_map/ppermute | solution.py:411
  15.0 3.6 %collective-permute-start.3 = (f32[16,128]{1,0:T(8,128)S(1)}, f32[16,128]{1,0:T(8,128)S(1)}, u32[]{:S(2)}, u32[]{:S(2)}) collective-permute-start(f32[16,128]{1,0:T(8,128)S(1)} %get-tuple-element.23), channel_id=1, source_target_pairs={{0,32},{32,0},{1,33},{33,1},{2,34},{34,2},{3,35},{35,3},{4,36},{36... | collective-permute-start | bytes 24584 | tf_op jit(solution)/shard_map/ppermute | solution.py:413

commit v13 on v9

--- a/solution.py
+++ b/solution.py
@@ -61,7 +61,7 @@
     num_hbm, den_hbm, basis_hbm, first_ref, second_ref, late_ref, sizes_ref, num_ref, den_ref, sems
 ):
     last = BLOCKS - 1
-    flip = (lax.axis_index("z") + lax.axis_index("core")) % 2
+    flip = (lax.axis_index("z") + lax.axis_index("core") + 1) % 2
     counts = [
         pltpu.make_async_copy(num_hbm, num_ref, sems.at[3]),
         pltpu.make_async_copy(den_hbm, den_ref, sems.at[4]),
@@ -137,20 +137,34 @@
     whole = parts_ref[: PARTS * ROWS]
     products = lax.dot_general(whole, whole, NT, preferred_element_type=F32)
     gram = part_products(products, ROWS, 0, ROWS)
-    rows = [gram[block * COLS : (block + 1) * COLS, block * COLS :] for block in range(BLOCKS)]
-    packed = jnp.concatenate([rows[0], rows[1], rows[3]], axis=1)
+    row = lax.broadcasted_iota(jnp.int32, (COLS, COLS), 0)
+    col = lax.broadcasted_iota(jnp.int32, (COLS, COLS), 1)
+    tiles = [
+        gram[block * COLS : (block + 1) * COLS, block * COLS : (block + 1) * COLS]
+        for block in range(BLOCKS)
+    ]
+    packed = jnp.concatenate(
+        [
+            gram[:COLS, COLS:],
+            gram[COLS : 2 * COLS, 2 * COLS :],
+            gram[2 * COLS : 3 * COLS, 3 * COLS :],
+            jnp.where(row <= col, tiles[0], tiles[1]),
+            jnp.where(row <= col, tiles[2], tiles[3]),
+        ],
+        axis=1,
+    )
     halves = []
     for half in range(2):
-        rest = rows[2][half * 8 : half * 8 + 8]
-        rest = jnp.concatenate([rest[2 * i : 2 * i + 2] for i in range(4)], axis=1)
-        halves.append((packed[half * 8 : half * 8 + 8], rest))
+        diagonal = jnp.sum(jnp.where(row == col, tiles[2 * half + 1], 0.0), axis=0, keepdims=True)
+        diagonal = jnp.concatenate([diagonal, jnp.zeros((1, 128 - COLS), F32)], axis=1)
+        halves.append((packed[half * 8 : half * 8 + 8], diagonal))
     own = lax.axis_index("core")
     first = jnp.full((8, 128), own) == 0
     for target, flip in ((keep_ref, False), (give_ref, True)):
         one, two = (halves[1], halves[0]) if flip else (halves[0], halves[1])
         target[0:8] = jnp.where(first, one[0], two[0])
-        target[8:10] = jnp.where(first[:2], one[1], two[1])
-        target[10:16] = jnp.zeros((6, 128), F32)
+        target[8:9] = jnp.where(first[:1], one[1], two[1])
+        target[9:16] = jnp.zeros((7, 128), F32)
 
 
 def basis_products(basis):
@@ -238,7 +252,7 @@
     sizes_ref, inner_ref, first_ref, second_ref, keep_ref, got_ref, parts_in_ref, parts_ref, copies_ref
 ):
     base = PARTS * ROWS
-    flip = (lax.axis_index("z") + lax.axis_index("core")) % 2
+    flip = (lax.axis_index("z") + lax.axis_index("core") + 1) % 2
     flipped = jnp.full((COLS, 128), flip) == 1
     for step in range(STEPS):
         kappa = 0.5 * sizes_ref[step]
@@ -257,18 +271,22 @@
     proj = part_products(products, COLS, 0, ROWS)
     gram = part_products(products, COLS, base, COLS)
     packed = jnp.concatenate([proj[:8], proj[8:]], axis=1)
+    chip = keep_ref[...] + got_ref[...]
+    row = lax.broadcasted_iota(jnp.int32, (COLS, COLS), 0)
+    col = lax.broadcasted_iota(jnp.int32, (COLS, COLS), 1)
+    diagonal = chip[8:9, :COLS]
+    turned = jnp.concatenate([diagonal[:, COLS - 1 :], diagonal[:, : COLS - 1]], axis=1)
+    mixed = jnp.where(row <= col, gram, jnp.where(row == COLS - 1, diagonal, turned))
     pieces = []
     for half in range(2):
-        lines = [gram[half * 8 + row : half * 8 + row + 1] for row in range(8)]
+        lines = [mixed[half * 8 + line : half * 8 + line + 1] for line in range(8)]
         pieces.append(jnp.concatenate(lines, axis=1))
-    chip = keep_ref[...] + got_ref[...]
-    last = jnp.concatenate(pieces + [chip[8:10]], axis=0)
+    parcels = [packed[2 * i : 2 * i + 2] for i in range(4)]
+    parcels += [chip[2 * i : 2 * i + 2] for i in range(4)]
+    parcels.append(jnp.concatenate(pieces, axis=0))
     for copy in range(SLABS):
-        copies_ref[copy, 0] = packed[:4]
-        copies_ref[copy, 1] = packed[4:]
-        copies_ref[copy, 2] = chip[0:4]
-        copies_ref[copy, 3] = chip[4:8]
-        copies_ref[copy, 4] = last
+        for index, parcel in enumerate(parcels):
+            copies_ref[copy, index] = parcel
 
 
 def image_products(sizes, inside, one, two, keep, got, parts):
@@ -276,7 +294,7 @@
         image_kernel,
         out_shape=(
             jax.ShapeDtypeStruct((PARTS * FULL, CELLS), BF16),
-            jax.ShapeDtypeStruct((SLABS, 5, 4, 128), F32),
+            jax.ShapeDtypeStruct((SLABS, 9, 2, 128), F32),
         ),
         in_specs=[VMEM] * 7,
         out_specs=(VMEM, VMEM),
@@ -297,7 +315,7 @@
 def regroup(sums):
     return pl.pallas_call(
         regroup_kernel,
-        out_shape=jax.ShapeDtypeStruct((GROUPS, 5, 4, 128), F32),
+        out_shape=jax.ShapeDtypeStruct((GROUPS, 9, 2, 128), F32),
         in_specs=[VMEM],
         out_specs=VMEM,
         compiler_params=params(4),
@@ -313,37 +331,52 @@
             total = total + sums_ref[piece]
         cores.append(total * (1.0 / TOTAL))
     sums = cores[0] + cores[1]
-    proj = jnp.concatenate(
-        [sums[0, :, :ROWS], sums[1, :, :ROWS], sums[0, :, ROWS:], sums[1, :, ROWS:]], axis=0
-    )
-    image_gram = jnp.concatenate(
+    high = jnp.concatenate([sums[i] for i in range(4)], axis=0)
+    proj = jnp.concatenate([high[:, :ROWS], high[:, ROWS:]], axis=0)
+    mixed = jnp.concatenate(
         [
-            sums[4, half : half + 1, line * COLS : (line + 1) * COLS]
+            sums[8, half : half + 1, line * COLS : (line + 1) * COLS]
             for half in range(2)
             for line in range(8)
         ],
         axis=0,
     )
-    packed = jnp.concatenate([cores[0][2], cores[0][3], cores[1][2], cores[1][3]], axis=0)
-    rest = jnp.concatenate(
-        [cores[core][4, 2:4, 32 * i : 32 * i + 32] for core in range(2) for i in range(4)], axis=0
-    )
-    kept = [packed[:, :64], packed[:, 64:112], rest, packed[:, 112:]]
-    upper = []
-    for block in range(BLOCKS):
-        pieces = [0.5 * kept[block][:, :COLS]]
-        if block:
-            pieces.insert(0, jnp.zeros((COLS, block * COLS), F32))
-        if block < BLOCKS - 1:
-            pieces.append(kept[block][:, COLS:])
-        upper.append(jnp.concatenate(pieces, axis=1))
-    half = jnp.concatenate(upper, axis=0)
+    packed = jnp.concatenate([cores[core][4 + i] for core in range(2) for i in range(4)], axis=0)
+    row = lax.broadcasted_iota(jnp.int32, (COLS, COLS), 0)
+    col = lax.broadcasted_iota(jnp.int32, (COLS, COLS), 1)
+
+    def upper_half(block, diagonal):
+        return jnp.where(row < col, block, 0.0) + jnp.where(row == col, 0.5 * diagonal, 0.0)
+
+    def lower_half(block, diagonal):
+        return jnp.where(row > col, block, 0.0) + jnp.where(row == col, 0.5 * diagonal, 0.0)
+
+    diagonals = [
+        jnp.concatenate(
+            [cores[core][8, 1:2, 7 * COLS : 8 * COLS - 1], cores[core][8, 1:2, 6 * COLS : 6 * COLS + 1]],
+            axis=1,
+        )
+        for core in range(2)
+    ]
+    pairs = [packed[:, 6 * COLS : 7 * COLS], packed[:, 7 * COLS :]]
+    zero = jnp.zeros((COLS, COLS), F32)
+    half = jnp.concatenate(
+        [
+            jnp.concatenate([upper_half(pairs[0], pairs[0]), packed[:, : 3 * COLS]], axis=1),
+            jnp.concatenate(
+                [zero, lower_half(pairs[0], diagonals[0]), packed[:, 3 * COLS : 5 * COLS]], axis=1
+            ),
+            jnp.concatenate(
+                [zero, zero, upper_half(pairs[1], pairs[1]), packed[:, 5 * COLS : 6 * COLS]], axis=1
+            ),
+            jnp.concatenate([zero, zero, zero, lower_half(pairs[1], diagonals[1])], axis=1),
+        ],
+        axis=0,
+    )
     carried = lax.dot_general(proj, half, NN, precision=HIGHEST, preferred_element_type=F32) - proj
     cross = lax.dot_general(carried, proj, NT, precision=HIGHEST, preferred_element_type=F32)
-    cross_t = lax.dot_general(proj, carried, NT, precision=HIGHEST, preferred_element_type=F32)
-    gram = image_gram + (cross + cross_t)
-    row = lax.broadcasted_iota(jnp.int32, (COLS, COLS), 0)
-    col = lax.broadcasted_iota(jnp.int32, (COLS, COLS), 1)
+    share = cross + upper_half(mixed, mixed)
+    gram = share + share.T
     eye = jnp.where(row == col, 1.0, 0.0).astype(F32)
     work = jnp.concatenate(
         [gram, -proj, eye, jnp.zeros((COLS, 128 - FULL - COLS), F32)], axis=1
@@ -404,8 +437,8 @@
     groups = size_of(TM)
     pairs = [(i, i ^ 1) for i in range(slabs)]
     others = [(i, ((i + 1) ^ 1) - 1) for i in range(1, slabs - 1)]
-    first = pairs + [(i + slabs, j + slabs) for i, j in others]
-    second = others + [(i + slabs, j + slabs) for i, j in pairs]
+    first = others + [(i + slabs, j + slabs) for i, j in pairs]
+    second = pairs + [(i + slabs, j + slabs) for i, j in others]
     later = [(i, i + 1) for i in range(groups - 1)]
     flat = basis.reshape(ROWS, PLACES, 1, 128)
     near, far, late, sizes = edges(num, den, basis)

time: 66.1 us -> 65.5 us (level)
  starting transfers between devices: 14.5 us -> 13.7 us
    ppermute x1, starting transfers between devices: 7.32 us -> 0.68 us  [per_device(): far = lax.ppermute(far, ('core',) + SPACE, second).reshape(-1, 128)]
    ppermute x1, starting transfers between devices: 0.68 us -> 4 us  [per_device(): near = lax.ppermute(near, ('core',) + SPACE, first).reshape(-1, 128)]
    ppermute x1, starting transfers between devices: 1.92 us -> 4.46 us  [per_device(): got = lax.ppermute(give, 'core', [(0, 1), (1, 0)])]
where the time goes in v13:
time: 65.5 us; the launch traced here: 65 us
  blocking collectives  41 us (63%)
  starting transfers between devices  13.7 us (21%)
  Pallas kernels  9.3 us (14%)
  between operations  0.7 us (1%)
    all_to_all x2, blocking collectives, exchanged(): return lax.all_to_all(copies, axes, 0, 0)  41 us
    ppermute x1, starting transfers between devices, per_device(): late = lax.ppermute(late, TM, later).reshape(-1, 128)  4.59 us
    ppermute x1, starting transfers between devices, per_device(): got = lax.ppermute(give, 'core', [(0, 1), (1, 0)])  4.46 us
    ppermute x1, starting transfers between devices, per_device(): near = lax.ppermute(near, ('core',) + SPACE, first).reshape(-1, 128)  4 us
    pallas_call x1, Pallas kernels, basis_products(): pl.pallas_call(basis_kernel, out_shape=(jax.ShapeDtypeStruct((PARTS * FUL...  3.56 us
    pallas_call x1, Pallas kernels, finish(): pl.pallas_call(finish_kernel, out_shape=(jax.ShapeDtypeStruct((ROWS, COLS...  2.4 us
    pallas_call x1, Pallas kernels, image_products(): pl.pallas_call(image_kernel, out_shape=(jax.ShapeDtypeStruct((PARTS * FUL...  1.62 us
  transfers between devices with their start and end apart: 4, of which 1 were waited for; matrix products, arithmetic and copies ran while one was open for 0% of the time, Pallas kernels for 6%

profile of v13, /device:TPU:1, one launch (start us, length us, event | category | flops | bytes accessed | tf_op | source)
XLA Modules:
  0.0 65.0 jit_solution(4027612091111126712)
XLA Ops:
  0.6 1.2 %edges.1 = (f32[16,4,8,128]{3,2,1,0:T(8,128)S(1)}, f32[16,4,8,128]{3,2,1,0:T(8,128)S(1)}, f32[17,2,2,8,128]{4,3,2,1,0:T(8,128)S(1)}, f32[4,16,128]{2,1,0:T(8,128)S(1)}) custom-call(s32[4]{0:T(128)} %num_hbm.1, s32[4]{0:T(128)} %den_hbm.1, f32[4,16,4,2,8,128]{5,4,3,2,1,0:T(8,128)} %basis_hbm.1), custom_call_target="tpu_custom_call" | custom-call | tf_op jit(solution)/shard_map/edges/pallas_call | solution.py:93
  1.8 4.6 %collective-permute-start = (f32[17,2,2,8,128]{4,3,2,1,0:T(8,128)S(1)}, f32[17,2,2,8,128]{4,3,2,1,0:T(8,128)S(1)}, u32[]{:S(2)}, u32[]{:S(2)}) collective-permute-start(f32[17,2,2,8,128]{4,3,2,1,0:T(8,128)S(1)} %get-tuple-element.18), channel_id=1, source_target_pairs={{0,32},{32,64},{64,96},{96,128},{128,160},{160,192},{192,224},{224... | collective-permute-start | bytes 835592 | tf_op jit(solution)/shard_map/ppermute | solution.py:447
  6.4 4.0 %collective-permute-start.1 = (f32[16,4,8,128]{3,2,1,0:T(8,128)S(1)}, f32[16,4,8,128]{3,2,1,0:T(8,128)S(1)}, u32[]{:S(2)}, u32[]{:S(2)}) collective-permute-start(f32[16,4,8,128]{3,2,1,0:T(8,128)S(1)} %get-tuple-element.19), channel_id=1, source_target_pairs={{1,2},{2,1},{3,4},{4,3},{5,6},{6,5},{7,8},{8,7},{9,10},{10,9},{11,... | collective-permute-start | bytes 786440 | tf_op jit(solution)/shard_map/ppermute | solution.py:445
  10.4 0.7 %collective-permute-start.2 = (f32[16,4,8,128]{3,2,1,0:T(8,128)S(1)}, f32[16,4,8,128]{3,2,1,0:T(8,128)S(1)}, u32[]{:S(2)}, u32[]{:S(2)}) collective-permute-start(f32[16,4,8,128]{3,2,1,0:T(8,128)S(1)} %get-tuple-element.20), channel_id=1, source_target_pairs={{0,1},{1,0},{2,3},{3,2},{4,5},{5,4},{6,7},{7,6},{8,9},{9,8},{10,11... | collective-permute-start | bytes 786440 | tf_op jit(solution)/shard_map/ppermute | solution.py:446
  11.1 3.6 %basis_products.1 = (bf16[240,8192]{1,0:T(8,128)(2,1)S(1)}, f32[64,16,128]{2,1,0:T(8,128)S(1)}, f32[16,128]{1,0:T(8,128)S(1)}, f32[16,128]{1,0:T(8,128)S(1)}) custom-call(f32[64,64,1,128]{3,2,1,0:T(1,128)} %bitcast.9), custom_call_target="tpu_custom_call" | custom-call | tf_op jit(solution)/shard_map/basis_products/pallas_call | solution.py:171
  14.7 4.5 %collective-permute-start.3 = (f32[16,128]{1,0:T(8,128)S(1)}, f32[16,128]{1,0:T(8,128)S(1)}, u32[]{:S(2)}, u32[]{:S(2)}) collective-permute-start(f32[16,128]{1,0:T(8,128)S(1)} %get-tuple-element.22), channel_id=1, source_target_pairs={{0,32},{32,0},{1,33},{33,1},{2,34},{34,2},{3,35},{35,3},{4,36},{36... | collective-permute-start | bytes 24584 | tf_op jit(solution)/shard_map/ppermute | solution.py:449
  19.1 0.0 collective-permute-done
  19.1 0.5 inner.1.inner_ref
  19.6 0.3 collective-permute-done.3.got_ref
  19.9 0.0 collective-permute-done.1
  19.9 0.0 collective-permute-done.2
  19.9 1.6 %image_products.1 = (bf16[240,8192]{1,0:T(8,128)(2,1)S(1)}, f32[32,9,2,128]{3,2,1,0:T(2,128)S(1)}) custom-call(f32[4,16,128]{2,1,0:T(8,128)S(1)} %get-tuple-element.16.sizes_ref, f32[64,16,128]{2,1,0:T(8,128)S(1)} %inner.1.inner_ref, f32[512,128]{1,0:T(8,128)S(1)} %bitcast.7, f32[512,128]{1,0:T(8,128)S(1)} %bitcast.8, ...), custom_call_target="tpu_custom_call", output_to_operand_aliasing={{0}: (6, {})} | custom-call | tf_op jit(solution)/shard_map/image_products/pallas_call | solution.py:293
  21.6 22.4 %all_to_all.10.sums_ref = f32[32,9,2,128]{3,2,1,0:T(2,128)S(1)} all-to-all(f32[32,9,2,128]{3,2,1,0:T(2,128)S(1)} %get-tuple-element.24), channel_id=1, replica_groups=mesh['y'=8,'core'=2,'x'=4,'z'=8] {'x','z'}, dimensions={0} | all-to-all | bytes 589824 | tf_op jit(solution)/shard_map/all_to_all | solution.py:432
  44.0 0.1 regroup.1
  44.1 18.5 %all_to_all.11.sums_ref = f32[16,9,2,128]{3,2,1,0:T(2,128)S(1)} all-to-all(f32[16,9,2,128]{3,2,1,0:T(2,128)S(1)} %regroup.1), channel_id=1, replica_groups=mesh['y'=8,'core'=2,'x'=4,'z'=8] {'y','core'}, dimensions={0} | all-to-all | bytes 294912 | tf_op jit(solution)/shard_map/all_to_all | solution.py:432
  62.6 2.4 %finish.1 = (f32[64,16]{1,0:T(8,128)}, f32[16,16]{1,0:T(8,128)}, f32[1024,128]{1,0:T(8,128)}) custom-call(f32[16,9,2,128]{3,2,1,0:T(2,128)S(1)} %all_to_all.11.sums_ref, bf16[240,8192]{1,0:T(8,128)(2,1)S(1)} %get-tuple-element.25.parts_ref), custom_call_target="tpu_custom_call" | custom-call | tf_op jit(solution)/shard_map/finish/pallas_call | solution.py:417
Async XLA Ops:
  1.8 17.3 %collective-permute-start = (f32[17,2,2,8,128]{4,3,2,1,0:T(8,128)S(1)}, f32[17,2,2,8,128]{4,3,2,1,0:T(8,128)S(1)}, u32[]{:S(2)}, u32[]{:S(2)}) collective-permute-start(f32[17,2,2,8,128]{4,3,2,1,0:T(8,128)S(1)} %get-tuple-element.18), channel_id=1, source_target_pairs={{0,32},{32,64},{64,96},{96,128},{128,160},{160,192},{192,224},{224... | collective-permute-start | bytes 835592 | tf_op jit(solution)/shard_map/ppermute | solution.py:447
  6.4 13.5 %collective-permute-start.1 = (f32[16,4,8,128]{3,2,1,0:T(8,128)S(1)}, f32[16,4,8,128]{3,2,1,0:T(8,128)S(1)}, u32[]{:S(2)}, u32[]{:S(2)}) collective-permute-start(f32[16,4,8,128]{3,2,1,0:T(8,128)S(1)} %get-tuple-element.19), channel_id=1, source_target_pairs={{1,2},{2,1},{3,4},{4,3},{5,6},{6,5},{7,8},{8,7},{9,10},{10,9},{11,... | collective-permute-start | bytes 786440 | tf_op jit(solution)/shard_map/ppermute | solution.py:445
  10.4 9.5 %collective-permute-start.2 = (f32[16,4,8,128]{3,2,1,0:T(8,128)S(1)}, f32[16,4,8,128]{3,2,1,0:T(8,128)S(1)}, u32[]{:S(2)}, u32[]{:S(2)}) collective-permute-start(f32[16,4,8,128]{3,2,1,0:T(8,128)S(1)} %get-tuple-element.20), channel_id=1, source_target_pairs={{0,1},{1,0},{2,3},{3,2},{4,5},{5,4},{6,7},{7,6},{8,9},{9,8},{10,11... | collective-permute-start | bytes 786440 | tf_op jit(solution)/shard_map/ppermute | solution.py:446
  14.7 5.3 %collective-permute-start.3 = (f32[16,128]{1,0:T(8,128)S(1)}, f32[16,128]{1,0:T(8,128)S(1)}, u32[]{:S(2)}, u32[]{:S(2)}) collective-permute-start(f32[16,128]{1,0:T(8,128)S(1)} %get-tuple-element.22), channel_id=1, source_target_pairs={{0,32},{32,0},{1,33},{33,1},{2,34},{34,2},{3,35},{35,3},{4,36},{36... | collective-permute-start | bytes 24584 | tf_op jit(solution)/shard_map/ppermute | solution.py:449

commit v14 on v13

--- a/solution.py
+++ b/solution.py
@@ -267,10 +267,23 @@
                         base + part * COLS : base + (part + 1) * COLS, place * 128 : (place + 1) * 128
                     ] = piece
     own_parts = parts_ref[base:]
-    products = lax.dot_general(own_parts, parts_ref[...], NT, preferred_element_type=F32)
-    proj = part_products(products, COLS, 0, ROWS)
-    gram = part_products(products, COLS, base, COLS)
-    packed = jnp.concatenate([proj[:8], proj[8:]], axis=1)
+    products = lax.dot_general(parts_ref[...], own_parts, NT, preferred_element_type=F32)
+
+    def pairs_of(offset, width):
+        total = None
+        for b in range(PARTS):
+            group = None
+            for a in range(PARTS - b):
+                piece = products[
+                    offset + b * width : offset + (b + 1) * width, a * COLS : (a + 1) * COLS
+                ]
+                group = piece if group is None else group + piece
+            total = group if total is None else total + group
+        return total
+
+    proj = pairs_of(0, ROWS)
+    gram = pairs_of(base, COLS)
+    packed = jnp.concatenate([proj[8 * i : 8 * i + 8] for i in range(8)], axis=1)
     chip = keep_ref[...] + got_ref[...]
     row = lax.broadcasted_iota(jnp.int32, (COLS, COLS), 0)
     col = lax.broadcasted_iota(jnp.int32, (COLS, COLS), 1)
@@ -332,7 +345,8 @@
         cores.append(total * (1.0 / TOTAL))
     sums = cores[0] + cores[1]
     high = jnp.concatenate([sums[i] for i in range(4)], axis=0)
-    proj = jnp.concatenate([high[:, :ROWS], high[:, ROWS:]], axis=0)
+    hess = jnp.concatenate([high[:, COLS * i : COLS * i + COLS] for i in range(8)], axis=0)
+    proj = hess.T
     mixed = jnp.concatenate(
         [
             sums[8, half : half + 1, line * COLS : (line + 1) * COLS]
@@ -392,7 +406,7 @@
         work = work - factor * work[step : step + 1]
         scale = jnp.where(wide_row == step, lax.rsqrt(pivot), scale)
     work = work * scale
-    hess_ref[...] = proj.T
+    hess_ref[...] = hess
     triangle_ref[...] = jnp.where(row <= col, work[:, :COLS], 0.0)
     factors = split(work[:, COLS : COLS + FULL])
     stacked = []

time: 65.5 us -> 65.4 us (level)
  no operation moved by 1% of the time
where the time goes in v14:
time: 65.4 us; the launch traced here: 65 us
  blocking collectives  41 us (63%)
  starting transfers between devices  13.7 us (21%)
  Pallas kernels  9.25 us (14%)
  between operations  0.7 us (1%)
    all_to_all x2, blocking collectives, exchanged(): return lax.all_to_all(copies, axes, 0, 0)  41 us
    ppermute x1, starting transfers between devices, per_device(): late = lax.ppermute(late, TM, later).reshape(-1, 128)  4.59 us
    ppermute x1, starting transfers between devices, per_device(): got = lax.ppermute(give, 'core', [(0, 1), (1, 0)])  4.46 us
    ppermute x1, starting transfers between devices, per_device(): near = lax.ppermute(near, ('core',) + SPACE, first).reshape(-1, 128)  4 us
    pallas_call x1, Pallas kernels, basis_products(): pl.pallas_call(basis_kernel, out_shape=(jax.ShapeDtypeStruct((PARTS * FUL...  3.56 us
    pallas_call x1, Pallas kernels, finish(): pl.pallas_call(finish_kernel, out_shape=(jax.ShapeDtypeStruct((ROWS, COLS...  2.43 us
    pallas_call x1, Pallas kernels, image_products(): pl.pallas_call(image_kernel, out_shape=(jax.ShapeDtypeStruct((PARTS * FUL...  1.53 us
  transfers between devices with their start and end apart: 4, of which 1 were waited for; matrix products, arithmetic and copies ran while one was open for 0% of the time, Pallas kernels for 6%

profile of v14, /device:TPU:1, one launch (start us, length us, event | category | flops | bytes accessed | tf_op | source)
XLA Modules:
  0.0 65.0 jit_solution(10114727133839705148)
XLA Ops:
  0.6 1.2 %edges.1 = (f32[16,4,8,128]{3,2,1,0:T(8,128)S(1)}, f32[16,4,8,128]{3,2,1,0:T(8,128)S(1)}, f32[17,2,2,8,128]{4,3,2,1,0:T(8,128)S(1)}, f32[4,16,128]{2,1,0:T(8,128)S(1)}) custom-call(s32[4]{0:T(128)} %num_hbm.1, s32[4]{0:T(128)} %den_hbm.1, f32[4,16,4,2,8,128]{5,4,3,2,1,0:T(8,128)} %basis_hbm.1), custom_call_target="tpu_custom_call" | custom-call | tf_op jit(solution)/shard_map/edges/pallas_call | solution.py:93
  1.8 4.6 %collective-permute-start = (f32[17,2,2,8,128]{4,3,2,1,0:T(8,128)S(1)}, f32[17,2,2,8,128]{4,3,2,1,0:T(8,128)S(1)}, u32[]{:S(2)}, u32[]{:S(2)}) collective-permute-start(f32[17,2,2,8,128]{4,3,2,1,0:T(8,128)S(1)} %get-tuple-element.18), channel_id=1, source_target_pairs={{0,32},{32,64},{64,96},{96,128},{128,160},{160,192},{192,224},{224... | collective-permute-start | bytes 835592 | tf_op jit(solution)/shard_map/ppermute | solution.py:461
  6.4 4.0 %collective-permute-start.1 = (f32[16,4,8,128]{3,2,1,0:T(8,128)S(1)}, f32[16,4,8,128]{3,2,1,0:T(8,128)S(1)}, u32[]{:S(2)}, u32[]{:S(2)}) collective-permute-start(f32[16,4,8,128]{3,2,1,0:T(8,128)S(1)} %get-tuple-element.19), channel_id=1, source_target_pairs={{1,2},{2,1},{3,4},{4,3},{5,6},{6,5},{7,8},{8,7},{9,10},{10,9},{11,... | collective-permute-start | bytes 786440 | tf_op jit(solution)/shard_map/ppermute | solution.py:459
  10.4 0.7 %collective-permute-start.2 = (f32[16,4,8,128]{3,2,1,0:T(8,128)S(1)}, f32[16,4,8,128]{3,2,1,0:T(8,128)S(1)}, u32[]{:S(2)}, u32[]{:S(2)}) collective-permute-start(f32[16,4,8,128]{3,2,1,0:T(8,128)S(1)} %get-tuple-element.20), channel_id=1, source_target_pairs={{0,1},{1,0},{2,3},{3,2},{4,5},{5,4},{6,7},{7,6},{8,9},{9,8},{10,11... | collective-permute-start | bytes 786440 | tf_op jit(solution)/shard_map/ppermute | solution.py:460
  11.1 3.6 %basis_products.1 = (bf16[240,8192]{1,0:T(8,128)(2,1)S(1)}, f32[64,16,128]{2,1,0:T(8,128)S(1)}, f32[16,128]{1,0:T(8,128)S(1)}, f32[16,128]{1,0:T(8,128)S(1)}) custom-call(f32[64,64,1,128]{3,2,1,0:T(1,128)} %bitcast.9), custom_call_target="tpu_custom_call" | custom-call | tf_op jit(solution)/shard_map/basis_products/pallas_call | solution.py:171
  14.7 4.5 %collective-permute-start.3 = (f32[16,128]{1,0:T(8,128)S(1)}, f32[16,128]{1,0:T(8,128)S(1)}, u32[]{:S(2)}, u32[]{:S(2)}) collective-permute-start(f32[16,128]{1,0:T(8,128)S(1)} %get-tuple-element.22), channel_id=1, source_target_pairs={{0,32},{32,0},{1,33},{33,1},{2,34},{34,2},{3,35},{35,3},{4,36},{36... | collective-permute-start | bytes 24584 | tf_op jit(solution)/shard_map/ppermute | solution.py:463
  19.1 0.0 collective-permute-done
  19.1 0.5 inner.1.inner_ref
  19.6 0.3 collective-permute-done.3.got_ref
  19.9 0.0 collective-permute-done.1
  19.9 0.0 collective-permute-done.2
  19.9 1.5 %image_products.1 = (bf16[240,8192]{1,0:T(8,128)(2,1)S(1)}, f32[32,9,2,128]{3,2,1,0:T(2,128)S(1)}) custom-call(f32[4,16,128]{2,1,0:T(8,128)S(1)} %get-tuple-element.16.sizes_ref, f32[64,16,128]{2,1,0:T(8,128)S(1)} %inner.1.inner_ref, f32[512,128]{1,0:T(8,128)S(1)} %bitcast.7, f32[512,128]{1,0:T(8,128)S(1)} %bitcast.8, ...), custom_call_target="tpu_custom_call", output_to_operand_aliasing={{0}: (6, {})} | custom-call | tf_op jit(solution)/shard_map/image_products/pallas_call | solution.py:306
  21.5 22.4 %all_to_all.10.sums_ref = f32[32,9,2,128]{3,2,1,0:T(2,128)S(1)} all-to-all(f32[32,9,2,128]{3,2,1,0:T(2,128)S(1)} %get-tuple-element.24), channel_id=1, replica_groups=mesh['y'=8,'core'=2,'x'=4,'z'=8] {'x','z'}, dimensions={0} | all-to-all | bytes 589824 | tf_op jit(solution)/shard_map/all_to_all | solution.py:446
  43.9 0.1 regroup.1
  44.0 18.5 %all_to_all.11.sums_ref = f32[16,9,2,128]{3,2,1,0:T(2,128)S(1)} all-to-all(f32[16,9,2,128]{3,2,1,0:T(2,128)S(1)} %regroup.1), channel_id=1, replica_groups=mesh['y'=8,'core'=2,'x'=4,'z'=8] {'y','core'}, dimensions={0} | all-to-all | bytes 294912 | tf_op jit(solution)/shard_map/all_to_all | solution.py:446
  62.5 2.4 %finish.1 = (f32[64,16]{1,0:T(8,128)}, f32[16,16]{1,0:T(8,128)}, f32[1024,128]{1,0:T(8,128)}) custom-call(f32[16,9,2,128]{3,2,1,0:T(2,128)S(1)} %all_to_all.11.sums_ref, bf16[240,8192]{1,0:T(8,128)(2,1)S(1)} %get-tuple-element.25.parts_ref), custom_call_target="tpu_custom_call" | custom-call | tf_op jit(solution)/shard_map/finish/pallas_call | solution.py:431
Async XLA Ops:
  1.8 17.3 %collective-permute-start = (f32[17,2,2,8,128]{4,3,2,1,0:T(8,128)S(1)}, f32[17,2,2,8,128]{4,3,2,1,0:T(8,128)S(1)}, u32[]{:S(2)}, u32[]{:S(2)}) collective-permute-start(f32[17,2,2,8,128]{4,3,2,1,0:T(8,128)S(1)} %get-tuple-element.18), channel_id=1, source_target_pairs={{0,32},{32,64},{64,96},{96,128},{128,160},{160,192},{192,224},{224... | collective-permute-start | bytes 835592 | tf_op jit(solution)/shard_map/ppermute | solution.py:461
  6.4 13.5 %collective-permute-start.1 = (f32[16,4,8,128]{3,2,1,0:T(8,128)S(1)}, f32[16,4,8,128]{3,2,1,0:T(8,128)S(1)}, u32[]{:S(2)}, u32[]{:S(2)}) collective-permute-start(f32[16,4,8,128]{3,2,1,0:T(8,128)S(1)} %get-tuple-element.19), channel_id=1, source_target_pairs={{1,2},{2,1},{3,4},{4,3},{5,6},{6,5},{7,8},{8,7},{9,10},{10,9},{11,... | collective-permute-start | bytes 786440 | tf_op jit(solution)/shard_map/ppermute | solution.py:459
  10.4 9.5 %collective-permute-start.2 = (f32[16,4,8,128]{3,2,1,0:T(8,128)S(1)}, f32[16,4,8,128]{3,2,1,0:T(8,128)S(1)}, u32[]{:S(2)}, u32[]{:S(2)}) collective-permute-start(f32[16,4,8,128]{3,2,1,0:T(8,128)S(1)} %get-tuple-element.20), channel_id=1, source_target_pairs={{0,1},{1,0},{2,3},{3,2},{4,5},{5,4},{6,7},{7,6},{8,9},{9,8},{10,11... | collective-permute-start | bytes 786440 | tf_op jit(solution)/shard_map/ppermute | solution.py:460
  14.7 5.3 %collective-permute-start.3 = (f32[16,128]{1,0:T(8,128)S(1)}, f32[16,128]{1,0:T(8,128)S(1)}, u32[]{:S(2)}, u32[]{:S(2)}) collective-permute-start(f32[16,128]{1,0:T(8,128)S(1)} %get-tuple-element.22), channel_id=1, source_target_pairs={{0,32},{32,0},{1,33},{33,1},{2,34},{34,2},{3,35},{35,3},{4,36},{36... | collective-permute-start | bytes 24584 | tf_op jit(solution)/shard_map/ppermute | solution.py:463
